TPU v7x, 256 devices: a whole 4x4x8 slice. The times are simulated.
256 devices in a mesh: rank: 32 (over x, z), group: 8 (over y, core).
Axes of the slice: x: 4, y: 4, z: 8, core: 2. Of those that a mesh axis runs over, the one named last changes fastest.
Arguments:
- residual: bfloat16 [6144, 3584], P(('group', 'rank')), parts along dimension 0, may hold values from -6 to 6
- queries: bfloat16 [6144, 64, 576], P(('group', 'rank')), parts along dimension 0
- latent_cache: bfloat16 [6144, 128, 576], P(('group', 'rank')), parts along dimension 0
- lengths: int32 [6144], P(('group', 'rank')), parts along dimension 0, may hold values from 2 to 128, as said below
- counts: int32 [256], P('group'), parts along dimension 0, may hold values from 1 to 24, as said below
- value_up: bfloat16 [64, 512, 128], P('rank'), may hold values from -0.25 to 0.25
- out_proj: bfloat16 [8192, 3584], P('rank'), may hold values from -0.0625 to 0.0625
- norm_gain: bfloat16 [3584], replicated, may hold values from 0.5 to 1.5
- gate_up: bfloat16 [3584, 18432], P(None, 'rank'), may hold values from -0.09375 to 0.09375
- down_proj: bfloat16 [9216, 3584], P('rank'), may hold values from -0.0625 to 0.0625
Outputs:
- layer_out: bfloat16 [6144, 3584], P(('group', 'rank')), parts along dimension 0
There are 8 independent parts, one for each index of `group`. A program takes and returns all parts, laid end to end along the dimension named above; an argument that names none is the same for every part. Nothing has to cross between parts.
Inputs may be any that keep to these rules, and one draw needn't show every extreme that they name: `counts`: some rank has all 24 slots live. `lengths`: some slot has the full 128 positions.
All inputs are finite; a program needn't handle non-finite values.
Results may differ from a plain program's by a relative error of at most 0.025.
Values may be sent and summed in bfloat16 or wider, within the bound.
No kernel may reach another device: no remote copies, remote signals or barrier semaphores. Data moves between devices by JAX's collectives and lax.ppermute only.
A program may use at most 128 MiB of HBM per device.

v0:
```python
import jax
import jax.numpy as jnp
from jax import lax
from jax.sharding import PartitionSpec as P


def round_trip(values_in):
    return lax.optimization_barrier(values_in.astype(jnp.bfloat16)).astype(jnp.float32)


def normalize(stream, norm_gain):
    factor = lax.rsqrt(jnp.mean(stream * stream, axis=-1, keepdims=True) + 1e-06)
    return (stream * factor * norm_gain.astype(jnp.float32)).astype(jnp.bfloat16)


def feed_hidden(row_block, gate_up):
    hidden_width = gate_up.shape[1] // 2
    joined = jnp.dot(row_block, gate_up, preferred_element_type=jnp.float32)
    return (jax.nn.silu(joined[:, :hidden_width]) * joined[:, hidden_width:]).astype(jnp.bfloat16)


def per_device(
    residual,
    queries,
    latent_cache,
    lengths,
    counts,
    value_up,
    out_proj,
    norm_gain,
    gate_up,
    down_proj,
):
    slots = residual.shape[0]
    ranks = lax.axis_size("rank")
    my_rank = lax.axis_index("rank")
    total_rows = slots * ranks
    latent_width = value_up.shape[1]
    value_width = value_up.shape[2]
    rotary_width = queries.shape[2] - latent_width
    positions = latent_cache.shape[1]
    alive_mask = jnp.arange(slots, dtype=jnp.int32) < counts[my_rank]
    score_scale = (value_width + rotary_width) ** (-0.5)
    scores = (
        jnp.einsum("shc,stc->sht", queries, latent_cache, preferred_element_type=jnp.float32)
        * score_scale
    )
    in_range = jnp.arange(positions, dtype=jnp.int32)[None, None, :] < lengths[:, None, None]
    scores = jnp.where(in_range, scores, -1e30)
    weights = jax.nn.softmax(scores, axis=-1).astype(jnp.bfloat16)
    latent = jnp.einsum(
        "sht,stc->shc",
        weights,
        latent_cache[:, :, :latent_width],
        preferred_element_type=jnp.float32,
    )
    latent = jnp.where(alive_mask[:, None, None], latent, 0.0).astype(jnp.bfloat16)
    arrived = lax.all_to_all(latent, "rank", split_axis=1, concat_axis=0, tiled=True)
    values = jnp.einsum(
        "shc,hcv->shv", arrived, value_up, preferred_element_type=jnp.float32
    ).astype(jnp.bfloat16)
    value_flat = values.reshape(total_rows, -1)
    row_block = value_flat
    own_attention = lax.psum_scatter(
        round_trip(jnp.dot(row_block, out_proj, preferred_element_type=jnp.float32)).astype(
            jnp.bfloat16
        ),
        "rank",
        scatter_dimension=0,
        tiled=True,
    ).astype(jnp.float32)
    mixed = residual.astype(jnp.float32) + own_attention
    own_normed = normalize(mixed, norm_gain)
    hidden = feed_hidden(lax.all_gather(own_normed, "rank", axis=0, tiled=True), gate_up)
    row_block = hidden
    feed = lax.psum_scatter(
        round_trip(jnp.dot(row_block, down_proj, preferred_element_type=jnp.float32)).astype(
            jnp.bfloat16
        ),
        "rank",
        scatter_dimension=0,
        tiled=True,
    ).astype(jnp.float32)
    return jnp.where(alive_mask[:, None], mixed + feed, 0.0).astype(jnp.bfloat16)


def solution(mesh):
    placed = (
        P(("group", "rank"), None),
        P(("group", "rank"), None, None),
        P(("group", "rank"), None, None),
        P(("group", "rank")),
        P("group"),
        P("rank", None, None),
        P("rank", None),
        P(),
        P(None, "rank"),
        P("rank", None),
    )
    return jax.shard_map(
        per_device,
        mesh=mesh,
        in_specs=placed,
        out_specs=P(("group", "rank"), None),
        check_vma=False,
    )
```

profile of v0, /device:TPU:24, one launch (start us, length us, event | category | flops | bytes accessed | tf_op | source)
XLA Modules:
  0.0 629.8 jit_solution(11036221241089450134)
XLA Ops:
  6.5 0.0 copy-start
  6.5 0.0 reduce-scatter.3.cloned.1.call-start
  6.5 1.4 dynamic_slice.3
  7.9 0.6 iota_compare_fusion.1
  8.6 0.7 iota_compare_fusion
  9.3 3.5 fusion.7
  12.9 0.5 fusion.14
  13.3 5.9 select_convert_fusion
  19.3 2.3 copy.15
  21.6 0.0 copy-start.4
  21.6 50.6 %all_to_all.18 = bf16[24,64,512]{2,0,1:T(8,128)(2,1)S(1)} all-to-all(bf16[24,64,512]{2,0,1:T(8,128)(2,1)S(1)} %copy.15), channel_id=1, replica_groups=mesh['rank'=32,'group'=8] {'rank'}, dimensions={1} | all-to-all | bytes 3145728 | tf_op jit(solution)/shard_map/all_to_all | solution.py:58
  72.2 0.0 copy-start.1
  72.2 0.1 copy.16
  72.3 0.0 copy-done.4
  72.3 0.7 convolution_convert_fusion.2
  73.0 0.7 copy-done.1
  73.7 4.0 convolution_convert_fusion
  77.7 0.0 copy-start.5
  77.7 0.0 copy-start.2
  77.7 0.0 reduce-scatter.3.cloned.1.call-update
  77.7 0.0 all-gather.2.cloned.1.call-start
  77.7 0.6 copy-done.5
  78.4 221.9 %reduce-scatter.3.cloned.1.call-done = bf16[24,3584]{1,0:T(8,128)(2,1)} async-done(((bf16[768,3584]{1,0:T(8,128)(2,1)}), bf16[24,3584]{1,0:T(8,128)(2,1)}) %reduce-scatter.3.cloned.1.call-update) | async-done | bytes 172048 | tf_op jit(solution)/shard_map/reduce_scatter | solution.py:64
  300.3 0.0 copy-done.2
  300.3 1.1 multiply_reduce_fusion
  301.4 1.7 multiply_convert_fusion
  303.1 0.0 all-gather.2.cloned.1.call-update
  303.1 0.0 reduce-scatter.5.cloned.1.call-start
  303.2 84.1 %all-gather.2.cloned.1.call-done = bf16[768,3584]{1,0:T(8,128)(2,1)} async-done(((bf16[24,3584]{1,0:T(8,128)(2,1)}), bf16[768,3584]{1,0:T(8,128)(2,1)}) %all-gather.2.cloned.1.call-update) | async-done | bytes 5505040 | tf_op jit(solution)/shard_map/all_gather | solution.py:74
  387.3 6.8 %fusion.15 = f32[768,576]{0,1:T(8,128)S(1)} fusion(bf16[768,3584]{1,0:T(8,128)(2,1)} %all-gather.2.cloned.1.call-done, bf16[3584,576]{0,1:T(8,128)(2,1)} %param.18), kind=kOutput, calls=%fused_computation.26 | convolution fusion | flops 3170893824 | bytes 11403264 | tf_op jit(solution)/shard_map/dot_general | solution.py:18
  394.1 0.0 copy-done
  394.1 5.0 convolution_convert_fusion.1
  399.1 0.0 copy-start.3
  399.1 0.0 reduce-scatter.5.cloned.1.call-update
  399.1 222.5 %reduce-scatter.5.cloned.1.call-done = bf16[24,3584]{1,0:T(8,128)(2,1)} async-done(((bf16[768,3584]{1,0:T(8,128)(2,1)}), bf16[24,3584]{1,0:T(8,128)(2,1)}) %reduce-scatter.5.cloned.1.call-update) | async-done | bytes 172048 | tf_op jit(solution)/shard_map/reduce_scatter | solution.py:76
  621.6 0.0 copy-done.3
  621.6 1.7 select_convert_fusion.1
  (2 shorter events, 0.0 us)
Async XLA Ops:
  6.5 387.6 %copy-start = (bf16[288,3584]{1,0:T(8,128)(2,1)S(1)}, bf16[288,3584]{1,0:T(8,128)(2,1)}, u32[]{:S(2)}) copy-start(bf16[288,3584]{1,0:T(8,128)(2,1)} %param.19) | copy-start | bytes 6193156
  6.5 293.8 %reduce-scatter.3.cloned.1.call-start = ((), (), s32[]{:S(2)}) async-start(), calls=%async_computation.3 | async-start | bytes 5677056 | tf_op jit(solution)/shard_map/reduce_scatter | solution.py:64
  21.6 50.7 %copy-start.4 = (bf16[2,512,128]{2,1,0:T(8,128)(2,1)S(1)}, bf16[2,512,128]{2,1,0:T(8,128)(2,1)}, u32[]{:S(2)}) copy-start(bf16[2,512,128]{2,1,0:T(8,128)(2,1)} %param.15) | copy-start | bytes 786436
  72.2 1.5 copy-start.1
  77.7 0.7 copy-start.5
  77.7 222.6 %copy-start.2 = (bf16[24,3584]{1,0:T(8,128)(2,1)S(1)}, bf16[24,3584]{1,0:T(8,128)(2,1)}, u32[]{:S(2)}) copy-start(bf16[24,3584]{1,0:T(8,128)(2,1)} %param.10) | copy-start | bytes 516100
  77.7 309.6 %all-gather.2.cloned.1.call-start = ((), (), s32[]{:S(2)}) async-start(), calls=%async_computation.4 | async-start | bytes 5677056 | tf_op jit(solution)/shard_map/all_gather | solution.py:74
  303.1 318.5 %reduce-scatter.5.cloned.1.call-start = ((), (), s32[]{:S(2)}) async-start(), calls=%async_computation.5 | async-start | bytes 5677056 | tf_op jit(solution)/shard_map/reduce_scatter | solution.py:76
  399.1 222.5 %copy-start.3 = (bf16[24,3584]{1,0:T(8,128)(2,1)S(1)}, bf16[24,3584]{1,0:T(8,128)(2,1)}, u32[]{:S(2)}) copy-start(bf16[24,3584]{1,0:T(8,128)(2,1)} %reduce-scatter.3.cloned.1.call-done) | copy-start | bytes 516100
Sparse Core Ops, SparseCore 0:
  77.8 222.4 reduce-scatter.2
  303.2 84.0 all-gather.1
  399.2 222.3 reduce-scatter.4
where the time goes:
time: 630 us
  waiting for transfers between devices  529 us (84%)
  blocking collectives  50.6 us (8%)
  matrix products  25.9 us (4%)
  between operations  13.2 us (2%)
  other arithmetic  6.33 us (1%)
    reduce_scatter x1, waiting for transfers between devices, per_device(): lax.psum_scatter(round_trip(jnp.dot(row_block, down_proj, preferred_eleme...  223 us
    reduce_scatter x1, waiting for transfers between devices, per_device(): lax.psum_scatter(round_trip(jnp.dot(row_block, out_proj, preferred_elemen...  222 us
    all_gather x1, waiting for transfers between devices, per_device(): lax.all_gather(own_normed, 'rank', axis=0, tiled=True)  84.1 us
    all_to_all x1, blocking collectives, per_device(): lax.all_to_all(latent, 'rank', split_axis=1, concat_axis=0, tiled=True)  50.6 us
  transfers between devices with their start and end apart: 3, of which 3 were waited for; matrix products, arithmetic and copies ran while one was open for 0% of the time, Pallas kernels for 0%

commit v1 on v0

v1 whole, which is shorter than its diff:
```python
import functools

import jax
import jax.numpy as jnp
from jax import lax
from jax.experimental import pallas as pl
from jax.experimental.pallas import tpu as pltpu
from jax.sharding import PartitionSpec as P

F32 = jnp.float32
BF16 = jnp.bfloat16
NX = 4
CAP = 384
CAP_Z = 64
EXTRA = 16
LANES = 128


def shift_x(ranks, k):
    nz = ranks // NX
    return [(x * nz + z, ((x + k) % NX) * nz + z) for x in range(NX) for z in range(nz)]


def shift_z(ranks, k):
    nz = ranks // NX
    return [(x * nz + z, x * nz + (z + k) % nz) for x in range(NX) for z in range(nz)]


def groups_x(ranks):
    nz = ranks // NX
    return [[x * nz + z for x in range(NX)] for z in range(nz)]


def groups_z(ranks):
    nz = ranks // NX
    return [[x * nz + z for z in range(nz)] for x in range(NX)]


def dot(a, b):
    return jnp.dot(a, b, preferred_element_type=F32)


def dot_nt(a, b):
    return lax.dot_general(a, b, (((1,), (1,)), ((), ())), preferred_element_type=F32)


def dot_tn(a, b):
    return lax.dot_general(a, b, (((0,), (0,)), ((), ())), preferred_element_type=F32)


def attend_kernel(scale, step_slots, lengths, queries, keys, out, *scratch):
    step = pl.program_id(0)
    slots, heads = out.shape[1], out.shape[0]
    latent_width = out.shape[2]
    positions = keys.shape[2]
    at = lax.broadcasted_iota(jnp.int32, (heads, positions), 1)
    for i in range(step_slots):
        slot = step * step_slots + i
        key = keys[i]
        scores = dot(queries[i], key) * scale
        scores = jnp.where(at < lengths[slot], scores, -1e30)
        weights = jnp.exp(scores - jnp.max(scores, axis=1, keepdims=True))
        weights = weights / jnp.sum(weights, axis=1, keepdims=True)
        latent = dot_nt(weights.astype(BF16), key[:latent_width])
        rows = pl.ds(pl.multiple_of(slot * heads, heads), heads)
        for lane, part in enumerate(scratch):
            part[rows, :] = latent[:, lane * LANES : (lane + 1) * LANES]

    @pl.when(step == pl.num_programs(0) - 1)
    def _():
        for head in range(heads):
            rows = [part[pl.ds(head, slots, stride=heads), :] for part in scratch]
            out[head] = jnp.concatenate(rows, axis=1).astype(BF16)


def attend(queries, latent_cache, lengths, latent_width, value_width):
    slots, heads, key_width = queries.shape
    positions = latent_cache.shape[1]
    rotary_width = key_width - latent_width
    scale = (value_width + rotary_width) ** (-0.5)
    step_slots = 4
    return pl.pallas_call(
        functools.partial(attend_kernel, scale, step_slots),
        out_shape=jax.ShapeDtypeStruct((heads, slots, latent_width), BF16),
        grid=(slots // step_slots,),
        in_specs=[
            pl.BlockSpec(memory_space=pltpu.SMEM),
            pl.BlockSpec((step_slots, heads, key_width), lambda i: (i, 0, 0)),
            pl.BlockSpec((step_slots, key_width, positions), lambda i: (i, 0, 0)),
        ],
        out_specs=pl.BlockSpec((heads, slots, latent_width), lambda i: (0, 0, 0)),
        scratch_shapes=[pltpu.VMEM((slots * heads, LANES), F32)] * (latent_width // LANES),
        compiler_params=pltpu.CompilerParams(vmem_limit_bytes=32 * 2**20),
        cost_estimate=pl.CostEstimate(
            flops=2 * slots * heads * positions * (key_width + latent_width),
            bytes_accessed=2 * slots * (heads + positions) * (key_width + latent_width),
            transcendentals=slots * heads * positions,
        ),
        name="attend",
    )(lengths, queries, latent_cache.transpose(0, 2, 1))


def down_kernel(terms, target, *refs):
    hiddens, downs, out = refs[:terms], refs[terms : 2 * terms], refs[2 * terms]
    total = dot_tn(hiddens[0][...], downs[0][...])
    for hidden, down in zip(hiddens[1:], downs[1:]):
        total = total + dot_tn(hidden[...], down[...])
    total = total.astype(BF16)
    nz, rows, _ = out.shape
    at = lax.broadcasted_iota(jnp.int32, (rows, total.shape[0]), 1)
    turn = lax.broadcasted_iota(jnp.int32, (rows, total.shape[0]), 0)
    for z in range(nz):
        pick = (at == turn + target[z]).astype(F32).astype(BF16)
        out[z] = dot(pick, total).astype(BF16)


def down_rows(hiddens, downs, first):
    nz = first.shape[0]
    cap = hiddens[0].shape[1]
    block = downs[0].shape[1]
    terms = len(hiddens)
    depth = sum(h.shape[0] for h in hiddens)
    return pl.pallas_call(
        functools.partial(down_kernel, terms),
        out_shape=jax.ShapeDtypeStruct((nz, CAP_Z, block), BF16),
        in_specs=[pl.BlockSpec(memory_space=pltpu.SMEM)]
        + [pl.BlockSpec(memory_space=pltpu.VMEM)] * (2 * terms),
        out_specs=pl.BlockSpec(memory_space=pltpu.VMEM),
        compiler_params=pltpu.CompilerParams(vmem_limit_bytes=32 * 2**20),
        cost_estimate=pl.CostEstimate(
            flops=2 * cap * block * (depth + nz * CAP_Z),
            bytes_accessed=2 * (depth * (cap + block) + nz * CAP_Z * block),
            transcendentals=0,
        ),
        name="down_rows",
    )(first, *hiddens, *downs)


def sends(ranks):
    return [shift_x(ranks, k) for k in range(1, NX)]


def take_cols(array, index, block):
    return lax.dynamic_slice_in_dim(array, index * block, block, 1)


def part_rows(height, members):
    rows = -(-height // (16 * members)) * 16
    while height % rows:
        rows += 16
    return rows


def exchange_weights(residual, out_proj, gate_up, down_proj, block):
    ranks = lax.axis_size("rank")
    members = lax.axis_size("group")
    member = lax.axis_index("group")
    my_x = lax.div(lax.axis_index("rank"), ranks // NX)
    matrices = [gate_up.T, down_proj, out_proj]
    parts = [part_rows(m.shape[0], members) for m in matrices]

    def cut(matrix, rows, x):
        piece = lax.dynamic_slice(matrix, (member * rows, x * block), (rows, block))
        return jnp.where(member * rows < matrix.shape[0], piece, jnp.zeros((), BF16))

    got = []
    for k in range(1, NX):
        x = lax.rem(my_x + k, NX)
        pieces = [cut(m, rows, x) for m, rows in zip(matrices, parts)]
        piece = jnp.concatenate(pieces + [take_cols(residual, x, block)], axis=0)
        got.append(lax.ppermute(piece, "rank", shift_x(ranks, k)))
    own = [take_cols(m, my_x, block) for m in matrices]
    res = [take_cols(residual, my_x, block)] + [g[sum(parts) :] for g in got]
    own[0] = jnp.pad(own[0], ((0, EXTRA), (0, 0)))
    return parts, got, own, jnp.concatenate(res, axis=0)


def gather_weights(parts, got, own):
    gathered, first = [], 0
    heights = [m.shape[0] for m in own]
    for height, rows in zip(heights, parts):
        piece = jnp.stack([g[first : first + rows] for g in got])
        gathered.append((height, piece))
        first += rows
    wholes = []
    for height, piece in gathered[::-1]:
        full = lax.all_gather(piece, "group", axis=1, tiled=True)
        full = jnp.pad(full, ((0, 0), (0, max(0, height - full.shape[1])), (0, 0)))
        wholes.append([full[k, :height] for k in range(NX - 1)])
    return [[m] + w for m, w in zip(own, wholes[::-1])]


def one_pass(index, values, res, joins, downs, outs, gain, place, base, width):
    ranks, slots = place.shape
    nz = ranks // NX
    block = gain.shape[0]
    rows_z = CAP // nz
    me = lax.axis_index("rank")
    my_x, my_z = lax.div(me, nz), lax.rem(me, nz)
    row = index * CAP + jnp.arange(CAP, dtype=jnp.int32)

    pick = (row[:, None] == place.reshape(-1)[None, :]).astype(BF16)
    packed = dot(pick, values).astype(BF16)
    heads = [packed] + [lax.ppermute(packed, "rank", perm) for perm in sends(ranks)]

    place_z = lax.dynamic_index_in_dim(place.reshape(NX, nz, slots), my_z, 1, False)
    order = lax.rem(my_x + NX - jnp.arange(NX, dtype=jnp.int32), NX)
    owners = place_z[order].reshape(-1)
    part = dot((row[:, None] == owners[None, :]).astype(BF16), res)
    for head, out in zip(heads, outs):
        part = part + dot(head, out)
    got = lax.all_to_all(
        part.astype(BF16).reshape(nz, rows_z, block),
        "rank",
        split_axis=0,
        concat_axis=0,
        tiled=True,
        axis_index_groups=groups_z(ranks),
    )
    mixed = jnp.sum(got.astype(F32), axis=0).astype(BF16)
    mixed = lax.all_to_all(
        jnp.broadcast_to(mixed[None], (nz, rows_z, block)),
        "rank",
        split_axis=0,
        concat_axis=0,
        tiled=True,
        axis_index_groups=groups_z(ranks),
    ).reshape(CAP, block)

    wide = mixed.astype(F32)
    square = jnp.sum(wide * wide, axis=1)
    high = lax.reduce_precision(square, 8, 7)
    both = joins[0].shape[0] - EXTRA
    line = jnp.arange(both + EXTRA, dtype=jnp.int32)[:, None]
    extra = jnp.where(line == both, high, jnp.where(line == both + 1, square - high, 0.0))
    scaled = (wide * gain[None, :]).astype(BF16)

    def share(join):
        return (dot_nt(join, scaled) + extra).astype(BF16)

    back = [shift_x(ranks, NX - k) for k in range(1, NX)]
    arrived = [lax.ppermute(share(join), "rank", perm) for join, perm in zip(joins[1:], back)]
    joined = share(joins[0]).astype(F32) + sum(a.astype(F32) for a in arrived)
    factor = lax.rsqrt((joined[both] + joined[both + 1]) / width + 1e-06)[None, :]
    gate, up = joined[: both // 2] * factor, joined[both // 2 : both] * factor
    hidden = (jax.nn.silu(gate) * up).astype(BF16)
    hiddens = [hidden] + [lax.ppermute(hidden, "rank", perm) for perm in sends(ranks)]

    sent = down_rows(hiddens, downs, base - index * CAP)
    got = lax.all_to_all(
        sent,
        "rank",
        split_axis=0,
        concat_axis=0,
        tiled=True,
        axis_index_groups=groups_z(ranks),
    )
    feed = jnp.sum(got.astype(F32), axis=0).astype(BF16)

    inside = (place_z >= index * CAP) & (place_z < (index + 1) * CAP)
    at = jnp.where(inside, place_z - base[my_z], -1).reshape(-1)
    take = (at[:, None] == jnp.arange(CAP_Z, dtype=jnp.int32)[None, :]).astype(BF16)
    keep = (place_z.reshape(-1)[:, None] == row[None, :]).astype(BF16)
    rows = (dot(take, feed) + dot(keep, mixed)).astype(BF16)
    rows = rows.reshape(NX, slots, block)
    pieces = [lax.dynamic_index_in_dim(rows, my_x, 0, False)] + [
        lax.ppermute(
            lax.dynamic_index_in_dim(rows, lax.rem(my_x + k, NX), 0, False),
            "rank",
            shift_x(ranks, k),
        )
        for k in range(1, NX)
    ]
    columns = []
    for x in range(NX):
        column = pieces[0]
        for k in range(1, NX):
            column = jnp.where(order[k] == x, pieces[k], column)
        columns.append(column)
    return jnp.concatenate(columns, axis=1), inside[my_x]


def packing(counts, slots):
    ranks = counts.shape[0]
    nz = ranks // NX
    grid = counts.reshape(NX, nz)
    before = jnp.cumsum(grid, axis=0) - grid
    total = jnp.sum(grid, axis=0)
    first = jnp.minimum(total, CAP_Z)
    rest = total - first
    passes = lax.div(jnp.sum(first) + CAP - 1, CAP)
    base_first = jnp.cumsum(first) - first
    base_rest = passes * CAP + jnp.cumsum(rest) - rest
    slot = jnp.arange(slots, dtype=jnp.int32)
    local = before[:, :, None] + slot
    place = jnp.where(
        local < CAP_Z, base_first[None, :, None] + local, base_rest[None, :, None] + local - CAP_Z
    )
    place = jnp.where(slot < grid[:, :, None], place, -1).reshape(ranks, slots)
    return place, base_first, base_rest, passes, passes + lax.div(jnp.sum(rest) + CAP - 1, CAP)


def per_device(
    residual,
    queries,
    latent_cache,
    lengths,
    counts,
    value_up,
    out_proj,
    norm_gain,
    gate_up,
    down_proj,
):
    slots = residual.shape[0]
    ranks = lax.axis_size("rank")
    latent_width, value_width = value_up.shape[1:]
    width = residual.shape[1]
    block = width // NX
    my_x = lax.div(lax.axis_index("rank"), ranks // NX)
    gain = lax.dynamic_slice_in_dim(norm_gain, my_x * block, block, 0).astype(F32)
    parts, got, own, res = exchange_weights(
        residual, out_proj, gate_up, down_proj, block
    )
    latent = attend(queries, latent_cache, lengths, latent_width, value_width)
    got = lax.optimization_barrier((got, latent))[0]
    joins, downs, outs = gather_weights(parts, got, own)
    arrived = lax.all_to_all(
        latent.reshape(ranks, -1, slots, latent_width), "rank", split_axis=0, concat_axis=0, tiled=True
    )
    arrived = arrived.transpose(0, 2, 1, 3).reshape(slots * ranks, -1, latent_width)
    values = jnp.einsum("shc,hcv->shv", arrived, value_up, preferred_element_type=F32)
    values = values.astype(BF16).reshape(slots * ranks, -1)
    place, base_first, base_rest, passes_first, passes = packing(counts, slots)

    def run(index):
        base = jnp.where(index < passes_first, base_first, base_rest)
        return one_pass(index, values, res, joins, downs, outs, gain, place, base, width)

    def more(state):
        index, out = state
        rows, inside = run(index)
        return index + 1, jnp.where(inside[:, None], rows, out)

    rows, inside = run(0)
    out = jnp.where(inside[:, None], rows, jnp.zeros((), BF16))
    return lax.while_loop(lambda state: state[0] < passes, more, (jnp.int32(1), out))[1]


def solution(mesh):
    placed = (
        P(("group", "rank"), None),
        P(("group", "rank"), None, None),
        P(("group", "rank"), None, None),
        P(("group", "rank")),
        P("group"),
        P("rank", None, None),
        P("rank", None),
        P(),
        P(None, "rank"),
        P("rank", None),
    )
    return jax.shard_map(
        per_device,
        mesh=mesh,
        in_specs=placed,
        out_specs=P(("group", "rank"), None),
        check_vma=False,
    )
```

time: 630 us -> 250 us (0.40)
  waiting for transfers between devices: 529 us -> 113 us
  blocking collectives: 50.6 us -> 0 us
  starting transfers between devices: 0.09 us -> 46.1 us
  local copies, waits for them, and re-layouts: 5.11 us -> 24.8 us
  Pallas kernels: 0 us -> 17 us
  matrix products: 25.9 us -> 13.3 us
  between operations: 13.2 us -> 22.2 us
    reduce_scatter x2 -> x0, waiting for transfers between devices: 444 us -> none  [the longest x1 223 us: per_device(): lax.psum_scatter(round_trip(jnp.dot(row_block, down_proj, preferred_eleme...]
    all_gather x1 -> x3, waiting for transfers between devices: 84.1 us -> 0.04 us  [gather_weights(): full = lax.all_gather(piece, 'group', axis=1, tiled=True)]
    all_to_all x0 -> x4, waiting for transfers between devices: none -> 82.1 us  [the longest x1 33.4 us: per_device(): lax.all_to_all(latent.reshape(ranks, -1, slots, latent_width), 'rank', sp...]
    all_to_all x1 -> x0, blocking collectives: 50.6 us -> none  [per_device(): lax.all_to_all(latent, 'rank', split_axis=1, concat_axis=0, tiled=True)]
    ppermute x0 -> x15, waiting for transfers between devices: none -> 30.3 us  [the longest x3 15.1 us: one_pass(): lax.ppermute(share(join), 'rank', perm)]
    all_to_all x0 -> x4, starting transfers between devices: none -> 25.5 us  [the longest x1 10.9 us: per_device(): lax.all_to_all(latent.reshape(ranks, -1, slots, latent_width), 'rank', sp...]
    ppermute x0 -> x15, starting transfers between devices: none -> 20.2 us  [the longest x3 5.9 us: exchange_weights(): got.append(lax.ppermute(piece, 'rank', shift_x(ranks, k)))]
    pallas_call x0 -> x2, Pallas kernels: none -> 17 us  [the longest x1 12.8 us: attend(): pl.pallas_call(functools.partial(attend_kernel, scale, step_slots), out_s...]
  transfers between devices with their start and end apart: 3 -> 22, of which waited for: 3 -> 13; matrix products, arithmetic and copies ran while one was open for 0% -> 16% of each run, Pallas kernels for 0% -> 5%
where the time goes in v1:
time: 250 us; the launch traced here: 248 us
  waiting for transfers between devices  113 us (45%)
  starting transfers between devices  46.1 us (18%)
  local copies, waits for them, and re-layouts  24.8 us (10%)
  between operations  22.2 us (9%)
  Pallas kernels  17 us (7%)
  matrix products  13.3 us (5%)
  other arithmetic  12.4 us (5%)
    all_to_all x1, waiting for transfers between devices, per_device(): lax.all_to_all(latent.reshape(ranks, -1, slots, latent_width), 'rank', sp...  33.4 us
    all_to_all x1, waiting for transfers between devices, one_pass(): lax.all_to_all(part.astype(BF16).reshape(nz, rows_z, block), 'rank', spli...  20.3 us
    all_to_all x1, waiting for transfers between devices, one_pass(): lax.all_to_all(jnp.broadcast_to(mixed[None], (nz, rows_z, block)), 'rank'...  18.9 us
    ppermute x3, waiting for transfers between devices, one_pass(): lax.ppermute(share(join), 'rank', perm)  15.1 us
    pallas_call x1, Pallas kernels, attend(): pl.pallas_call(functools.partial(attend_kernel, scale, step_slots), out_s...  12.8 us
    all_to_all x1, starting transfers between devices, per_device(): lax.all_to_all(latent.reshape(ranks, -1, slots, latent_width), 'rank', sp...  10.9 us
    all_to_all x1, waiting for transfers between devices, one_pass(): lax.all_to_all(sent, 'rank', split_axis=0, concat_axis=0, tiled=True, axi...  9.55 us
    ppermute x3, waiting for transfers between devices, one_pass(): lax.ppermute(hidden, 'rank', perm)  8.49 us
  transfers between devices with their start and end apart: 22, of which 13 were waited for; matrix products, arithmetic and copies ran while one was open for 16% of the time, Pallas kernels for 5%

profile of v1, /device:TPU:24, one launch (start us, length us, event | category | flops | bytes accessed | tf_op | source)
XLA Modules:
  0.0 248.5 jit_solution(9134618289532713995)
XLA Ops:
  8.4 1.2 dynamic-slice_select_fusion
  9.6 1.2 select_bitcast_fusion
  10.8 1.6 collective-permute-start.12
  12.4 2.8 %collective-permute-start.13 = (bf16[200,896]{1,0:T(8,128)(2,1)S(1)}, bf16[200,896]{1,0:T(8,128)(2,1)S(1)}, u32[]{:S(2)}, u32[]{:S(2)}) collective-permute-start(bf16[200,896]{1,0:T(8,128)(2,1)S(1)} %pad_maximum_fusion.2), channel_id=1, source_target_pairs={{0,128},{8,136},{16,144},{24,152},{32,160},{40,168},{48,176},{56,1... | collective-permute-start | bytes 1075208 | tf_op jit(solution)/shard_map/ppermute | solution.py:171
  15.3 1.5 collective-permute-start.14
  16.8 1.5 copy-done.3
  18.3 12.8 %attend.1 = bf16[64,24,512]{2,1,0:T(8,128)(2,1)} custom-call(s32[24]{0:T(128)S(1)} %copy-done.4, bf16[24,64,576]{2,1,0:T(8,128)(2,1)S(1)} %copy-done.3, bf16[24,576,128]{2,1,0:T(8,128)(2,1)S(1)} %bitcast.345), custom_call_target="tpu_custom_call" | custom-call | flops 427819008 | bytes 10027008 | tf_op jit(solution)/shard_map/attend/pallas_call | solution.py:82
  33.0 10.9 %all-to-all-start.3 = ((bf16[32,2,24,512]{3,2,1,0:T(8,128)(2,1)}), bf16[32,2,24,512]{3,2,1,0:T(8,128)(2,1)S(1)}, u32[]{:S(2)}, u32[]{:S(2)}) async-start(bf16[32,2,24,512]{3,2,1,0:T(8,128)(2,1)} %bitcast.40), calls=%async_computation.3 | async-start | bytes 3145728 | tf_op jit(solution)/shard_map/all_to_all | solution.py:328
  47.7 1.1 constant_dynamic-slice_fusion.2
  49.6 33.4 %all-to-all-done.3 = bf16[32,2,24,512]{3,2,1,0:T(8,128)(2,1)S(1)} async-done(((bf16[32,2,24,512]{3,2,1,0:T(8,128)(2,1)}), bf16[32,2,24,512]{3,2,1,0:T(8,128)(2,1)S(1)}, u32[]{:S(2)}, u32[]{:S(2)}) %all-to-all-start.3) | async-done | bytes 1572896 | tf_op jit(solution)/shard_map/all_to_all | solution.py:328
  85.6 1.0 collective-permute-start.15
  86.9 3.1 %collective-permute-done.17 = bf16[384,256]{1,0:T(8,128)(2,1)} collective-permute-done((bf16[384,256]{1,0:T(8,128)(2,1)S(1)}, bf16[384,256]{1,0:T(8,128)(2,1)}, u32[]{:S(2)}, u32[]{:S(2)}) %collective-permute-start.17) | collective-permute-done | bytes 196640 | tf_op jit(solution)/shard_map/ppermute | solution.py:204
  90.1 1.5 fusion.81
  92.8 1.6 collective-permute-done.15
  94.8 1.3 fusion.47
  96.2 6.8 %all-to-all-start.4 = ((bf16[8,48,896]{2,1,0:T(8,128)(2,1)}), bf16[8,48,896]{2,1,0:T(8,128)(2,1)S(1)}, u32[]{:S(2)}, u32[]{:S(2)}) async-start(bf16[8,48,896]{2,1,0:T(8,128)(2,1)} %bitcast.51), calls=%async_computation.4 | async-start | bytes 1376256 | tf_op jit(solution)/shard_map/all_to_all | solution.py:212
  103.9 20.3 %all-to-all-done.4 = bf16[8,48,896]{2,1,0:T(8,128)(2,1)S(1)} async-done(((bf16[8,48,896]{2,1,0:T(8,128)(2,1)}), bf16[8,48,896]{2,1,0:T(8,128)(2,1)S(1)}, u32[]{:S(2)}, u32[]{:S(2)}) %all-to-all-start.4) | async-done | bytes 688160 | tf_op jit(solution)/shard_map/all_to_all | solution.py:212
  124.3 1.0 broadcast_in_dim.187
  125.3 3.5 %all-to-all-start.5 = ((bf16[8,48,896]{2,1,0:T(8,128)(2,1)}), bf16[8,48,896]{2,1,0:T(8,128)(2,1)S(1)}, u32[]{:S(2)}, u32[]{:S(2)}) async-start(bf16[8,48,896]{2,1,0:T(8,128)(2,1)} %broadcast_in_dim.187), calls=%async_computation.5 | async-start | bytes 1376256 | tf_op jit(solution)/shard_map/all_to_all | solution.py:221
  129.9 1.4 dynamic-slice_convert_fusion
  131.3 18.9 %all-to-all-done.5 = bf16[8,48,896]{2,1,0:T(8,128)(2,1)S(1)} async-done(((bf16[8,48,896]{2,1,0:T(8,128)(2,1)}), bf16[8,48,896]{2,1,0:T(8,128)(2,1)S(1)}, u32[]{:S(2)}, u32[]{:S(2)}) %all-to-all-start.5) | async-done | bytes 688160 | tf_op jit(solution)/shard_map/all_to_all | solution.py:221
  150.2 1.0 fusion.45
  151.3 2.1 fusion.51
  153.4 2.1 fusion.50
  155.5 1.5 collective-permute-start.19
  157.0 2.0 fusion.49
  159.0 2.2 collective-permute-start.18
  161.2 1.9 constant_dynamic-slice_fusion.1.refs_4_
  163.1 1.3 dynamic-slice_bitcast_fusion.4
  164.4 12.3 %collective-permute-done.20 = bf16[592,384]{1,0:T(8,128)(2,1)S(1)} collective-permute-done((bf16[592,384]{1,0:T(8,128)(2,1)S(1)}, bf16[592,384]{1,0:T(8,128)(2,1)S(1)}, u32[]{:S(2)}, u32[]{:S(2)}) %collective-permute-start.20) | collective-permute-done | bytes 454688 | tf_op jit(solution)/shard_map/ppermute | solution.py:242
  176.7 2.8 %collective-permute-done.18 = bf16[592,384]{1,0:T(8,128)(2,1)S(1)} collective-permute-done((bf16[592,384]{1,0:T(8,128)(2,1)S(1)}, bf16[592,384]{1,0:T(8,128)(2,1)S(1)}, u32[]{:S(2)}, u32[]{:S(2)}) %collective-permute-start.18) | collective-permute-done | bytes 454688 | tf_op jit(solution)/shard_map/ppermute | solution.py:242
  179.5 1.6 add_add_fusion.1
  181.6 3.8 %collective-permute-start.22 = (bf16[288,384]{1,0:T(8,128)(2,1)S(1)}, bf16[288,384]{1,0:T(8,128)(2,1)S(1)}, u32[]{:S(2)}, u32[]{:S(2)}) collective-permute-start(bf16[288,384]{1,0:T(8,128)(2,1)S(1)} %fusion.59.refs_0_), channel_id=1, source_target_pairs={{0,128},{8,136},{16,144},{24,152},{32,160},{40,168},{48,176},{56,1... | collective-permute-start | bytes 663560 | tf_op jit(solution)/shard_map/ppermute | solution.py:247
  185.4 1.5 slice_bitcast_fusion.3
  187.0 2.6 %collective-permute-done.21.refs_1_ = bf16[288,384]{1,0:T(8,128)(2,1)S(1)} collective-permute-done((bf16[288,384]{1,0:T(8,128)(2,1)S(1)}, bf16[288,384]{1,0:T(8,128)(2,1)S(1)}, u32[]{:S(2)}, u32[]{:S(2)}) %collective-permute-start.21) | collective-permute-done | bytes 221216 | tf_op jit(solution)/shard_map/ppermute | solution.py:247
  189.6 5.9 %collective-permute-done.22.refs_2_ = bf16[288,384]{1,0:T(8,128)(2,1)S(1)} collective-permute-done((bf16[288,384]{1,0:T(8,128)(2,1)S(1)}, bf16[288,384]{1,0:T(8,128)(2,1)S(1)}, u32[]{:S(2)}, u32[]{:S(2)}) %collective-permute-start.22) | collective-permute-done | bytes 221216 | tf_op jit(solution)/shard_map/ppermute | solution.py:247
  195.5 4.3 %down_rows.6 = bf16[8,64,896]{2,1,0:T(8,128)(2,1)} custom-call(s32[8]{0:T(128)S(1)} %get-tuple-element.447.target, bf16[288,384]{1,0:T(8,128)(2,1)S(1)} %fusion.59.refs_0_, bf16[288,384]{1,0:T(8,128)(2,1)S(1)} %collective-permute-done.21.refs_1_, bf16[288,384]{1,0:T(8,128)(2,1)S(1)} %collective-permute-done.22.refs_2_, ...), custom_call_target="tpu_custom_call" | custom-call | flops 1145044992 | bytes 3866624 | tf_op jit(solution)/shard_map/down_rows/pallas_call | solution.py:123
  199.8 4.2 %all-to-all-start.6 = ((bf16[8,64,896]{2,1,0:T(8,128)(2,1)}), bf16[8,64,896]{2,1,0:T(8,128)(2,1)}, u32[]{:S(2)}, u32[]{:S(2)}) async-start(bf16[8,64,896]{2,1,0:T(8,128)(2,1)} %down_rows.6), calls=%async_computation.6 | async-start | bytes 1835008 | tf_op jit(solution)/shard_map/all_to_all | solution.py:250
  212.6 1.1 pad.4
  216.5 2.2 slice_bitcast_fusion.6
  218.8 0.9 copy.21
  220.0 9.6 %all-to-all-done.6 = bf16[8,64,896]{2,1,0:T(8,128)(2,1)} async-done(((bf16[8,64,896]{2,1,0:T(8,128)(2,1)}), bf16[8,64,896]{2,1,0:T(8,128)(2,1)}, u32[]{:S(2)}, u32[]{:S(2)}) %all-to-all-start.6) | async-done | bytes 917536 | tf_op jit(solution)/shard_map/all_to_all | solution.py:250
  229.6 1.3 reduce_sum.105
  231.2 3.1 %collective-permute-start.24 = (bf16[24,896]{1,0:T(8,128)(2,1)S(1)}, bf16[24,896]{1,0:T(8,128)(2,1)S(1)}, u32[]{:S(2)}, u32[]{:S(2)}) collective-permute-start(bf16[24,896]{1,0:T(8,128)(2,1)S(1)} %get-tuple-element.492), channel_id=1, source_target_pairs={{0,192},{8,200},{16,208},{24,216},{32,224},{40,232},{48,240},{56,2... | collective-permute-start | bytes 129032 | tf_op jit(solution)/shard_map/ppermute | solution.py:267
  234.3 1.0 collective-permute-start.26
  235.2 3.6 %slice_bitcast_fusion = (bf16[592,896]{1,0:T(8,128)(2,1)}, bf16[592,896]{1,0:T(8,128)(2,1)}, bf16[592,896]{1,0:T(8,128)(2,1)}) fusion(bf16[3,768,896]{2,1,0:T(8,128)(2,1)} %all-gather.6.cloned.1.call-done), kind=kLoop, calls=%fused_computation.107 | loop fusion | bytes 6365184 | tf_op jit(solution)/shard_map/squeeze | solution.py:189
  238.8 1.0 collective-permute-done.25
  241.0 0.9 copy-done.1
  (111 shorter events, 20.1 us)
Async XLA Ops:
  6.5 76.6 %copy-start = (bf16[2,512,128]{2,1,0:T(8,128)(2,1)S(1)}, bf16[2,512,128]{2,1,0:T(8,128)(2,1)}, u32[]{:S(2)}) copy-start(bf16[2,512,128]{2,1,0:T(8,128)(2,1)} %param.17) | copy-start | bytes 786436
  6.5 80.4 %all-gather.4.cloned.1.call-start = ((), (), s32[]{:S(2)}) async-start(), calls=%async_computation.7 | async-start | bytes 1548288 | tf_op jit(solution)/shard_map/all_gather | solution.py:187
  8.4 8.4 %copy-start.2 = (bf16[24,128,576]{1,2,0:T(8,128)(2,1)S(1)}, bf16[24,128,576]{1,2,0:T(8,128)(2,1)}, u32[]{:S(2)}) copy-start(bf16[24,128,576]{1,2,0:T(8,128)(2,1)} %param.14) | copy-start | bytes 10616836
  9.6 7.2 %copy-start.4 = (s32[24]{0:T(128)S(1)}, s32[24]{0:T(128)}, u32[]{:S(2)}) copy-start(s32[24]{0:T(128)} %lengths.1) | copy-start | bytes 292
  10.8 20.3 %collective-permute-start.12 = (bf16[200,896]{1,0:T(8,128)(2,1)S(1)}, bf16[200,896]{1,0:T(8,128)(2,1)S(1)}, u32[]{:S(2)}, u32[]{:S(2)}) collective-permute-start(bf16[200,896]{1,0:T(8,128)(2,1)S(1)} %pad_maximum_fusion.1), channel_id=1, source_target_pairs={{0,64},{8,72},{16,80},{24,88},{32,96},{40,104},{48,112},{56,120},{... | collective-permute-start | bytes 1075208 | tf_op jit(solution)/shard_map/ppermute | solution.py:171
  12.4 18.7 %collective-permute-start.13 = (bf16[200,896]{1,0:T(8,128)(2,1)S(1)}, bf16[200,896]{1,0:T(8,128)(2,1)S(1)}, u32[]{:S(2)}, u32[]{:S(2)}) collective-permute-start(bf16[200,896]{1,0:T(8,128)(2,1)S(1)} %pad_maximum_fusion.2), channel_id=1, source_target_pairs={{0,128},{8,136},{16,144},{24,152},{32,160},{40,168},{48,176},{56,1... | collective-permute-start | bytes 1075208 | tf_op jit(solution)/shard_map/ppermute | solution.py:171
  15.3 15.8 %collective-permute-start.14 = (bf16[200,896]{1,0:T(8,128)(2,1)S(1)}, bf16[200,896]{1,0:T(8,128)(2,1)S(1)}, u32[]{:S(2)}, u32[]{:S(2)}) collective-permute-start(bf16[200,896]{1,0:T(8,128)(2,1)S(1)} %pad_maximum_fusion.3), channel_id=1, source_target_pairs={{0,192},{8,200},{16,208},{24,216},{32,224},{40,232},{48,240},{56,2... | collective-permute-start | bytes 1075208 | tf_op jit(solution)/shard_map/ppermute | solution.py:171
  16.8 1.5 copy-start.3
  31.1 1.8 copy-start.19
  31.9 119.3 %all-gather.6.cloned.1.call-start = ((), (), s32[]{:S(2)}) async-start(), calls=%async_computation.8 | async-start | bytes 4644864 | tf_op jit(solution)/shard_map/all_gather | solution.py:187
  33.0 10.9 %copy-start.20 = (s32[32]{0:T(128)S(1)}, s32[32]{0:T(128)}, u32[]{:S(2)}) copy-start(s32[32]{0:T(128)} %param.16) | copy-start | bytes 388
  33.0 50.0 %all-to-all-start.3 = ((bf16[32,2,24,512]{3,2,1,0:T(8,128)(2,1)}), bf16[32,2,24,512]{3,2,1,0:T(8,128)(2,1)S(1)}, u32[]{:S(2)}, u32[]{:S(2)}) async-start(bf16[32,2,24,512]{3,2,1,0:T(8,128)(2,1)} %bitcast.40), calls=%async_computation.3 | async-start | bytes 3145728 | tf_op jit(solution)/shard_map/all_to_all | solution.py:328
  83.8 1.7 copy-start.7
  84.2 5.9 %collective-permute-start.17 = (bf16[384,256]{1,0:T(8,128)(2,1)S(1)}, bf16[384,256]{1,0:T(8,128)(2,1)}, u32[]{:S(2)}, u32[]{:S(2)}) collective-permute-start(bf16[384,256]{1,0:T(8,128)(2,1)S(1)} %fusion.54), channel_id=1, source_target_pairs={{0,192},{8,200},{16,208},{24,216},{32,224},{40,232},{48,240},{56,2... | collective-permute-start | bytes 589832 | tf_op jit(solution)/shard_map/ppermute | solution.py:204
  85.1 7.4 %collective-permute-start.16 = (bf16[384,256]{1,0:T(8,128)(2,1)S(1)}, bf16[384,256]{1,0:T(8,128)(2,1)S(1)}, u32[]{:S(2)}, u32[]{:S(2)}) collective-permute-start(bf16[384,256]{1,0:T(8,128)(2,1)S(1)} %fusion.54), channel_id=1, source_target_pairs={{0,128},{8,136},{16,144},{24,152},{32,160},{40,168},{48,176},{56,1... | collective-permute-start | bytes 589832 | tf_op jit(solution)/shard_map/ppermute | solution.py:204
  85.6 8.9 %collective-permute-start.15 = (bf16[384,256]{1,0:T(8,128)(2,1)S(1)}, bf16[384,256]{1,0:T(8,128)(2,1)S(1)}, u32[]{:S(2)}, u32[]{:S(2)}) collective-permute-start(bf16[384,256]{1,0:T(8,128)(2,1)S(1)} %fusion.54), channel_id=1, source_target_pairs={{0,64},{8,72},{16,80},{24,88},{32,96},{40,104},{48,112},{56,120},{... | collective-permute-start | bytes 589832 | tf_op jit(solution)/shard_map/ppermute | solution.py:204
  86.9 5.6 %copy-start.6 = (bf16[3,256,896]{2,1,0:T(8,128)(2,1)S(1)}, bf16[3,256,896]{2,1,0:T(8,128)(2,1)}, u32[]{:S(2)}) copy-start(bf16[3,256,896]{2,1,0:T(8,128)(2,1)} %all-gather.4.cloned.1.call-done) | copy-start | bytes 4128772
  96.2 28.0 %all-to-all-start.4 = ((bf16[8,48,896]{2,1,0:T(8,128)(2,1)}), bf16[8,48,896]{2,1,0:T(8,128)(2,1)S(1)}, u32[]{:S(2)}, u32[]{:S(2)}) async-start(bf16[8,48,896]{2,1,0:T(8,128)(2,1)} %bitcast.51), calls=%async_computation.4 | async-start | bytes 1376256 | tf_op jit(solution)/shard_map/all_to_all | solution.py:212
  125.3 24.9 %all-to-all-start.5 = ((bf16[8,48,896]{2,1,0:T(8,128)(2,1)}), bf16[8,48,896]{2,1,0:T(8,128)(2,1)S(1)}, u32[]{:S(2)}, u32[]{:S(2)}) async-start(bf16[8,48,896]{2,1,0:T(8,128)(2,1)} %broadcast_in_dim.187), calls=%async_computation.5 | async-start | bytes 1376256 | tf_op jit(solution)/shard_map/all_to_all | solution.py:221
  128.8 56.6 %all-gather.8.cloned.1.call-start = ((), (), s32[]{:S(2)}) async-start(), calls=%async_computation.9 | async-start | bytes 2322432 | tf_op jit(solution)/shard_map/all_gather | solution.py:187
  153.3 23.4 %collective-permute-start.20 = (bf16[592,384]{1,0:T(8,128)(2,1)S(1)}, bf16[592,384]{1,0:T(8,128)(2,1)S(1)}, u32[]{:S(2)}, u32[]{:S(2)}) collective-permute-start(bf16[592,384]{1,0:T(8,128)(2,1)S(1)} %fusion.51), channel_id=1, source_target_pairs={{0,64},{8,72},{16,80},{24,88},{32,96},{40,104},{48,112},{56,120},{... | collective-permute-start | bytes 1363976 | tf_op jit(solution)/shard_map/ppermute | solution.py:242
  155.5 21.2 %collective-permute-start.19 = (bf16[592,384]{1,0:T(8,128)(2,1)S(1)}, bf16[592,384]{1,0:T(8,128)(2,1)S(1)}, u32[]{:S(2)}, u32[]{:S(2)}) collective-permute-start(bf16[592,384]{1,0:T(8,128)(2,1)S(1)} %fusion.50), channel_id=1, source_target_pairs={{0,128},{8,136},{16,144},{24,152},{32,160},{40,168},{48,176},{56,1... | collective-permute-start | bytes 1363976 | tf_op jit(solution)/shard_map/ppermute | solution.py:242
  159.0 20.4 %collective-permute-start.18 = (bf16[592,384]{1,0:T(8,128)(2,1)S(1)}, bf16[592,384]{1,0:T(8,128)(2,1)S(1)}, u32[]{:S(2)}, u32[]{:S(2)}) collective-permute-start(bf16[592,384]{1,0:T(8,128)(2,1)S(1)} %fusion.49), channel_id=1, source_target_pairs={{0,192},{8,200},{16,208},{24,216},{32,224},{40,232},{48,240},{56,2... | collective-permute-start | bytes 1363976 | tf_op jit(solution)/shard_map/ppermute | solution.py:242
  181.3 8.3 %collective-permute-start.21 = (bf16[288,384]{1,0:T(8,128)(2,1)S(1)}, bf16[288,384]{1,0:T(8,128)(2,1)S(1)}, u32[]{:S(2)}, u32[]{:S(2)}) collective-permute-start(bf16[288,384]{1,0:T(8,128)(2,1)S(1)} %fusion.59.refs_0_), channel_id=1, source_target_pairs={{0,64},{8,72},{16,80},{24,88},{32,96},{40,104},{48,112},{56,120},{... | collective-permute-start | bytes 663560 | tf_op jit(solution)/shard_map/ppermute | solution.py:247
  181.6 13.9 %collective-permute-start.22 = (bf16[288,384]{1,0:T(8,128)(2,1)S(1)}, bf16[288,384]{1,0:T(8,128)(2,1)S(1)}, u32[]{:S(2)}, u32[]{:S(2)}) collective-permute-start(bf16[288,384]{1,0:T(8,128)(2,1)S(1)} %fusion.59.refs_0_), channel_id=1, source_target_pairs={{0,128},{8,136},{16,144},{24,152},{32,160},{40,168},{48,176},{56,1... | collective-permute-start | bytes 663560 | tf_op jit(solution)/shard_map/ppermute | solution.py:247
  185.4 10.1 %collective-permute-start.23 = (bf16[288,384]{1,0:T(8,128)(2,1)S(1)}, bf16[288,384]{1,0:T(8,128)(2,1)S(1)}, u32[]{:S(2)}, u32[]{:S(2)}) collective-permute-start(bf16[288,384]{1,0:T(8,128)(2,1)S(1)} %fusion.59.refs_0_), channel_id=1, source_target_pairs={{0,192},{8,200},{16,208},{24,216},{32,224},{40,232},{48,240},{56,2... | collective-permute-start | bytes 663560 | tf_op jit(solution)/shard_map/ppermute | solution.py:247
  185.4 10.1 %copy-start.11 = (bf16[288,896]{1,0:T(8,128)(2,1)S(1)}, bf16[288,896]{1,0:T(8,128)(2,1)}, u32[]{:S(2)}) copy-start(bf16[288,896]{1,0:T(8,128)(2,1)} %constant_dynamic-slice_fusion.1.refs_4_) | copy-start | bytes 1548292
  187.0 8.5 %copy-start.13 = (bf16[288,896]{1,0:T(8,128)(2,1)}, bf16[288,896]{1,0:T(8,128)(2,1)S(1)}, u32[]{:S(2)}) copy-start(bf16[288,896]{1,0:T(8,128)(2,1)S(1)} %get-tuple-element.818.refs_7_) | copy-start | bytes 1548292
  187.0 8.5 %copy-start.15 = (bf16[288,896]{1,0:T(8,128)(2,1)}, bf16[288,896]{1,0:T(8,128)(2,1)S(1)}, u32[]{:S(2)}) copy-start(bf16[288,896]{1,0:T(8,128)(2,1)S(1)} %get-tuple-element.817.refs_6_) | copy-start | bytes 1548292
  187.0 8.5 %copy-start.17 = (bf16[288,896]{1,0:T(8,128)(2,1)}, bf16[288,896]{1,0:T(8,128)(2,1)S(1)}, u32[]{:S(2)}) copy-start(bf16[288,896]{1,0:T(8,128)(2,1)S(1)} %get-tuple-element.816.refs_5_) | copy-start | bytes 1548292
  199.8 29.8 %all-to-all-start.6 = ((bf16[8,64,896]{2,1,0:T(8,128)(2,1)}), bf16[8,64,896]{2,1,0:T(8,128)(2,1)}, u32[]{:S(2)}, u32[]{:S(2)}) async-start(bf16[8,64,896]{2,1,0:T(8,128)(2,1)} %down_rows.6), calls=%async_computation.6 | async-start | bytes 1835008 | tf_op jit(solution)/shard_map/all_to_all | solution.py:250
  216.5 2.2 copy-start.8
  231.2 7.7 %collective-permute-start.24 = (bf16[24,896]{1,0:T(8,128)(2,1)S(1)}, bf16[24,896]{1,0:T(8,128)(2,1)S(1)}, u32[]{:S(2)}, u32[]{:S(2)}) collective-permute-start(bf16[24,896]{1,0:T(8,128)(2,1)S(1)} %get-tuple-element.492), channel_id=1, source_target_pairs={{0,192},{8,200},{16,208},{24,216},{32,224},{40,232},{48,240},{56,2... | collective-permute-start | bytes 129032 | tf_op jit(solution)/shard_map/ppermute | solution.py:267
  234.2 5.6 %collective-permute-start.25 = (bf16[24,896]{1,0:T(8,128)(2,1)S(1)}, bf16[24,896]{1,0:T(8,128)(2,1)S(1)}, u32[]{:S(2)}, u32[]{:S(2)}) collective-permute-start(bf16[24,896]{1,0:T(8,128)(2,1)S(1)} %get-tuple-element.491), channel_id=1, source_target_pairs={{0,128},{8,136},{16,144},{24,152},{32,160},{40,168},{48,176},{56,1... | collective-permute-start | bytes 129032 | tf_op jit(solution)/shard_map/ppermute | solution.py:267
  234.3 5.7 %collective-permute-start.26 = (bf16[24,896]{1,0:T(8,128)(2,1)S(1)}, bf16[24,896]{1,0:T(8,128)(2,1)S(1)}, u32[]{:S(2)}, u32[]{:S(2)}) collective-permute-start(bf16[24,896]{1,0:T(8,128)(2,1)S(1)} %get-tuple-element.490), channel_id=1, source_target_pairs={{0,64},{8,72},{16,80},{24,88},{32,96},{40,104},{48,112},{56,120},{... | collective-permute-start | bytes 129032 | tf_op jit(solution)/shard_map/ppermute | solution.py:267
  240.3 0.7 copy-start.5
  241.0 0.9 copy-start.1
Sparse Core Ops, SparseCore 0:
  32.0 27.1 all-gather.3
  61.1 34.2 all-gather.5
  131.5 25.7 all-gather.7

commit v2 on v1

--- a/solution.py
+++ b/solution.py
@@ -54,15 +54,18 @@
     latent_width = out.shape[2]
     positions = keys.shape[2]
     at = lax.broadcasted_iota(jnp.int32, (heads, positions), 1)
+    first = step * step_slots
+    scores = [
+        jnp.where(at < lengths[first + i], dot(queries[i], keys[i]) * scale, -1e30)
+        for i in range(step_slots)
+    ]
+    scores = jnp.concatenate(scores, axis=0)
+    weights = jnp.exp(scores - jnp.max(scores, axis=1, keepdims=True))
+    weights = weights * (1.0 / jnp.sum(weights, axis=1, keepdims=True))
+    weights = weights.astype(BF16)
     for i in range(step_slots):
-        slot = step * step_slots + i
-        key = keys[i]
-        scores = dot(queries[i], key) * scale
-        scores = jnp.where(at < lengths[slot], scores, -1e30)
-        weights = jnp.exp(scores - jnp.max(scores, axis=1, keepdims=True))
-        weights = weights / jnp.sum(weights, axis=1, keepdims=True)
-        latent = dot_nt(weights.astype(BF16), key[:latent_width])
-        rows = pl.ds(pl.multiple_of(slot * heads, heads), heads)
+        latent = dot_nt(weights[i * heads : (i + 1) * heads], keys[i, :latent_width])
+        rows = pl.ds(pl.multiple_of((first + i) * heads, heads), heads)
         for lane, part in enumerate(scratch):
             part[rows, :] = latent[:, lane * LANES : (lane + 1) * LANES]
 
@@ -78,7 +81,7 @@
     positions = latent_cache.shape[1]
     rotary_width = key_width - latent_width
     scale = (value_width + rotary_width) ** (-0.5)
-    step_slots = 4
+    step_slots = 8
     return pl.pallas_call(
         functools.partial(attend_kernel, scale, step_slots),
         out_shape=jax.ShapeDtypeStruct((heads, slots, latent_width), BF16),
@@ -90,7 +93,7 @@
         ],
         out_specs=pl.BlockSpec((heads, slots, latent_width), lambda i: (0, 0, 0)),
         scratch_shapes=[pltpu.VMEM((slots * heads, LANES), F32)] * (latent_width // LANES),
-        compiler_params=pltpu.CompilerParams(vmem_limit_bytes=32 * 2**20),
+        compiler_params=pltpu.CompilerParams(vmem_limit_bytes=56 * 2**20),
         cost_estimate=pl.CostEstimate(
             flops=2 * slots * heads * positions * (key_width + latent_width),
             bytes_accessed=2 * slots * (heads + positions) * (key_width + latent_width),
@@ -169,34 +172,40 @@
         pieces = [cut(m, rows, x) for m, rows in zip(matrices, parts)]
         piece = jnp.concatenate(pieces + [take_cols(residual, x, block)], axis=0)
         got.append(lax.ppermute(piece, "rank", shift_x(ranks, k)))
-    own = [take_cols(m, my_x, block) for m in matrices]
     res = [take_cols(residual, my_x, block)] + [g[sum(parts) :] for g in got]
-    own[0] = jnp.pad(own[0], ((0, EXTRA), (0, 0)))
-    return parts, got, own, jnp.concatenate(res, axis=0)
-
-
-def gather_weights(parts, got, own):
+    return parts, got, matrices, jnp.concatenate(res, axis=0)
+
+
+def gather_weights(parts, got):
     gathered, first = [], 0
-    heights = [m.shape[0] for m in own]
-    for height, rows in zip(heights, parts):
-        piece = jnp.stack([g[first : first + rows] for g in got])
-        gathered.append((height, piece))
+    for rows in parts:
+        gathered.append(jnp.stack([g[first : first + rows] for g in got]))
         first += rows
-    wholes = []
-    for height, piece in gathered[::-1]:
-        full = lax.all_gather(piece, "group", axis=1, tiled=True)
+    return [lax.all_gather(g, "group", axis=1, tiled=True) for g in gathered[::-1]][::-1]
+
+
+def own_blocks(matrices, my_x, block):
+    blocks = [take_cols(m, my_x, block) for m in matrices]
+    return [jnp.pad(blocks[0], ((0, EXTRA), (0, 0)))] + blocks[1:]
+
+
+def weight_blocks(own, gathered):
+    blocks = []
+    for mine, full in zip(own, gathered):
+        height = mine.shape[0]
         full = jnp.pad(full, ((0, 0), (0, max(0, height - full.shape[1])), (0, 0)))
-        wholes.append([full[k, :height] for k in range(NX - 1)])
-    return [[m] + w for m, w in zip(own, wholes[::-1])]
-
-
-def one_pass(index, values, res, joins, downs, outs, gain, place, base, width):
+        blocks.append([mine] + [full[k, :height] for k in range(NX - 1)])
+    return blocks
+
+
+def one_pass(index, values, res, own, gathered, gain, place, base, width):
     ranks, slots = place.shape
     nz = ranks // NX
     block = gain.shape[0]
     rows_z = CAP // nz
     me = lax.axis_index("rank")
     my_x, my_z = lax.div(me, nz), lax.rem(me, nz)
+    joins, downs, outs = weight_blocks(own, gathered)
     row = index * CAP + jnp.arange(CAP, dtype=jnp.int32)
 
     pick = (row[:, None] == place.reshape(-1)[None, :]).astype(BF16)
@@ -319,12 +328,11 @@
     block = width // NX
     my_x = lax.div(lax.axis_index("rank"), ranks // NX)
     gain = lax.dynamic_slice_in_dim(norm_gain, my_x * block, block, 0).astype(F32)
-    parts, got, own, res = exchange_weights(
-        residual, out_proj, gate_up, down_proj, block
-    )
+    parts, got, own, res = exchange_weights(residual, out_proj, gate_up, down_proj, block)
     latent = attend(queries, latent_cache, lengths, latent_width, value_width)
     got = lax.optimization_barrier((got, latent))[0]
-    joins, downs, outs = gather_weights(parts, got, own)
+    gathered = gather_weights(parts, got)
+    own = own_blocks(own, my_x, block)
     arrived = lax.all_to_all(
         latent.reshape(ranks, -1, slots, latent_width), "rank", split_axis=0, concat_axis=0, tiled=True
     )
@@ -335,7 +343,7 @@
 
     def run(index):
         base = jnp.where(index < passes_first, base_first, base_rest)
-        return one_pass(index, values, res, joins, downs, outs, gain, place, base, width)
+        return one_pass(index, values, res, own, gathered, gain, place, base, width)
 
     def more(state):
         index, out = state

time: 250 us -> 251 us (level)
  waiting for transfers between devices: 113 us -> 118 us
  Pallas kernels: 17 us -> 12.3 us
  local copies, waits for them, and re-layouts: 24.8 us -> 20.2 us
  matrix products: 13.3 us -> 16.2 us
    ppermute x3, waiting for transfers between devices: 0.01 us -> 6.05 us  [exchange_weights(): got.append(lax.ppermute(piece, 'rank', shift_x(ranks, k)))]
    squeeze x3 -> x1, local copies, waits for them, and re-layouts: 7.4 us -> 1.53 us  [weight_blocks(): blocks.append([mine] + [full[k, :height] for k in range(NX - 1)])]
    pallas_call x1, Pallas kernels: 12.8 us -> 8.04 us  [attend(): pl.pallas_call(functools.partial(attend_kernel, scale, step_slots), out_s...]
    dot_general x8, matrix products: 4.87 us -> 7.74 us  [dot(): return jnp.dot(a, b, preferred_element_type=F32)]
  transfers between devices with their start and end apart: 22 -> 22, of which waited for: 13 -> 14; matrix products, arithmetic and copies ran while one was open for 16% -> 17% of each run, Pallas kernels for 5% -> 3%
where the time goes in v2:
time: 251 us; the launch traced here: 249 us
  waiting for transfers between devices  118 us (47%)
  starting transfers between devices  46.3 us (18%)
  between operations  22.1 us (9%)
  local copies, waits for them, and re-layouts  20.2 us (8%)
  matrix products  16.2 us (6%)
  other arithmetic  14.1 us (6%)
  Pallas kernels  12.3 us (5%)
    all_to_all x1, waiting for transfers between devices, per_device(): lax.all_to_all(latent.reshape(ranks, -1, slots, latent_width), 'rank', sp...  31 us
    all_to_all x1, waiting for transfers between devices, one_pass(): lax.all_to_all(part.astype(BF16).reshape(nz, rows_z, block), 'rank', spli...  19.3 us
    all_to_all x1, waiting for transfers between devices, one_pass(): lax.all_to_all(jnp.broadcast_to(mixed[None], (nz, rows_z, block)), 'rank'...  18.9 us
    ppermute x3, waiting for transfers between devices, one_pass(): lax.ppermute(share(join), 'rank', perm)  15.1 us
    all_to_all x1, waiting for transfers between devices, one_pass(): lax.all_to_all(sent, 'rank', split_axis=0, concat_axis=0, tiled=True, axi...  12.1 us
    all_to_all x1, starting transfers between devices, per_device(): lax.all_to_all(latent.reshape(ranks, -1, slots, latent_width), 'rank', sp...  11 us
    ppermute x3, waiting for transfers between devices, one_pass(): lax.ppermute(hidden, 'rank', perm)  8.53 us
    pallas_call x1, Pallas kernels, attend(): pl.pallas_call(functools.partial(attend_kernel, scale, step_slots), out_s...  8.04 us
  transfers between devices with their start and end apart: 22, of which 14 were waited for; matrix products, arithmetic and copies ran while one was open for 17% of the time, Pallas kernels for 3%

profile of v2, /device:TPU:24, one launch (start us, length us, event | category | flops | bytes accessed | tf_op | source)
XLA Modules:
  0.0 249.4 jit_solution(6052983070152934338)
XLA Ops:
  8.4 1.0 dynamic-slice_select_fusion
  9.4 1.2 select_bitcast_fusion
  10.7 1.6 collective-permute-start.12
  12.3 2.8 %collective-permute-start.13 = (bf16[200,896]{1,0:T(8,128)(2,1)S(1)}, bf16[200,896]{1,0:T(8,128)(2,1)S(1)}, u32[]{:S(2)}, u32[]{:S(2)}) collective-permute-start(bf16[200,896]{1,0:T(8,128)(2,1)S(1)} %pad_maximum_fusion.2), channel_id=1, source_target_pairs={{0,128},{8,136},{16,144},{24,152},{32,160},{40,168},{48,176},{56,1... | collective-permute-start | bytes 1075208 | tf_op jit(solution)/shard_map/ppermute | solution.py:174
  15.1 1.5 collective-permute-start.14
  16.6 8.0 %attend.1 = bf16[64,24,512]{2,1,0:T(8,128)(2,1)} custom-call(s32[24]{0:T(128)} %lengths.1, bf16[24,64,576]{2,1,0:T(8,128)(2,1)} %queries.1, bf16[24,576,128]{2,1,0:T(8,128)(2,1)} %bitcast.396), custom_call_target="tpu_custom_call" | custom-call | flops 427819008 | bytes 10027008 | tf_op jit(solution)/shard_map/attend/pallas_call | solution.py:85
  24.7 6.0 %collective-permute-done.13 = bf16[200,896]{1,0:T(8,128)(2,1)S(1)} collective-permute-done((bf16[200,896]{1,0:T(8,128)(2,1)S(1)}, bf16[200,896]{1,0:T(8,128)(2,1)S(1)}, u32[]{:S(2)}, u32[]{:S(2)}) %collective-permute-start.13) | collective-permute-done | bytes 358432 | tf_op jit(solution)/shard_map/ppermute | solution.py:174
  32.6 11.0 %all-to-all-start.3 = ((bf16[32,2,24,512]{3,2,1,0:T(8,128)(2,1)}), bf16[32,2,24,512]{3,2,1,0:T(8,128)(2,1)S(1)}, u32[]{:S(2)}, u32[]{:S(2)}) async-start(bf16[32,2,24,512]{3,2,1,0:T(8,128)(2,1)} %bitcast.50), calls=%async_computation.3 | async-start | bytes 3145728 | tf_op jit(solution)/shard_map/all_to_all | solution.py:336
  47.3 1.2 fusion.101
  49.1 1.8 constant_dynamic-slice_fusion.2
  51.8 31.0 %all-to-all-done.3 = bf16[32,2,24,512]{3,2,1,0:T(8,128)(2,1)S(1)} async-done(((bf16[32,2,24,512]{3,2,1,0:T(8,128)(2,1)}), bf16[32,2,24,512]{3,2,1,0:T(8,128)(2,1)S(1)}, u32[]{:S(2)}, u32[]{:S(2)}) %all-to-all-start.3) | async-done | bytes 1572896 | tf_op jit(solution)/shard_map/all_to_all | solution.py:336
  85.4 1.0 collective-permute-start.15
  86.3 1.4 fusion.109
  87.8 2.1 collective-permute-done.17
  89.9 1.5 fusion.75
  91.4 1.0 collective-permute-done.16
  92.4 1.3 fusion.76
  94.4 1.3 fusion.77
  95.7 1.3 fusion.64
  97.0 6.9 %all-to-all-start.4 = ((bf16[8,48,896]{2,1,0:T(8,128)(2,1)}), bf16[8,48,896]{2,1,0:T(8,128)(2,1)S(1)}, u32[]{:S(2)}, u32[]{:S(2)}) async-start(bf16[8,48,896]{2,1,0:T(8,128)(2,1)} %bitcast.61), calls=%async_computation.4 | async-start | bytes 1376256 | tf_op jit(solution)/shard_map/all_to_all | solution.py:221
  105.7 19.3 %all-to-all-done.4 = bf16[8,48,896]{2,1,0:T(8,128)(2,1)S(1)} async-done(((bf16[8,48,896]{2,1,0:T(8,128)(2,1)}), bf16[8,48,896]{2,1,0:T(8,128)(2,1)S(1)}, u32[]{:S(2)}, u32[]{:S(2)}) %all-to-all-start.4) | async-done | bytes 688160 | tf_op jit(solution)/shard_map/all_to_all | solution.py:221
  125.2 1.0 broadcast_in_dim.187
  126.1 3.5 %all-to-all-start.5 = ((bf16[8,48,896]{2,1,0:T(8,128)(2,1)}), bf16[8,48,896]{2,1,0:T(8,128)(2,1)S(1)}, u32[]{:S(2)}, u32[]{:S(2)}) async-start(bf16[8,48,896]{2,1,0:T(8,128)(2,1)} %broadcast_in_dim.187), calls=%async_computation.5 | async-start | bytes 1376256 | tf_op jit(solution)/shard_map/all_to_all | solution.py:230
  130.8 1.4 dynamic-slice_convert_fusion
  132.2 18.9 %all-to-all-done.5 = bf16[8,48,896]{2,1,0:T(8,128)(2,1)S(1)} async-done(((bf16[8,48,896]{2,1,0:T(8,128)(2,1)}), bf16[8,48,896]{2,1,0:T(8,128)(2,1)S(1)}, u32[]{:S(2)}, u32[]{:S(2)}) %all-to-all-start.5) | async-done | bytes 688160 | tf_op jit(solution)/shard_map/all_to_all | solution.py:230
  151.1 1.0 fusion.62
  152.1 2.1 fusion.68
  154.3 2.1 fusion.67
  156.4 2.3 collective-permute-start.19
  158.7 2.1 fusion.66
  160.7 1.3 collective-permute-start.18
  162.0 1.9 constant_dynamic-slice_fusion.1.refs_4_
  163.9 1.3 dynamic-slice_bitcast_fusion.4
  165.2 12.3 %collective-permute-done.20 = bf16[592,384]{1,0:T(8,128)(2,1)S(1)} collective-permute-done((bf16[592,384]{1,0:T(8,128)(2,1)S(1)}, bf16[592,384]{1,0:T(8,128)(2,1)S(1)}, u32[]{:S(2)}, u32[]{:S(2)}) %collective-permute-start.20) | collective-permute-done | bytes 454688 | tf_op jit(solution)/shard_map/ppermute | solution.py:251
  177.6 2.8 %collective-permute-done.18 = bf16[592,384]{1,0:T(8,128)(2,1)S(1)} collective-permute-done((bf16[592,384]{1,0:T(8,128)(2,1)S(1)}, bf16[592,384]{1,0:T(8,128)(2,1)S(1)}, u32[]{:S(2)}, u32[]{:S(2)}) %collective-permute-start.18) | collective-permute-done | bytes 454688 | tf_op jit(solution)/shard_map/ppermute | solution.py:251
  180.4 1.6 add_add_fusion.1
  182.5 3.8 %collective-permute-start.22 = (bf16[288,384]{1,0:T(8,128)(2,1)S(1)}, bf16[288,384]{1,0:T(8,128)(2,1)S(1)}, u32[]{:S(2)}, u32[]{:S(2)}) collective-permute-start(bf16[288,384]{1,0:T(8,128)(2,1)S(1)} %fusion.79.refs_0_), channel_id=1, source_target_pairs={{0,128},{8,136},{16,144},{24,152},{32,160},{40,168},{48,176},{56,1... | collective-permute-start | bytes 663560 | tf_op jit(solution)/shard_map/ppermute | solution.py:256
  186.3 1.5 slice_bitcast_fusion.9
  187.9 2.6 %collective-permute-done.21.refs_1_ = bf16[288,384]{1,0:T(8,128)(2,1)S(1)} collective-permute-done((bf16[288,384]{1,0:T(8,128)(2,1)S(1)}, bf16[288,384]{1,0:T(8,128)(2,1)S(1)}, u32[]{:S(2)}, u32[]{:S(2)}) %collective-permute-start.21) | collective-permute-done | bytes 221216 | tf_op jit(solution)/shard_map/ppermute | solution.py:256
  190.5 5.9 %collective-permute-done.22.refs_2_ = bf16[288,384]{1,0:T(8,128)(2,1)S(1)} collective-permute-done((bf16[288,384]{1,0:T(8,128)(2,1)S(1)}, bf16[288,384]{1,0:T(8,128)(2,1)S(1)}, u32[]{:S(2)}, u32[]{:S(2)}) %collective-permute-start.22) | collective-permute-done | bytes 221216 | tf_op jit(solution)/shard_map/ppermute | solution.py:256
  196.4 4.2 %down_rows.6 = bf16[8,64,896]{2,1,0:T(8,128)(2,1)} custom-call(s32[8]{0:T(128)S(1)} %get-tuple-element.336.target, bf16[288,384]{1,0:T(8,128)(2,1)S(1)} %fusion.79.refs_0_, bf16[288,384]{1,0:T(8,128)(2,1)S(1)} %collective-permute-done.21.refs_1_, bf16[288,384]{1,0:T(8,128)(2,1)S(1)} %collective-permute-done.22.refs_2_, ...), custom_call_target="tpu_custom_call" | custom-call | flops 1145044992 | bytes 3866624 | tf_op jit(solution)/shard_map/down_rows/pallas_call | solution.py:126
  200.6 4.4 %all-to-all-start.6 = ((bf16[8,64,896]{2,1,0:T(8,128)(2,1)}), bf16[8,64,896]{2,1,0:T(8,128)(2,1)}, u32[]{:S(2)}, u32[]{:S(2)}) async-start(bf16[8,64,896]{2,1,0:T(8,128)(2,1)} %down_rows.6), calls=%async_computation.6 | async-start | bytes 1835008 | tf_op jit(solution)/shard_map/all_to_all | solution.py:259
  213.6 1.1 pad.4
  218.5 12.1 %all-to-all-done.6 = bf16[8,64,896]{2,1,0:T(8,128)(2,1)} async-done(((bf16[8,64,896]{2,1,0:T(8,128)(2,1)}), bf16[8,64,896]{2,1,0:T(8,128)(2,1)}, u32[]{:S(2)}, u32[]{:S(2)}) %all-to-all-start.6) | async-done | bytes 917536 | tf_op jit(solution)/shard_map/all_to_all | solution.py:259
  230.5 1.3 reduce_sum.105
  232.1 3.1 %collective-permute-start.24 = (bf16[24,896]{1,0:T(8,128)(2,1)S(1)}, bf16[24,896]{1,0:T(8,128)(2,1)S(1)}, u32[]{:S(2)}, u32[]{:S(2)}) collective-permute-start(bf16[24,896]{1,0:T(8,128)(2,1)S(1)} %get-tuple-element.380), channel_id=1, source_target_pairs={{0,192},{8,200},{16,208},{24,216},{32,224},{40,232},{48,240},{56,2... | collective-permute-start | bytes 129032 | tf_op jit(solution)/shard_map/ppermute | solution.py:276
  235.2 1.0 collective-permute-start.26
  237.8 3.0 %collective-permute-done.25 = bf16[24,896]{1,0:T(8,128)(2,1)S(1)} collective-permute-done((bf16[24,896]{1,0:T(8,128)(2,1)S(1)}, bf16[24,896]{1,0:T(8,128)(2,1)S(1)}, u32[]{:S(2)}, u32[]{:S(2)}) %collective-permute-start.25) | collective-permute-done | bytes 43040 | tf_op jit(solution)/shard_map/ppermute | solution.py:276
  (115 shorter events, 23.5 us)
Async XLA Ops:
  6.5 76.4 %copy-start = (bf16[2,512,128]{2,1,0:T(8,128)(2,1)S(1)}, bf16[2,512,128]{2,1,0:T(8,128)(2,1)}, u32[]{:S(2)}) copy-start(bf16[2,512,128]{2,1,0:T(8,128)(2,1)} %param.17) | copy-start | bytes 786436
  6.5 81.2 %all-gather.4.cloned.1.call-start = ((), (), s32[]{:S(2)}) async-start(), calls=%async_computation.7 | async-start | bytes 1548288 | tf_op jit(solution)/shard_map/all_gather | solution.py:184
  7.4 88.2 %copy-start.13 = (bf16[24,896]{1,0:T(8,128)(2,1)}, bf16[24,896]{1,0:T(8,128)(2,1)S(1)}, u32[]{:S(2)}) copy-start(bf16[24,896]{1,0:T(8,128)(2,1)S(1)} %get-tuple-element.381) | copy-start | bytes 129028
  10.7 14.0 %collective-permute-start.12 = (bf16[200,896]{1,0:T(8,128)(2,1)S(1)}, bf16[200,896]{1,0:T(8,128)(2,1)S(1)}, u32[]{:S(2)}, u32[]{:S(2)}) collective-permute-start(bf16[200,896]{1,0:T(8,128)(2,1)S(1)} %pad_maximum_fusion.1), channel_id=1, source_target_pairs={{0,64},{8,72},{16,80},{24,88},{32,96},{40,104},{48,112},{56,120},{... | collective-permute-start | bytes 1075208 | tf_op jit(solution)/shard_map/ppermute | solution.py:174
  12.3 18.5 %collective-permute-start.13 = (bf16[200,896]{1,0:T(8,128)(2,1)S(1)}, bf16[200,896]{1,0:T(8,128)(2,1)S(1)}, u32[]{:S(2)}, u32[]{:S(2)}) collective-permute-start(bf16[200,896]{1,0:T(8,128)(2,1)S(1)} %pad_maximum_fusion.2), channel_id=1, source_target_pairs={{0,128},{8,136},{16,144},{24,152},{32,160},{40,168},{48,176},{56,1... | collective-permute-start | bytes 1075208 | tf_op jit(solution)/shard_map/ppermute | solution.py:174
  15.1 15.6 %collective-permute-start.14 = (bf16[200,896]{1,0:T(8,128)(2,1)S(1)}, bf16[200,896]{1,0:T(8,128)(2,1)S(1)}, u32[]{:S(2)}, u32[]{:S(2)}) collective-permute-start(bf16[200,896]{1,0:T(8,128)(2,1)S(1)} %pad_maximum_fusion.3), channel_id=1, source_target_pairs={{0,192},{8,200},{16,208},{24,216},{32,224},{40,232},{48,240},{56,2... | collective-permute-start | bytes 1075208 | tf_op jit(solution)/shard_map/ppermute | solution.py:174
  24.7 27.1 %copy-start.15 = (bf16[200,896]{1,0:T(8,128)(2,1)}, bf16[200,896]{1,0:T(8,128)(2,1)S(1)}, u32[]{:S(2)}) copy-start(bf16[200,896]{1,0:T(8,128)(2,1)S(1)} %collective-permute-done.12) | copy-start | bytes 1075204
  30.7 21.0 %copy-start.16 = (bf16[200,896]{1,0:T(8,128)(2,1)}, bf16[200,896]{1,0:T(8,128)(2,1)S(1)}, u32[]{:S(2)}) copy-start(bf16[200,896]{1,0:T(8,128)(2,1)S(1)} %collective-permute-done.13) | copy-start | bytes 1075204
  30.7 1.9 copy-start.17
  31.6 120.5 %all-gather.6.cloned.1.call-start = ((), (), s32[]{:S(2)}) async-start(), calls=%async_computation.8 | async-start | bytes 4644864 | tf_op jit(solution)/shard_map/all_gather | solution.py:184
  32.6 11.0 %copy-start.19 = (s32[32]{0:T(128)S(1)}, s32[32]{0:T(128)}, u32[]{:S(2)}) copy-start(s32[32]{0:T(128)} %param.16) | copy-start | bytes 388
  32.6 50.2 %all-to-all-start.3 = ((bf16[32,2,24,512]{3,2,1,0:T(8,128)(2,1)}), bf16[32,2,24,512]{3,2,1,0:T(8,128)(2,1)S(1)}, u32[]{:S(2)}, u32[]{:S(2)}) async-start(bf16[32,2,24,512]{3,2,1,0:T(8,128)(2,1)} %bitcast.50), calls=%async_computation.3 | async-start | bytes 3145728 | tf_op jit(solution)/shard_map/all_to_all | solution.py:336
  48.5 34.5 %copy-start.18 = (s32[4,1,24]{2,1,0:T(1,128)}, s32[4,1,24]{2,1,0:T(1,128)S(1)}, u32[]{:S(2)}) copy-start(s32[4,1,24]{2,1,0:T(1,128)S(1)} %get-tuple-element.340) | copy-start | bytes 1156
  51.8 43.9 %copy-start.9 = (bf16[24,896]{1,0:T(8,128)(2,1)}, bf16[24,896]{1,0:T(8,128)(2,1)S(1)}, u32[]{:S(2)}) copy-start(bf16[24,896]{1,0:T(8,128)(2,1)S(1)} %slice.251) | copy-start | bytes 129028
  51.8 43.9 %copy-start.11 = (bf16[24,896]{1,0:T(8,128)(2,1)}, bf16[24,896]{1,0:T(8,128)(2,1)S(1)}, u32[]{:S(2)}) copy-start(bf16[24,896]{1,0:T(8,128)(2,1)S(1)} %slice.250) | copy-start | bytes 129028
  84.0 5.9 %collective-permute-start.17 = (bf16[384,256]{1,0:T(8,128)(2,1)S(1)}, bf16[384,256]{1,0:T(8,128)(2,1)}, u32[]{:S(2)}, u32[]{:S(2)}) collective-permute-start(bf16[384,256]{1,0:T(8,128)(2,1)S(1)} %fusion.71), channel_id=1, source_target_pairs={{0,192},{8,200},{16,208},{24,216},{32,224},{40,232},{48,240},{56,2... | collective-permute-start | bytes 589832 | tf_op jit(solution)/shard_map/ppermute | solution.py:213
  84.9 7.5 %collective-permute-start.16 = (bf16[384,256]{1,0:T(8,128)(2,1)S(1)}, bf16[384,256]{1,0:T(8,128)(2,1)}, u32[]{:S(2)}, u32[]{:S(2)}) collective-permute-start(bf16[384,256]{1,0:T(8,128)(2,1)S(1)} %fusion.71), channel_id=1, source_target_pairs={{0,128},{8,136},{16,144},{24,152},{32,160},{40,168},{48,176},{56,1... | collective-permute-start | bytes 589832 | tf_op jit(solution)/shard_map/ppermute | solution.py:213
  85.4 9.0 %collective-permute-start.15 = (bf16[384,256]{1,0:T(8,128)(2,1)S(1)}, bf16[384,256]{1,0:T(8,128)(2,1)}, u32[]{:S(2)}, u32[]{:S(2)}) collective-permute-start(bf16[384,256]{1,0:T(8,128)(2,1)S(1)} %fusion.71), channel_id=1, source_target_pairs={{0,64},{8,72},{16,80},{24,88},{32,96},{40,104},{48,112},{56,120},{... | collective-permute-start | bytes 589832 | tf_op jit(solution)/shard_map/ppermute | solution.py:213
  87.7 4.6 %copy-start.2 = (bf16[3,256,896]{2,1,0:T(8,128)(2,1)S(1)}, bf16[3,256,896]{2,1,0:T(8,128)(2,1)}, u32[]{:S(2)}) copy-start(bf16[3,256,896]{2,1,0:T(8,128)(2,1)} %all-gather.4.cloned.1.call-done) | copy-start | bytes 4128772
  97.0 28.0 %all-to-all-start.4 = ((bf16[8,48,896]{2,1,0:T(8,128)(2,1)}), bf16[8,48,896]{2,1,0:T(8,128)(2,1)S(1)}, u32[]{:S(2)}, u32[]{:S(2)}) async-start(bf16[8,48,896]{2,1,0:T(8,128)(2,1)} %bitcast.61), calls=%async_computation.4 | async-start | bytes 1376256 | tf_op jit(solution)/shard_map/all_to_all | solution.py:221
  126.1 24.9 %all-to-all-start.5 = ((bf16[8,48,896]{2,1,0:T(8,128)(2,1)}), bf16[8,48,896]{2,1,0:T(8,128)(2,1)S(1)}, u32[]{:S(2)}, u32[]{:S(2)}) async-start(bf16[8,48,896]{2,1,0:T(8,128)(2,1)} %broadcast_in_dim.187), calls=%async_computation.5 | async-start | bytes 1376256 | tf_op jit(solution)/shard_map/all_to_all | solution.py:230
  129.7 56.6 %all-gather.8.cloned.1.call-start = ((), (), s32[]{:S(2)}) async-start(), calls=%async_computation.9 | async-start | bytes 2322432 | tf_op jit(solution)/shard_map/all_gather | solution.py:184
  154.2 23.4 %collective-permute-start.20 = (bf16[592,384]{1,0:T(8,128)(2,1)S(1)}, bf16[592,384]{1,0:T(8,128)(2,1)S(1)}, u32[]{:S(2)}, u32[]{:S(2)}) collective-permute-start(bf16[592,384]{1,0:T(8,128)(2,1)S(1)} %fusion.68), channel_id=1, source_target_pairs={{0,64},{8,72},{16,80},{24,88},{32,96},{40,104},{48,112},{56,120},{... | collective-permute-start | bytes 1363976 | tf_op jit(solution)/shard_map/ppermute | solution.py:251
  156.4 21.2 %collective-permute-start.19 = (bf16[592,384]{1,0:T(8,128)(2,1)S(1)}, bf16[592,384]{1,0:T(8,128)(2,1)S(1)}, u32[]{:S(2)}, u32[]{:S(2)}) collective-permute-start(bf16[592,384]{1,0:T(8,128)(2,1)S(1)} %fusion.67), channel_id=1, source_target_pairs={{0,128},{8,136},{16,144},{24,152},{32,160},{40,168},{48,176},{56,1... | collective-permute-start | bytes 1363976 | tf_op jit(solution)/shard_map/ppermute | solution.py:251
  160.7 19.6 %collective-permute-start.18 = (bf16[592,384]{1,0:T(8,128)(2,1)S(1)}, bf16[592,384]{1,0:T(8,128)(2,1)S(1)}, u32[]{:S(2)}, u32[]{:S(2)}) collective-permute-start(bf16[592,384]{1,0:T(8,128)(2,1)S(1)} %fusion.66), channel_id=1, source_target_pairs={{0,192},{8,200},{16,208},{24,216},{32,224},{40,232},{48,240},{56,2... | collective-permute-start | bytes 1363976 | tf_op jit(solution)/shard_map/ppermute | solution.py:251
  165.2 16.8 %copy-start.4 = (bf16[576,896]{1,0:T(8,128)(2,1)}, bf16[576,896]{1,0:T(8,128)(2,1)S(1)}, u32[]{:S(2)}) copy-start(bf16[576,896]{1,0:T(8,128)(2,1)S(1)} %dynamic-slice_bitcast_fusion.4) | copy-start | bytes 3096580
  182.2 8.3 %collective-permute-start.21 = (bf16[288,384]{1,0:T(8,128)(2,1)S(1)}, bf16[288,384]{1,0:T(8,128)(2,1)S(1)}, u32[]{:S(2)}, u32[]{:S(2)}) collective-permute-start(bf16[288,384]{1,0:T(8,128)(2,1)S(1)} %fusion.79.refs_0_), channel_id=1, source_target_pairs={{0,64},{8,72},{16,80},{24,88},{32,96},{40,104},{48,112},{56,120},{... | collective-permute-start | bytes 663560 | tf_op jit(solution)/shard_map/ppermute | solution.py:256
  182.5 13.9 %collective-permute-start.22 = (bf16[288,384]{1,0:T(8,128)(2,1)S(1)}, bf16[288,384]{1,0:T(8,128)(2,1)S(1)}, u32[]{:S(2)}, u32[]{:S(2)}) collective-permute-start(bf16[288,384]{1,0:T(8,128)(2,1)S(1)} %fusion.79.refs_0_), channel_id=1, source_target_pairs={{0,128},{8,136},{16,144},{24,152},{32,160},{40,168},{48,176},{56,1... | collective-permute-start | bytes 663560 | tf_op jit(solution)/shard_map/ppermute | solution.py:256
  186.3 10.1 %collective-permute-start.23 = (bf16[288,384]{1,0:T(8,128)(2,1)S(1)}, bf16[288,384]{1,0:T(8,128)(2,1)S(1)}, u32[]{:S(2)}, u32[]{:S(2)}) collective-permute-start(bf16[288,384]{1,0:T(8,128)(2,1)S(1)} %fusion.79.refs_0_), channel_id=1, source_target_pairs={{0,192},{8,200},{16,208},{24,216},{32,224},{40,232},{48,240},{56,2... | collective-permute-start | bytes 663560 | tf_op jit(solution)/shard_map/ppermute | solution.py:256
  186.3 10.1 %copy-start.7 = (bf16[288,896]{1,0:T(8,128)(2,1)S(1)}, bf16[288,896]{1,0:T(8,128)(2,1)}, u32[]{:S(2)}) copy-start(bf16[288,896]{1,0:T(8,128)(2,1)} %constant_dynamic-slice_fusion.1.refs_4_) | copy-start | bytes 1548292
  200.6 13.0 %copy-start.5 = (bf16[576,896]{1,0:T(8,128)(2,1)S(1)}, bf16[576,896]{1,0:T(8,128)(2,1)}, u32[]{:S(2)}) copy-start(bf16[576,896]{1,0:T(8,128)(2,1)} %copy-done.4) | copy-start | bytes 3096580
  200.6 29.9 %all-to-all-start.6 = ((bf16[8,64,896]{2,1,0:T(8,128)(2,1)}), bf16[8,64,896]{2,1,0:T(8,128)(2,1)}, u32[]{:S(2)}, u32[]{:S(2)}) async-start(bf16[8,64,896]{2,1,0:T(8,128)(2,1)} %down_rows.6), calls=%async_computation.6 | async-start | bytes 1835008 | tf_op jit(solution)/shard_map/all_to_all | solution.py:259
  218.1 18.0 %copy-start.10 = (bf16[24,896]{1,0:T(8,128)(2,1)S(1)}, bf16[24,896]{1,0:T(8,128)(2,1)}, u32[]{:S(2)}) copy-start(bf16[24,896]{1,0:T(8,128)(2,1)} %copy-done.9) | copy-start | bytes 129028
  218.1 18.0 %copy-start.12 = (bf16[24,896]{1,0:T(8,128)(2,1)S(1)}, bf16[24,896]{1,0:T(8,128)(2,1)}, u32[]{:S(2)}) copy-start(bf16[24,896]{1,0:T(8,128)(2,1)} %copy-done.11) | copy-start | bytes 129028
  218.2 18.0 %copy-start.14 = (bf16[24,896]{1,0:T(8,128)(2,1)S(1)}, bf16[24,896]{1,0:T(8,128)(2,1)}, u32[]{:S(2)}) copy-start(bf16[24,896]{1,0:T(8,128)(2,1)} %copy-done.13) | copy-start | bytes 129028
  232.1 5.7 %collective-permute-start.24 = (bf16[24,896]{1,0:T(8,128)(2,1)S(1)}, bf16[24,896]{1,0:T(8,128)(2,1)S(1)}, u32[]{:S(2)}, u32[]{:S(2)}) collective-permute-start(bf16[24,896]{1,0:T(8,128)(2,1)S(1)} %get-tuple-element.380), channel_id=1, source_target_pairs={{0,192},{8,200},{16,208},{24,216},{32,224},{40,232},{48,240},{56,2... | collective-permute-start | bytes 129032 | tf_op jit(solution)/shard_map/ppermute | solution.py:276
  235.2 5.6 %collective-permute-start.25 = (bf16[24,896]{1,0:T(8,128)(2,1)S(1)}, bf16[24,896]{1,0:T(8,128)(2,1)S(1)}, u32[]{:S(2)}, u32[]{:S(2)}) collective-permute-start(bf16[24,896]{1,0:T(8,128)(2,1)S(1)} %get-tuple-element.379), channel_id=1, source_target_pairs={{0,128},{8,136},{16,144},{24,152},{32,160},{40,168},{48,176},{56,1... | collective-permute-start | bytes 129032 | tf_op jit(solution)/shard_map/ppermute | solution.py:276
  235.2 5.7 %collective-permute-start.26 = (bf16[24,896]{1,0:T(8,128)(2,1)S(1)}, bf16[24,896]{1,0:T(8,128)(2,1)S(1)}, u32[]{:S(2)}, u32[]{:S(2)}) collective-permute-start(bf16[24,896]{1,0:T(8,128)(2,1)S(1)} %get-tuple-element.378), channel_id=1, source_target_pairs={{0,64},{8,72},{16,80},{24,88},{32,96},{40,104},{48,112},{56,120},{... | collective-permute-start | bytes 129032 | tf_op jit(solution)/shard_map/ppermute | solution.py:276
  241.3 0.7 copy-start.3
  242.0 0.9 copy-start.1
Sparse Core Ops, SparseCore 0:
  31.7 27.3 all-gather.3
  60.9 34.2 all-gather.5
  132.4 26.5 all-gather.7

commit v3 on v2

--- a/solution.py
+++ b/solution.py
@@ -103,6 +103,42 @@
     )(lengths, queries, latent_cache.transpose(0, 2, 1))
 
 
+def values_kernel(terms, local, *refs):
+    latents, value_up, out = refs[:terms], refs[terms], refs[terms + 1]
+    heads = value_up.shape[0]
+    value_width = value_up.shape[2]
+    blocks, rows, _ = out.shape
+    slots = local.shape[1]
+    turn = lax.broadcasted_iota(jnp.int32, (rows, slots), 0)
+    pick = (turn == local[...]).astype(F32).astype(BF16)
+    for head in range(heads):
+        latent = jnp.concatenate([ref[head].astype(F32) for ref in latents], axis=0)
+        values = dot(latent.astype(BF16), value_up[head]).astype(BF16)
+        each = heads // blocks
+        columns = slice(head % each * value_width, (head % each + 1) * value_width)
+        out[head // each, :, columns] = dot(pick, values).astype(BF16)
+
+
+def packed_values(latents, value_up, local, blocks):
+    heads, slots, latent_width = latents[0].shape
+    value_width = value_up.shape[2]
+    terms = len(latents)
+    macs = terms * slots * heads * (latent_width + CAP_Z) * value_width
+    return pl.pallas_call(
+        functools.partial(values_kernel, terms),
+        out_shape=jax.ShapeDtypeStruct((blocks, CAP_Z, heads // blocks * value_width), BF16),
+        in_specs=[pl.BlockSpec(memory_space=pltpu.VMEM)] * (terms + 2),
+        out_specs=pl.BlockSpec(memory_space=pltpu.VMEM),
+        compiler_params=pltpu.CompilerParams(vmem_limit_bytes=32 * 2**20),
+        cost_estimate=pl.CostEstimate(
+            flops=2 * macs,
+            bytes_accessed=2 * heads * (terms * slots + value_width) * latent_width,
+            transcendentals=0,
+        ),
+        name="packed_values",
+    )(local[None], *latents, value_up)
+
+
 def down_kernel(terms, target, *refs):
     hiddens, downs, out = refs[:terms], refs[terms : 2 * terms], refs[2 * terms]
     total = dot_tn(hiddens[0][...], downs[0][...])
@@ -154,12 +190,10 @@
     return rows
 
 
-def exchange_weights(residual, out_proj, gate_up, down_proj, block):
+def exchange_parts(matrices, wholes, member, block):
     ranks = lax.axis_size("rank")
     members = lax.axis_size("group")
-    member = lax.axis_index("group")
     my_x = lax.div(lax.axis_index("rank"), ranks // NX)
-    matrices = [gate_up.T, down_proj, out_proj]
     parts = [part_rows(m.shape[0], members) for m in matrices]
 
     def cut(matrix, rows, x):
@@ -170,56 +204,84 @@
     for k in range(1, NX):
         x = lax.rem(my_x + k, NX)
         pieces = [cut(m, rows, x) for m, rows in zip(matrices, parts)]
-        piece = jnp.concatenate(pieces + [take_cols(residual, x, block)], axis=0)
-        got.append(lax.ppermute(piece, "rank", shift_x(ranks, k)))
-    res = [take_cols(residual, my_x, block)] + [g[sum(parts) :] for g in got]
-    return parts, got, matrices, jnp.concatenate(res, axis=0)
-
-
-def gather_weights(parts, got):
+        pieces += [take_cols(m, x, block) for m in wholes]
+        got.append(lax.ppermute(jnp.concatenate(pieces, axis=0), "rank", shift_x(ranks, k)))
+    return parts, got
+
+
+def gather_parts(parts, got):
     gathered, first = [], 0
     for rows in parts:
         gathered.append(jnp.stack([g[first : first + rows] for g in got]))
         first += rows
-    return [lax.all_gather(g, "group", axis=1, tiled=True) for g in gathered[::-1]][::-1]
-
-
-def own_blocks(matrices, my_x, block):
-    blocks = [take_cols(m, my_x, block) for m in matrices]
-    return [jnp.pad(blocks[0], ((0, EXTRA), (0, 0)))] + blocks[1:]
-
-
-def weight_blocks(own, gathered):
-    blocks = []
-    for mine, full in zip(own, gathered):
-        height = mine.shape[0]
-        full = jnp.pad(full, ((0, 0), (0, max(0, height - full.shape[1])), (0, 0)))
-        blocks.append([mine] + [full[k, :height] for k in range(NX - 1)])
-    return blocks
-
-
-def one_pass(index, values, res, own, gathered, gain, place, base, width):
+    return [lax.all_gather(g, "group", axis=1, tiled=True) for g in gathered]
+
+
+def weight_blocks(mine, full):
+    height = mine.shape[0]
+    full = jnp.pad(full, ((0, 0), (0, max(0, height - full.shape[1])), (0, 0)))
+    return [mine] + [full[k, :height] for k in range(NX - 1)]
+
+
+def x_order(my_x):
+    return lax.rem(my_x + NX - jnp.arange(NX, dtype=jnp.int32), NX)
+
+
+def at_z(array, my_z):
+    return lax.dynamic_index_in_dim(array, my_z, 1, False)
+
+
+def local_values(index, latents, value_up, pack):
+    local, _, _, passes_first = pack[1:5]
+    ranks = lax.axis_size("rank")
+    nz = ranks // NX
+    me = lax.axis_index("rank")
+    my_x, my_z = lax.div(me, nz), lax.rem(me, nz)
+    mine = at_z(local, my_z)[x_order(my_x)].reshape(-1)
+    mine = mine - jnp.where(index < passes_first, 0, CAP_Z)
+    return packed_values(latents, value_up, mine, nz)
+
+
+def project(index, sent, res, outs, pack):
+    place, _, counted, bases, passes_first = pack
+    ranks, slots = place.shape
+    nz = ranks // NX
+    me = lax.axis_index("rank")
+    my_x, my_z = lax.div(me, nz), lax.rem(me, nz)
+    row = index * CAP + jnp.arange(CAP, dtype=jnp.int32)
+    got = lax.all_to_all(
+        sent, "rank", split_axis=0, concat_axis=0, tiled=True, axis_index_groups=groups_z(ranks)
+    )
+
+    turn = jnp.arange(CAP_Z, dtype=jnp.int32)
+    which = jnp.where(index < passes_first, 0, 1)
+    target = jnp.where(turn < counted[which][:, None], bases[which][:, None] + turn, -1)
+    pick = (row[:, None] == target.reshape(-1)[None, :]).astype(BF16)
+    packed = dot(pick, got.reshape(nz * CAP_Z, -1)).astype(BF16)
+    heads = [packed] + [lax.ppermute(packed, "rank", perm) for perm in sends(ranks)]
+
+    place_z = at_z(place.reshape(NX, nz, slots), my_z)
+    owners = place_z[x_order(my_x)].reshape(-1)
+    part = dot((row[:, None] == owners[None, :]).astype(BF16), res)
+    for head, out in zip(heads, outs):
+        part = part + dot(head, out)
+    return part.astype(BF16)
+
+
+def finish(index, part, joins, downs, gain, pack, width):
+    place, _, _, bases, passes_first = pack
     ranks, slots = place.shape
     nz = ranks // NX
     block = gain.shape[0]
     rows_z = CAP // nz
     me = lax.axis_index("rank")
     my_x, my_z = lax.div(me, nz), lax.rem(me, nz)
-    joins, downs, outs = weight_blocks(own, gathered)
     row = index * CAP + jnp.arange(CAP, dtype=jnp.int32)
-
-    pick = (row[:, None] == place.reshape(-1)[None, :]).astype(BF16)
-    packed = dot(pick, values).astype(BF16)
-    heads = [packed] + [lax.ppermute(packed, "rank", perm) for perm in sends(ranks)]
-
-    place_z = lax.dynamic_index_in_dim(place.reshape(NX, nz, slots), my_z, 1, False)
-    order = lax.rem(my_x + NX - jnp.arange(NX, dtype=jnp.int32), NX)
-    owners = place_z[order].reshape(-1)
-    part = dot((row[:, None] == owners[None, :]).astype(BF16), res)
-    for head, out in zip(heads, outs):
-        part = part + dot(head, out)
+    place_z = at_z(place.reshape(NX, nz, slots), my_z)
+    order = x_order(my_x)
+    base = bases[jnp.where(index < passes_first, 0, 1)]
     got = lax.all_to_all(
-        part.astype(BF16).reshape(nz, rows_z, block),
+        part.reshape(nz, rows_z, block),
         "rank",
         split_axis=0,
         concat_axis=0,
@@ -305,8 +367,12 @@
     place = jnp.where(
         local < CAP_Z, base_first[None, :, None] + local, base_rest[None, :, None] + local - CAP_Z
     )
-    place = jnp.where(slot < grid[:, :, None], place, -1).reshape(ranks, slots)
-    return place, base_first, base_rest, passes, passes + lax.div(jnp.sum(rest) + CAP - 1, CAP)
+    live = slot < grid[:, :, None]
+    place = jnp.where(live, place, -1).reshape(ranks, slots)
+    local = jnp.where(live, local, -1)
+    counted, bases = jnp.stack([first, rest]), jnp.stack([base_first, base_rest])
+    pack = (place, local, counted, bases, passes)
+    return pack, passes + lax.div(jnp.sum(rest) + CAP - 1, CAP)
 
 
 def per_device(
@@ -328,29 +394,49 @@
     block = width // NX
     my_x = lax.div(lax.axis_index("rank"), ranks // NX)
     gain = lax.dynamic_slice_in_dim(norm_gain, my_x * block, block, 0).astype(F32)
-    parts, got, own, res = exchange_weights(residual, out_proj, gate_up, down_proj, block)
+    member = lax.axis_index("group")
+    pack, passes = packing(counts, slots)
+
+    parts, got = exchange_parts([out_proj], [residual], member, block)
     latent = attend(queries, latent_cache, lengths, latent_width, value_width)
     got = lax.optimization_barrier((got, latent))[0]
-    gathered = gather_weights(parts, got)
-    own = own_blocks(own, my_x, block)
-    arrived = lax.all_to_all(
-        latent.reshape(ranks, -1, slots, latent_width), "rank", split_axis=0, concat_axis=0, tiled=True
-    )
-    arrived = arrived.transpose(0, 2, 1, 3).reshape(slots * ranks, -1, latent_width)
-    values = jnp.einsum("shc,hcv->shv", arrived, value_up, preferred_element_type=F32)
-    values = values.astype(BF16).reshape(slots * ranks, -1)
-    place, base_first, base_rest, passes_first, passes = packing(counts, slots)
-
-    def run(index):
-        base = jnp.where(index < passes_first, base_first, base_rest)
-        return one_pass(index, values, res, own, gathered, gain, place, base, width)
+    value_up = lax.all_gather(
+        value_up, "rank", axis=0, tiled=True, axis_index_groups=groups_z(ranks)
+    )
+    (projs,) = gather_parts(parts, got)
+    my_proj = take_cols(out_proj, my_x, block)
+    res = [take_cols(residual, my_x, block)] + [g[parts[0] :] for g in got]
+    res = jnp.concatenate(res, axis=0)
+
+    each = latent.shape[0] // NX
+
+    def heads_of(x):
+        return lax.dynamic_slice_in_dim(latent, x * each, each, 0)
+
+    latents = [heads_of(my_x)] + [
+        lax.ppermute(heads_of(lax.rem(my_x + k, NX)), "rank", shift_x(ranks, k))
+        for k in range(1, NX)
+    ]
+    sent = local_values(0, latents, value_up, pack)
+
+    member = lax.optimization_barrier((member, sent))[0]
+    parts, got = exchange_parts([gate_up.T, down_proj], [], member, block)
+    feeds = gather_parts(parts, got)
+    my_join = jnp.pad(take_cols(gate_up.T, my_x, block), ((0, EXTRA), (0, 0)))
+    my_down = take_cols(down_proj, my_x, block)
+
+    def run(index, sent):
+        part = project(index, sent, res, weight_blocks(my_proj, projs), pack)
+        joins = weight_blocks(my_join, feeds[0])
+        downs = weight_blocks(my_down, feeds[1])
+        return finish(index, part, joins, downs, gain, pack, width)
 
     def more(state):
         index, out = state
-        rows, inside = run(index)
+        rows, inside = run(index, local_values(index, latents, value_up, pack))
         return index + 1, jnp.where(inside[:, None], rows, out)
 
-    rows, inside = run(0)
+    rows, inside = run(0, sent)
     out = jnp.where(inside[:, None], rows, jnp.zeros((), BF16))
     return lax.while_loop(lambda state: state[0] < passes, more, (jnp.int32(1), out))[1]
 

time: 251 us -> 256 us (1.020); the launches traced: 249 us -> 251 us
  starting transfers between devices: 46.3 us -> 62.2 us
  waiting for transfers between devices: 118 us -> 103 us
  Pallas kernels: 12.3 us -> 18.3 us
    all_to_all x4, waiting for transfers between devices: 81.3 us -> 53.2 us  [the longest x1 17.2 us: finish(): lax.all_to_all(jnp.broadcast_to(mixed[None], (nz, rows_z, block)), 'rank'...]
    ppermute x15 -> x21, starting transfers between devices: 20.1 us -> 45.2 us  [the longest x3 19.2 us: finish(): lax.ppermute(hidden, 'rank', perm)]
    all_to_all x4, starting transfers between devices: 25.8 us -> 16.9 us  [the longest x1 5.46 us: project(): lax.all_to_all(sent, 'rank', split_axis=0, concat_axis=0, tiled=True, axi...]
    all_gather x3 -> x4, waiting for transfers between devices: 0.04 us -> 7.89 us  [the longest x1 7.85 us: per_device(): lax.all_gather(value_up, 'rank', axis=0, tiled=True, axis_index_groups=gr...]
    pallas_call x0 -> x1, Pallas kernels: none -> 5.45 us  [packed_values(): pl.pallas_call(functools.partial(values_kernel, terms), out_shape=jax.Sha...]
    ppermute x15 -> x21, waiting for transfers between devices: 36.6 us -> 41.5 us  [the longest x3 13.3 us: finish(): lax.ppermute(share(join), 'rank', perm)]
  transfers between devices with their start and end apart: 22 -> 29, of which waited for: 14 -> 19; matrix products, arithmetic and copies ran while one was open for 17% -> 17% of each run, Pallas kernels for 3% -> 5%
where the time goes in v3:
time: 256 us; the launch traced here: 251 us
  waiting for transfers between devices  103 us (40%)
  starting transfers between devices  62.2 us (24%)
  between operations  22.5 us (9%)
  Pallas kernels  18.3 us (7%)
  local copies, waits for them, and re-layouts  18.1 us (7%)
  matrix products  13.9 us (5%)
  other arithmetic  12.9 us (5%)
    ppermute x3, starting transfers between devices, finish(): lax.ppermute(hidden, 'rank', perm)  19.2 us
    all_to_all x1, waiting for transfers between devices, finish(): lax.all_to_all(jnp.broadcast_to(mixed[None], (nz, rows_z, block)), 'rank'...  17.2 us
    all_to_all x1, waiting for transfers between devices, finish(): lax.all_to_all(part.reshape(nz, rows_z, block), 'rank', split_axis=0, con...  16.6 us
    ppermute x3, waiting for transfers between devices, finish(): lax.ppermute(share(join), 'rank', perm)  13.3 us
    all_to_all x1, waiting for transfers between devices, finish(): lax.all_to_all(sent, 'rank', split_axis=0, concat_axis=0, tiled=True, axi...  12.9 us
    ppermute x6, starting transfers between devices, exchange_parts(): lax.ppermute(jnp.concatenate(pieces, axis=0), 'rank', shift_x(ranks, k))  11.2 us
    ppermute x6, waiting for transfers between devices, exchange_parts(): lax.ppermute(jnp.concatenate(pieces, axis=0), 'rank', shift_x(ranks, k))  10.9 us
    pallas_call x1, Pallas kernels, attend(): pl.pallas_call(functools.partial(attend_kernel, scale, step_slots), out_s...  8.08 us
  transfers between devices with their start and end apart: 29, of which 19 were waited for; matrix products, arithmetic and copies ran while one was open for 17% of the time, Pallas kernels for 5%

profile of v3, /device:TPU:24, one launch (start us, length us, event | category | flops | bytes accessed | tf_op | source)
XLA Modules:
  0.0 251.1 jit_solution(14846366762057896582)
XLA Ops:
  7.4 8.1 %attend.1 = bf16[64,24,512]{2,1,0:T(8,128)(2,1)} custom-call(s32[24]{0:T(128)} %lengths.1, bf16[24,64,576]{2,1,0:T(8,128)(2,1)} %queries.1, bf16[24,576,128]{2,1,0:T(8,128)(2,1)} %bitcast.376), custom_call_target="tpu_custom_call" | custom-call | flops 427819008 | bytes 10027008 | tf_op jit(solution)/shard_map/attend/pallas_call | solution.py:85
  15.4 2.3 constant_dynamic-slice_fusion.7
  17.7 1.5 collective-permute-start.15
  20.2 1.6 collective-permute-start.12
  21.8 1.8 collective-permute-start.13
  23.6 2.2 collective-permute-start.14
  28.7 3.4 %collective-permute-done.12 = bf16[56,896]{1,0:T(8,128)(2,1)S(1)} collective-permute-done((bf16[56,896]{1,0:T(8,128)(2,1)S(1)}, bf16[56,896]{1,0:T(8,128)(2,1)S(1)}, u32[]{:S(2)}, u32[]{:S(2)}) %collective-permute-start.12) | collective-permute-done | bytes 100384 | tf_op jit(solution)/shard_map/ppermute | solution.py:208
  32.1 2.5 %collective-permute-start.17 = (bf16[16,24,512]{2,1,0:T(8,128)(2,1)S(1)}, bf16[16,24,512]{2,1,0:T(8,128)(2,1)}, u32[]{:S(2)}, u32[]{:S(2)}) collective-permute-start(bf16[16,24,512]{2,1,0:T(8,128)(2,1)S(1)} %get-tuple-element.510), channel_id=1, source_target_pairs={{0,192},{8,200},{16,208},{24,216},{32,224},{40,232},{48,240},{56,2... | collective-permute-start | bytes 1179656 | tf_op jit(solution)/shard_map/ppermute | solution.py:417
  34.6 1.6 collective-permute-done.13
  38.4 5.2 %collective-permute-done.16.refs_2_ = bf16[16,24,512]{2,1,0:T(8,128)(2,1)} collective-permute-done((bf16[16,24,512]{2,1,0:T(8,128)(2,1)S(1)}, bf16[16,24,512]{2,1,0:T(8,128)(2,1)}, u32[]{:S(2)}, u32[]{:S(2)}) %collective-permute-start.16) | collective-permute-done | bytes 393248 | tf_op jit(solution)/shard_map/ppermute | solution.py:417
  43.6 2.0 collective-permute-done.17.refs_3_
  45.5 7.8 %all-gather.5.cloned.1.call-done.refs_4_ = bf16[16,512,128]{2,1,0:T(8,128)(2,1)} async-done(((bf16[2,512,128]{2,1,0:T(8,128)(2,1)}), bf16[16,512,128]{2,1,0:T(8,128)(2,1)}) %all-gather.5.cloned.1.call-update) | async-done | bytes 2097168 | tf_op jit(solution)/shard_map/all_gather | solution.py:403
  53.4 5.5 %packed_values.7 = bf16[8,64,256]{2,1,0:T(8,128)(2,1)} custom-call(s32[1,96]{1,0:T(1,128)S(1)} %sub.237.local, bf16[16,24,512]{2,1,0:T(8,128)(2,1)} %get-tuple-element.732.refs_0_, bf16[16,24,512]{2,1,0:T(8,128)(2,1)} %collective-permute-done.15.refs_1_, bf16[16,24,512]{2,1,0:T(8,128)(2,1)} %collective-permute-done.16.refs_2_, ...), custom_call_target="tpu_custom_call" | custom-call | flops 226492416 | bytes 3670016 | tf_op jit(solution)/shard_map/packed_values/pallas_call | solution.py:127
  61.1 1.5 collective-permute-start.21
  62.6 2.3 collective-permute-start.22
  64.9 1.8 collective-permute-start.23
  66.7 3.2 %collective-permute-done.21 = bf16[144,896]{1,0:T(8,128)(2,1)S(1)} collective-permute-done((bf16[144,896]{1,0:T(8,128)(2,1)S(1)}, bf16[144,896]{1,0:T(8,128)(2,1)S(1)}, u32[]{:S(2)}, u32[]{:S(2)}) %collective-permute-start.21) | collective-permute-done | bytes 258080 | tf_op jit(solution)/shard_map/ppermute | solution.py:208
  69.9 2.7 %collective-permute-done.22 = bf16[144,896]{1,0:T(8,128)(2,1)S(1)} collective-permute-done((bf16[144,896]{1,0:T(8,128)(2,1)S(1)}, bf16[144,896]{1,0:T(8,128)(2,1)S(1)}, u32[]{:S(2)}, u32[]{:S(2)}) %collective-permute-start.22) | collective-permute-done | bytes 258080 | tf_op jit(solution)/shard_map/ppermute | solution.py:208
  74.5 5.5 %all-to-all-start.4 = ((bf16[8,64,256]{2,1,0:T(8,128)(2,1)}), bf16[8,64,256]{2,1,0:T(8,128)(2,1)S(1)}, u32[]{:S(2)}, u32[]{:S(2)}) async-start(bf16[8,64,256]{2,1,0:T(8,128)(2,1)} %packed_values.7), calls=%async_computation.4 | async-start | bytes 524288 | tf_op jit(solution)/shard_map/all_to_all | solution.py:252
  82.0 1.8 constant_dynamic-slice_fusion.6
  83.9 6.5 %all-to-all-done.4 = bf16[8,64,256]{2,1,0:T(8,128)(2,1)S(1)} async-done(((bf16[8,64,256]{2,1,0:T(8,128)(2,1)}), bf16[8,64,256]{2,1,0:T(8,128)(2,1)S(1)}, u32[]{:S(2)}, u32[]{:S(2)}) %all-to-all-start.4) | async-done | bytes 262176 | tf_op jit(solution)/shard_map/all_to_all | solution.py:252
  90.7 2.1 collective-permute-start.19
  92.8 1.9 collective-permute-start.20
  94.9 1.5 fusion.106
  96.7 1.4 collective-permute-done.19
  98.2 1.5 fusion.71
  102.9 3.5 %all-to-all-start.5 = ((bf16[8,48,896]{2,1,0:T(8,128)(2,1)}), bf16[8,48,896]{2,1,0:T(8,128)(2,1)S(1)}, u32[]{:S(2)}, u32[]{:S(2)}) async-start(bf16[8,48,896]{2,1,0:T(8,128)(2,1)} %bitcast.377), calls=%async_computation.5 | async-start | bytes 1376256 | tf_op jit(solution)/shard_map/all_to_all | solution.py:283
  109.1 16.6 %all-to-all-done.5 = bf16[8,48,896]{2,1,0:T(8,128)(2,1)S(1)} async-done(((bf16[8,48,896]{2,1,0:T(8,128)(2,1)}), bf16[8,48,896]{2,1,0:T(8,128)(2,1)S(1)}, u32[]{:S(2)}, u32[]{:S(2)}) %all-to-all-start.5) | async-done | bytes 688160 | tf_op jit(solution)/shard_map/all_to_all | solution.py:283
  126.7 3.5 %all-to-all-start.6 = ((bf16[8,48,896]{2,1,0:T(8,128)(2,1)}), bf16[8,48,896]{2,1,0:T(8,128)(2,1)S(1)}, u32[]{:S(2)}, u32[]{:S(2)}) async-start(bf16[8,48,896]{2,1,0:T(8,128)(2,1)} %broadcast_in_dim.210), calls=%async_computation.6 | async-start | bytes 1376256 | tf_op jit(solution)/shard_map/all_to_all | solution.py:292
  131.8 17.2 %all-to-all-done.6 = bf16[8,48,896]{2,1,0:T(8,128)(2,1)S(1)} async-done(((bf16[8,48,896]{2,1,0:T(8,128)(2,1)}), bf16[8,48,896]{2,1,0:T(8,128)(2,1)S(1)}, u32[]{:S(2)}, u32[]{:S(2)}) %all-to-all-start.6) | async-done | bytes 688160 | tf_op jit(solution)/shard_map/all_to_all | solution.py:292
  149.4 2.1 fusion.64
  151.5 2.1 fusion.65
  153.7 2.1 fusion.66
  155.8 2.0 collective-permute-start.26
  157.8 1.9 constant_dynamic-slice_fusion.5.refs_4_
  161.0 3.8 %collective-permute-done.24 = bf16[592,384]{1,0:T(8,128)(2,1)S(1)} collective-permute-done((bf16[592,384]{1,0:T(8,128)(2,1)S(1)}, bf16[592,384]{1,0:T(8,128)(2,1)S(1)}, u32[]{:S(2)}, u32[]{:S(2)}) %collective-permute-start.24) | collective-permute-done | bytes 454688 | tf_op jit(solution)/shard_map/ppermute | solution.py:313
  164.9 3.7 %collective-permute-done.25 = bf16[592,384]{1,0:T(8,128)(2,1)S(1)} collective-permute-done((bf16[592,384]{1,0:T(8,128)(2,1)S(1)}, bf16[592,384]{1,0:T(8,128)(2,1)S(1)}, u32[]{:S(2)}, u32[]{:S(2)}) %collective-permute-start.25) | collective-permute-done | bytes 454688 | tf_op jit(solution)/shard_map/ppermute | solution.py:313
  168.6 5.7 %collective-permute-done.26 = bf16[592,384]{1,0:T(8,128)(2,1)S(1)} collective-permute-done((bf16[592,384]{1,0:T(8,128)(2,1)S(1)}, bf16[592,384]{1,0:T(8,128)(2,1)S(1)}, u32[]{:S(2)}, u32[]{:S(2)}) %collective-permute-start.26) | collective-permute-done | bytes 454688 | tf_op jit(solution)/shard_map/ppermute | solution.py:313
  175.5 2.1 collective-permute-start.28
  177.6 17.1 %collective-permute-start.29 = (bf16[288,384]{1,0:T(8,128)(2,1)S(1)}, bf16[288,384]{1,0:T(8,128)(2,1)S(1)}, u32[]{:S(2)}, u32[]{:S(2)}) collective-permute-start(bf16[288,384]{1,0:T(8,128)(2,1)S(1)} %fusion.73.refs_0_), channel_id=1, source_target_pairs={{0,192},{8,200},{16,208},{24,216},{32,224},{40,232},{48,240},{56,2... | collective-permute-start | bytes 663560 | tf_op jit(solution)/shard_map/ppermute | solution.py:318
  194.6 1.5 slice_bitcast_fusion.9
  196.1 3.6 %collective-permute-done.29.refs_3_ = bf16[288,384]{1,0:T(8,128)(2,1)S(1)} collective-permute-done((bf16[288,384]{1,0:T(8,128)(2,1)S(1)}, bf16[288,384]{1,0:T(8,128)(2,1)S(1)}, u32[]{:S(2)}, u32[]{:S(2)}) %collective-permute-start.29) | collective-permute-done | bytes 221216 | tf_op jit(solution)/shard_map/ppermute | solution.py:318
  199.8 4.7 %down_rows.7 = bf16[8,64,896]{2,1,0:T(8,128)(2,1)} custom-call(s32[8]{0:T(128)S(1)} %fusion.94.target, bf16[288,384]{1,0:T(8,128)(2,1)S(1)} %fusion.73.refs_0_, bf16[288,384]{1,0:T(8,128)(2,1)S(1)} %collective-permute-done.27.refs_1_, bf16[288,384]{1,0:T(8,128)(2,1)S(1)} %collective-permute-done.28.refs_2_, ...), custom_call_target="tpu_custom_call" | custom-call | flops 1145044992 | bytes 3866624 | tf_op jit(solution)/shard_map/down_rows/pallas_call | solution.py:162
  204.5 4.4 %all-to-all-start.7 = ((bf16[8,64,896]{2,1,0:T(8,128)(2,1)}), bf16[8,64,896]{2,1,0:T(8,128)(2,1)}, u32[]{:S(2)}, u32[]{:S(2)}) async-start(bf16[8,64,896]{2,1,0:T(8,128)(2,1)} %down_rows.7), calls=%async_computation.7 | async-start | bytes 1835008 | tf_op jit(solution)/shard_map/all_to_all | solution.py:321
  220.4 12.9 %all-to-all-done.7 = bf16[8,64,896]{2,1,0:T(8,128)(2,1)} async-done(((bf16[8,64,896]{2,1,0:T(8,128)(2,1)}), bf16[8,64,896]{2,1,0:T(8,128)(2,1)}, u32[]{:S(2)}, u32[]{:S(2)}) %all-to-all-start.7) | async-done | bytes 917536 | tf_op jit(solution)/shard_map/all_to_all | solution.py:321
  233.3 1.3 reduce_sum.108
  234.9 2.5 collective-permute-start.30
  239.2 3.7 %collective-permute-done.31 = bf16[24,896]{1,0:T(8,128)(2,1)S(1)} collective-permute-done((bf16[24,896]{1,0:T(8,128)(2,1)S(1)}, bf16[24,896]{1,0:T(8,128)(2,1)S(1)}, u32[]{:S(2)}, u32[]{:S(2)}) %collective-permute-start.31) | collective-permute-done | bytes 43040 | tf_op jit(solution)/shard_map/ppermute | solution.py:338
  (135 shorter events, 31.7 us)
Async XLA Ops:
  6.5 46.9 %all-gather.5.cloned.1.call-start = ((), (), s32[]{:S(2)}) async-start(), calls=%async_computation.8 | async-start | bytes 2359296 | tf_op jit(solution)/shard_map/all_gather | solution.py:403
  7.3 89.5 %all-gather.7.cloned.1.call-start = ((), (), s32[]{:S(2)}) async-start(), calls=%async_computation.9 | async-start | bytes 1548288 | tf_op jit(solution)/shard_map/all_gather | solution.py:217
  15.4 3.8 %copy-start.13 = (bf16[24,3584]{1,0:T(8,128)(2,1)S(1)}, bf16[24,3584]{1,0:T(8,128)(2,1)}, u32[]{:S(2)}) copy-start(bf16[24,3584]{1,0:T(8,128)(2,1)} %param.12) | copy-start | bytes 516100
  15.4 10.4 %copy-start.14 = (s32[32]{0:T(128)S(1)}, s32[32]{0:T(128)}, u32[]{:S(2)}) copy-start(s32[32]{0:T(128)} %param.16) | copy-start | bytes 388
  17.7 20.7 %collective-permute-start.15 = (bf16[16,24,512]{2,1,0:T(8,128)(2,1)S(1)}, bf16[16,24,512]{2,1,0:T(8,128)(2,1)}, u32[]{:S(2)}, u32[]{:S(2)}) collective-permute-start(bf16[16,24,512]{2,1,0:T(8,128)(2,1)S(1)} %get-tuple-element.512), channel_id=1, source_target_pairs={{0,64},{8,72},{16,80},{24,88},{32,96},{40,104},{48,112},{56,120},{... | collective-permute-start | bytes 1179656 | tf_op jit(solution)/shard_map/ppermute | solution.py:417
  19.2 77.1 %copy-start.8 = (bf16[24,896]{1,0:T(8,128)(2,1)}, bf16[24,896]{1,0:T(8,128)(2,1)S(1)}, u32[]{:S(2)}) copy-start(bf16[24,896]{1,0:T(8,128)(2,1)S(1)} %get-tuple-element.523) | copy-start | bytes 129028
  20.2 11.9 %collective-permute-start.12 = (bf16[56,896]{1,0:T(8,128)(2,1)S(1)}, bf16[56,896]{1,0:T(8,128)(2,1)S(1)}, u32[]{:S(2)}, u32[]{:S(2)}) collective-permute-start(bf16[56,896]{1,0:T(8,128)(2,1)S(1)} %pad_maximum_fusion.7), channel_id=1, source_target_pairs={{0,64},{8,72},{16,80},{24,88},{32,96},{40,104},{48,112},{56,120},{... | collective-permute-start | bytes 301064 | tf_op jit(solution)/shard_map/ppermute | solution.py:208
  21.8 14.5 %collective-permute-start.13 = (bf16[56,896]{1,0:T(8,128)(2,1)S(1)}, bf16[56,896]{1,0:T(8,128)(2,1)S(1)}, u32[]{:S(2)}, u32[]{:S(2)}) collective-permute-start(bf16[56,896]{1,0:T(8,128)(2,1)S(1)} %pad_maximum_fusion.8), channel_id=1, source_target_pairs={{0,128},{8,136},{16,144},{24,152},{32,160},{40,168},{48,176},{56,1... | collective-permute-start | bytes 301064 | tf_op jit(solution)/shard_map/ppermute | solution.py:208
  23.6 12.6 %collective-permute-start.14 = (bf16[56,896]{1,0:T(8,128)(2,1)S(1)}, bf16[56,896]{1,0:T(8,128)(2,1)S(1)}, u32[]{:S(2)}, u32[]{:S(2)}) collective-permute-start(bf16[56,896]{1,0:T(8,128)(2,1)S(1)} %pad_maximum_fusion.9), channel_id=1, source_target_pairs={{0,192},{8,200},{16,208},{24,216},{32,224},{40,232},{48,240},{56,2... | collective-permute-start | bytes 301064 | tf_op jit(solution)/shard_map/ppermute | solution.py:208
  27.9 15.6 %collective-permute-start.16 = (bf16[16,24,512]{2,1,0:T(8,128)(2,1)S(1)}, bf16[16,24,512]{2,1,0:T(8,128)(2,1)}, u32[]{:S(2)}, u32[]{:S(2)}) collective-permute-start(bf16[16,24,512]{2,1,0:T(8,128)(2,1)S(1)} %get-tuple-element.511), channel_id=1, source_target_pairs={{0,128},{8,136},{16,144},{24,152},{32,160},{40,168},{48,176},{56,1... | collective-permute-start | bytes 1179656 | tf_op jit(solution)/shard_map/ppermute | solution.py:417
  32.1 13.5 %collective-permute-start.17 = (bf16[16,24,512]{2,1,0:T(8,128)(2,1)S(1)}, bf16[16,24,512]{2,1,0:T(8,128)(2,1)}, u32[]{:S(2)}, u32[]{:S(2)}) collective-permute-start(bf16[16,24,512]{2,1,0:T(8,128)(2,1)S(1)} %get-tuple-element.510), channel_id=1, source_target_pairs={{0,192},{8,200},{16,208},{24,216},{32,224},{40,232},{48,240},{56,2... | collective-permute-start | bytes 1179656 | tf_op jit(solution)/shard_map/ppermute | solution.py:417
  37.0 112.4 %all-gather.9.cloned.1.call-start = ((), (), s32[]{:S(2)}) async-start(), calls=%async_computation.10 | async-start | bytes 4644864 | tf_op jit(solution)/shard_map/all_gather | solution.py:217
  61.1 8.8 %collective-permute-start.21 = (bf16[144,896]{1,0:T(8,128)(2,1)S(1)}, bf16[144,896]{1,0:T(8,128)(2,1)S(1)}, u32[]{:S(2)}, u32[]{:S(2)}) collective-permute-start(bf16[144,896]{1,0:T(8,128)(2,1)S(1)} %pad_maximum_fusion.1), channel_id=1, source_target_pairs={{0,64},{8,72},{16,80},{24,88},{32,96},{40,104},{48,112},{56,120},{... | collective-permute-start | bytes 774152 | tf_op jit(solution)/shard_map/ppermute | solution.py:208
  62.6 10.1 %collective-permute-start.22 = (bf16[144,896]{1,0:T(8,128)(2,1)S(1)}, bf16[144,896]{1,0:T(8,128)(2,1)S(1)}, u32[]{:S(2)}, u32[]{:S(2)}) collective-permute-start(bf16[144,896]{1,0:T(8,128)(2,1)S(1)} %pad_maximum_fusion.2), channel_id=1, source_target_pairs={{0,128},{8,136},{16,144},{24,152},{32,160},{40,168},{48,176},{56,1... | collective-permute-start | bytes 774152 | tf_op jit(solution)/shard_map/ppermute | solution.py:208
  64.9 7.8 %collective-permute-start.23 = (bf16[144,896]{1,0:T(8,128)(2,1)S(1)}, bf16[144,896]{1,0:T(8,128)(2,1)S(1)}, u32[]{:S(2)}, u32[]{:S(2)}) collective-permute-start(bf16[144,896]{1,0:T(8,128)(2,1)S(1)} %pad_maximum_fusion.3), channel_id=1, source_target_pairs={{0,192},{8,200},{16,208},{24,216},{32,224},{40,232},{48,240},{56,2... | collective-permute-start | bytes 774152 | tf_op jit(solution)/shard_map/ppermute | solution.py:208
  69.9 4.6 %copy-start.10 = (bf16[144,896]{1,0:T(8,128)(2,1)}, bf16[144,896]{1,0:T(8,128)(2,1)S(1)}, u32[]{:S(2)}) copy-start(bf16[144,896]{1,0:T(8,128)(2,1)S(1)} %collective-permute-done.21) | copy-start | bytes 774148
  72.7 1.8 copy-start.11
  72.7 0.8 copy-start.12
  74.5 15.9 %all-to-all-start.4 = ((bf16[8,64,256]{2,1,0:T(8,128)(2,1)}), bf16[8,64,256]{2,1,0:T(8,128)(2,1)S(1)}, u32[]{:S(2)}, u32[]{:S(2)}) async-start(bf16[8,64,256]{2,1,0:T(8,128)(2,1)} %packed_values.7), calls=%async_computation.4 | async-start | bytes 524288 | tf_op jit(solution)/shard_map/all_to_all | solution.py:252
  83.9 12.8 %copy-start.6 = (bf16[24,896]{1,0:T(8,128)(2,1)}, bf16[24,896]{1,0:T(8,128)(2,1)S(1)}, u32[]{:S(2)}) copy-start(bf16[24,896]{1,0:T(8,128)(2,1)S(1)} %slice.233) | copy-start | bytes 129028
  90.7 7.5 %collective-permute-start.19 = (bf16[384,256]{1,0:T(8,128)(2,1)S(1)}, bf16[384,256]{1,0:T(8,128)(2,1)}, u32[]{:S(2)}, u32[]{:S(2)}) collective-permute-start(bf16[384,256]{1,0:T(8,128)(2,1)S(1)} %convolution_convert_fusion.1), channel_id=1, source_target_pairs={{0,128},{8,136},{16,144},{24,152},{32,160},{40,168},{48,176},{56,1... | collective-permute-start | bytes 589832 | tf_op jit(solution)/shard_map/ppermute | solution.py:261
  92.8 6.8 %collective-permute-start.20 = (bf16[384,256]{1,0:T(8,128)(2,1)S(1)}, bf16[384,256]{1,0:T(8,128)(2,1)}, u32[]{:S(2)}, u32[]{:S(2)}) collective-permute-start(bf16[384,256]{1,0:T(8,128)(2,1)S(1)} %convolution_convert_fusion.1), channel_id=1, source_target_pairs={{0,192},{8,200},{16,208},{24,216},{32,224},{40,232},{48,240},{56,2... | collective-permute-start | bytes 589832 | tf_op jit(solution)/shard_map/ppermute | solution.py:261
  94.7 6.9 %collective-permute-start.18 = (bf16[384,256]{1,0:T(8,128)(2,1)S(1)}, bf16[384,256]{1,0:T(8,128)(2,1)S(1)}, u32[]{:S(2)}, u32[]{:S(2)}) collective-permute-start(bf16[384,256]{1,0:T(8,128)(2,1)S(1)} %convolution_convert_fusion.1), channel_id=1, source_target_pairs={{0,64},{8,72},{16,80},{24,88},{32,96},{40,104},{48,112},{56,120},{... | collective-permute-start | bytes 589832 | tf_op jit(solution)/shard_map/ppermute | solution.py:261
  96.7 3.0 %copy-start = (bf16[3,256,896]{2,1,0:T(8,128)(2,1)S(1)}, bf16[3,256,896]{2,1,0:T(8,128)(2,1)}, u32[]{:S(2)}) copy-start(bf16[3,256,896]{2,1,0:T(8,128)(2,1)} %all-gather.7.cloned.1.call-done) | copy-start | bytes 4128772
  102.9 22.8 %all-to-all-start.5 = ((bf16[8,48,896]{2,1,0:T(8,128)(2,1)}), bf16[8,48,896]{2,1,0:T(8,128)(2,1)S(1)}, u32[]{:S(2)}, u32[]{:S(2)}) async-start(bf16[8,48,896]{2,1,0:T(8,128)(2,1)} %bitcast.377), calls=%async_computation.5 | async-start | bytes 1376256 | tf_op jit(solution)/shard_map/all_to_all | solution.py:283
  126.7 22.3 %all-to-all-start.6 = ((bf16[8,48,896]{2,1,0:T(8,128)(2,1)}), bf16[8,48,896]{2,1,0:T(8,128)(2,1)S(1)}, u32[]{:S(2)}, u32[]{:S(2)}) async-start(bf16[8,48,896]{2,1,0:T(8,128)(2,1)} %broadcast_in_dim.210), calls=%async_computation.6 | async-start | bytes 1376256 | tf_op jit(solution)/shard_map/all_to_all | solution.py:292
  130.2 64.4 %all-gather.11.cloned.1.call-start = ((), (), s32[]{:S(2)}) async-start(), calls=%async_computation.11 | async-start | bytes 2322432 | tf_op jit(solution)/shard_map/all_gather | solution.py:217
  151.4 13.4 %collective-permute-start.24 = (bf16[592,384]{1,0:T(8,128)(2,1)S(1)}, bf16[592,384]{1,0:T(8,128)(2,1)S(1)}, u32[]{:S(2)}, u32[]{:S(2)}) collective-permute-start(bf16[592,384]{1,0:T(8,128)(2,1)S(1)} %fusion.64), channel_id=1, source_target_pairs={{0,192},{8,200},{16,208},{24,216},{32,224},{40,232},{48,240},{56,2... | collective-permute-start | bytes 1363976 | tf_op jit(solution)/shard_map/ppermute | solution.py:313
  153.6 15.0 %collective-permute-start.25 = (bf16[592,384]{1,0:T(8,128)(2,1)S(1)}, bf16[592,384]{1,0:T(8,128)(2,1)S(1)}, u32[]{:S(2)}, u32[]{:S(2)}) collective-permute-start(bf16[592,384]{1,0:T(8,128)(2,1)S(1)} %fusion.65), channel_id=1, source_target_pairs={{0,128},{8,136},{16,144},{24,152},{32,160},{40,168},{48,176},{56,1... | collective-permute-start | bytes 1363976 | tf_op jit(solution)/shard_map/ppermute | solution.py:313
  155.8 18.5 %collective-permute-start.26 = (bf16[592,384]{1,0:T(8,128)(2,1)S(1)}, bf16[592,384]{1,0:T(8,128)(2,1)S(1)}, u32[]{:S(2)}, u32[]{:S(2)}) collective-permute-start(bf16[592,384]{1,0:T(8,128)(2,1)S(1)} %fusion.66), channel_id=1, source_target_pairs={{0,64},{8,72},{16,80},{24,88},{32,96},{40,104},{48,112},{56,120},{... | collective-permute-start | bytes 1363976 | tf_op jit(solution)/shard_map/ppermute | solution.py:313
  161.0 14.2 %copy-start.3 = (bf16[576,896]{1,0:T(8,128)(2,1)}, bf16[576,896]{1,0:T(8,128)(2,1)S(1)}, u32[]{:S(2)}) copy-start(bf16[576,896]{1,0:T(8,128)(2,1)S(1)} %dynamic-slice_bitcast_fusion.3) | copy-start | bytes 3096580
  175.4 20.7 %collective-permute-start.27 = (bf16[288,384]{1,0:T(8,128)(2,1)S(1)}, bf16[288,384]{1,0:T(8,128)(2,1)S(1)}, u32[]{:S(2)}, u32[]{:S(2)}) collective-permute-start(bf16[288,384]{1,0:T(8,128)(2,1)S(1)} %fusion.73.refs_0_), channel_id=1, source_target_pairs={{0,64},{8,72},{16,80},{24,88},{32,96},{40,104},{48,112},{56,120},{... | collective-permute-start | bytes 663560 | tf_op jit(solution)/shard_map/ppermute | solution.py:318
  175.5 20.6 %collective-permute-start.28 = (bf16[288,384]{1,0:T(8,128)(2,1)S(1)}, bf16[288,384]{1,0:T(8,128)(2,1)S(1)}, u32[]{:S(2)}, u32[]{:S(2)}) collective-permute-start(bf16[288,384]{1,0:T(8,128)(2,1)S(1)} %fusion.73.refs_0_), channel_id=1, source_target_pairs={{0,128},{8,136},{16,144},{24,152},{32,160},{40,168},{48,176},{56,1... | collective-permute-start | bytes 663560 | tf_op jit(solution)/shard_map/ppermute | solution.py:318
  177.6 22.2 %collective-permute-start.29 = (bf16[288,384]{1,0:T(8,128)(2,1)S(1)}, bf16[288,384]{1,0:T(8,128)(2,1)S(1)}, u32[]{:S(2)}, u32[]{:S(2)}) collective-permute-start(bf16[288,384]{1,0:T(8,128)(2,1)S(1)} %fusion.73.refs_0_), channel_id=1, source_target_pairs={{0,192},{8,200},{16,208},{24,216},{32,224},{40,232},{48,240},{56,2... | collective-permute-start | bytes 663560 | tf_op jit(solution)/shard_map/ppermute | solution.py:318
  204.5 12.5 %copy-start.4 = (bf16[576,896]{1,0:T(8,128)(2,1)S(1)}, bf16[576,896]{1,0:T(8,128)(2,1)}, u32[]{:S(2)}) copy-start(bf16[576,896]{1,0:T(8,128)(2,1)} %copy-done.3) | copy-start | bytes 3096580
  204.5 28.8 %all-to-all-start.7 = ((bf16[8,64,896]{2,1,0:T(8,128)(2,1)}), bf16[8,64,896]{2,1,0:T(8,128)(2,1)}, u32[]{:S(2)}, u32[]{:S(2)}) async-start(bf16[8,64,896]{2,1,0:T(8,128)(2,1)} %down_rows.7), calls=%async_computation.7 | async-start | bytes 1835008 | tf_op jit(solution)/shard_map/all_to_all | solution.py:321
  208.9 10.5 %copy-start.15 = (pred[4,24]{1,0:T(4,128)(4,1)S(1)}, pred[4,24]{1,0:T(4,128)(4,1)}, u32[]{:S(2)}) copy-start(pred[4,24]{1,0:T(4,128)(4,1)} %get-tuple-element.477) | copy-start | bytes 292
  220.0 18.5 %copy-start.7 = (bf16[24,896]{1,0:T(8,128)(2,1)S(1)}, bf16[24,896]{1,0:T(8,128)(2,1)}, u32[]{:S(2)}) copy-start(bf16[24,896]{1,0:T(8,128)(2,1)} %copy-done.6) | copy-start | bytes 129028
  220.0 18.5 %copy-start.9 = (bf16[24,896]{1,0:T(8,128)(2,1)S(1)}, bf16[24,896]{1,0:T(8,128)(2,1)}, u32[]{:S(2)}) copy-start(bf16[24,896]{1,0:T(8,128)(2,1)} %copy-done.8) | copy-start | bytes 129028
  234.9 4.3 %collective-permute-start.30 = (bf16[24,896]{1,0:T(8,128)(2,1)S(1)}, bf16[24,896]{1,0:T(8,128)(2,1)S(1)}, u32[]{:S(2)}, u32[]{:S(2)}) collective-permute-start(bf16[24,896]{1,0:T(8,128)(2,1)S(1)} %get-tuple-element.522), channel_id=1, source_target_pairs={{0,192},{8,200},{16,208},{24,216},{32,224},{40,232},{48,240},{56,2... | collective-permute-start | bytes 129032 | tf_op jit(solution)/shard_map/ppermute | solution.py:338
  237.3 5.5 %collective-permute-start.31 = (bf16[24,896]{1,0:T(8,128)(2,1)S(1)}, bf16[24,896]{1,0:T(8,128)(2,1)S(1)}, u32[]{:S(2)}, u32[]{:S(2)}) collective-permute-start(bf16[24,896]{1,0:T(8,128)(2,1)S(1)} %get-tuple-element.521), channel_id=1, source_target_pairs={{0,128},{8,136},{16,144},{24,152},{32,160},{40,168},{48,176},{56,1... | collective-permute-start | bytes 129032 | tf_op jit(solution)/shard_map/ppermute | solution.py:338
  238.5 5.2 %collective-permute-start.32 = (bf16[24,896]{1,0:T(8,128)(2,1)S(1)}, bf16[24,896]{1,0:T(8,128)(2,1)S(1)}, u32[]{:S(2)}, u32[]{:S(2)}) collective-permute-start(bf16[24,896]{1,0:T(8,128)(2,1)S(1)} %get-tuple-element.520), channel_id=1, source_target_pairs={{0,64},{8,72},{16,80},{24,88},{32,96},{40,104},{48,112},{56,120},{... | collective-permute-start | bytes 129032 | tf_op jit(solution)/shard_map/ppermute | solution.py:338
  243.9 0.7 copy-start.2
Sparse Core Ops, SparseCore 0:
  9.1 44.2 all-gather.4
  55.2 23.2 all-gather.6
  80.4 34.3 all-gather.8
  132.6 25.5 all-gather.10

commit v4 on v3

--- a/solution.py
+++ b/solution.py
@@ -71,9 +71,11 @@
 
     @pl.when(step == pl.num_programs(0) - 1)
     def _():
-        for head in range(heads):
-            rows = [part[pl.ds(head, slots, stride=heads), :] for part in scratch]
-            out[head] = jnp.concatenate(rows, axis=1).astype(BF16)
+        @pl.loop(0, heads, step=8)
+        def _(first):
+            for i in range(8):
+                rows = [part[pl.ds(first + i, slots, stride=heads), :] for part in scratch]
+                out[first + i] = jnp.concatenate(rows, axis=1).astype(BF16)
 
 
 def attend(queries, latent_cache, lengths, latent_width, value_width):
@@ -111,12 +113,16 @@
     slots = local.shape[1]
     turn = lax.broadcasted_iota(jnp.int32, (rows, slots), 0)
     pick = (turn == local[...]).astype(F32).astype(BF16)
-    for head in range(heads):
-        latent = jnp.concatenate([ref[head].astype(F32) for ref in latents], axis=0)
-        values = dot(latent.astype(BF16), value_up[head]).astype(BF16)
-        each = heads // blocks
-        columns = slice(head % each * value_width, (head % each + 1) * value_width)
-        out[head // each, :, columns] = dot(pick, values).astype(BF16)
+    each = heads // blocks
+
+    @pl.loop(0, blocks)
+    def _(block):
+        for i in range(each):
+            head = block * each + i
+            latent = jnp.concatenate([ref[head].astype(F32) for ref in latents], axis=0)
+            values = dot(latent.astype(BF16), value_up[head]).astype(BF16)
+            columns = slice(i * value_width, (i + 1) * value_width)
+            out[block, :, columns] = dot(pick, values).astype(BF16)
 
 
 def packed_values(latents, value_up, local, blocks):
@@ -148,7 +154,9 @@
     nz, rows, _ = out.shape
     at = lax.broadcasted_iota(jnp.int32, (rows, total.shape[0]), 1)
     turn = lax.broadcasted_iota(jnp.int32, (rows, total.shape[0]), 0)
-    for z in range(nz):
+
+    @pl.loop(0, nz)
+    def _(z):
         pick = (at == turn + target[z]).astype(F32).astype(BF16)
         out[z] = dot(pick, total).astype(BF16)
 
@@ -397,15 +405,15 @@
     member = lax.axis_index("group")
     pack, passes = packing(counts, slots)
 
-    parts, got = exchange_parts([out_proj], [residual], member, block)
+    parts, got = exchange_parts([out_proj, gate_up.T, down_proj], [residual], member, block)
     latent = attend(queries, latent_cache, lengths, latent_width, value_width)
     got = lax.optimization_barrier((got, latent))[0]
     value_up = lax.all_gather(
         value_up, "rank", axis=0, tiled=True, axis_index_groups=groups_z(ranks)
     )
-    (projs,) = gather_parts(parts, got)
+    projs, *feeds = gather_parts(parts, got)
     my_proj = take_cols(out_proj, my_x, block)
-    res = [take_cols(residual, my_x, block)] + [g[parts[0] :] for g in got]
+    res = [take_cols(residual, my_x, block)] + [g[sum(parts) :] for g in got]
     res = jnp.concatenate(res, axis=0)
 
     each = latent.shape[0] // NX
@@ -419,9 +427,6 @@
     ]
     sent = local_values(0, latents, value_up, pack)
 
-    member = lax.optimization_barrier((member, sent))[0]
-    parts, got = exchange_parts([gate_up.T, down_proj], [], member, block)
-    feeds = gather_parts(parts, got)
     my_join = jnp.pad(take_cols(gate_up.T, my_x, block), ((0, EXTRA), (0, 0)))
     my_down = take_cols(down_proj, my_x, block)
 

time: 256 us -> 247 us (0.965); the launches traced: 251 us -> 246 us
  starting transfers between devices: 62.2 us -> 50.2 us
  waiting for transfers between devices: 103 us -> 109 us
    ppermute x3, starting transfers between devices: 19.2 us -> 3.42 us  [finish(): lax.ppermute(hidden, 'rank', perm)]
    all_gather x1, waiting for transfers between devices: 7.85 us -> 0.01 us  [per_device(): lax.all_gather(value_up, 'rank', axis=0, tiled=True, axis_index_groups=gr...]
    ppermute x3, waiting for transfers between devices: 7.13 us -> 13.2 us  [per_device(): lax.ppermute(heads_of(lax.rem(my_x + k, NX)), 'rank', shift_x(ranks, k))]
    ppermute x6 -> x3, starting transfers between devices: 11.2 us -> 5.29 us  [exchange_parts(): lax.ppermute(jnp.concatenate(pieces, axis=0), 'rank', shift_x(ranks, k))]
    ppermute x3, waiting for transfers between devices: 3.65 us -> 9.09 us  [finish(): lax.ppermute(hidden, 'rank', perm)]
    ppermute x6 -> x3, waiting for transfers between devices: 10.9 us -> 5.85 us  [exchange_parts(): lax.ppermute(jnp.concatenate(pieces, axis=0), 'rank', shift_x(ranks, k))]
    ppermute x3, starting transfers between devices: 2.21 us -> 7.06 us  [finish(): lax.ppermute(share(join), 'rank', perm)]
    ppermute x3, waiting for transfers between devices: 13.3 us -> 17.1 us  [finish(): lax.ppermute(share(join), 'rank', perm)]
  transfers between devices with their start and end apart: 29 -> 26, of which waited for: 19 -> 15; matrix products, arithmetic and copies ran while one was open for 17% -> 17% of each run, Pallas kernels for 5% -> 6%
where the time goes in v4:
time: 247 us; the launch traced here: 246 us
  waiting for transfers between devices  109 us (44%)
  starting transfers between devices  50.2 us (20%)
  between operations  22.4 us (9%)
  Pallas kernels  20.2 us (8%)
  local copies, waits for them, and re-layouts  17.1 us (7%)
  matrix products  14.7 us (6%)
  other arithmetic  11.8 us (5%)
    all_to_all x1, waiting for transfers between devices, finish(): lax.all_to_all(part.reshape(nz, rows_z, block), 'rank', split_axis=0, con...  18.1 us
    ppermute x3, waiting for transfers between devices, finish(): lax.ppermute(share(join), 'rank', perm)  17.1 us
    all_to_all x1, waiting for transfers between devices, finish(): lax.all_to_all(jnp.broadcast_to(mixed[None], (nz, rows_z, block)), 'rank'...  16.7 us
    all_to_all x1, waiting for transfers between devices, finish(): lax.all_to_all(sent, 'rank', split_axis=0, concat_axis=0, tiled=True, axi...  13.8 us
    ppermute x3, waiting for transfers between devices, per_device(): lax.ppermute(heads_of(lax.rem(my_x + k, NX)), 'rank', shift_x(ranks, k))  13.2 us
    ppermute x3, waiting for transfers between devices, finish(): lax.ppermute(hidden, 'rank', perm)  9.09 us
    all_to_all x1, starting transfers between devices, project(): lax.all_to_all(sent, 'rank', split_axis=0, concat_axis=0, tiled=True, axi...  8.58 us
    pallas_call x1, Pallas kernels, attend(): pl.pallas_call(functools.partial(attend_kernel, scale, step_slots), out_s...  8.3 us
  transfers between devices with their start and end apart: 26, of which 15 were waited for; matrix products, arithmetic and copies ran while one was open for 17% of the time, Pallas kernels for 6%

profile of v4, /device:TPU:24, one launch (start us, length us, event | category | flops | bytes accessed | tf_op | source)
XLA Modules:
  0.0 245.8 jit_solution(9593787407127664209)
XLA Ops:
  9.2 1.0 dynamic-slice_select_fusion
  10.2 1.2 select_bitcast_fusion
  11.4 3.1 %collective-permute-start.13 = (bf16[200,896]{1,0:T(8,128)(2,1)S(1)}, bf16[200,896]{1,0:T(8,128)(2,1)S(1)}, u32[]{:S(2)}, u32[]{:S(2)}) collective-permute-start(bf16[200,896]{1,0:T(8,128)(2,1)S(1)} %pad_maximum_fusion.2), channel_id=1, source_target_pairs={{0,128},{8,136},{16,144},{24,152},{32,160},{40,168},{48,176},{56,1... | collective-permute-start | bytes 1075208 | tf_op jit(solution)/shard_map/ppermute | solution.py:216
  14.6 1.2 collective-permute-start.14
  15.8 1.0 collective-permute-start.12
  16.8 8.3 %attend.1 = bf16[64,24,512]{2,1,0:T(8,128)(2,1)} custom-call(s32[24]{0:T(128)} %lengths.1, bf16[24,64,576]{2,1,0:T(8,128)(2,1)} %queries.1, bf16[24,576,128]{2,1,0:T(8,128)(2,1)} %bitcast.376), custom_call_target="tpu_custom_call" | custom-call | flops 427819008 | bytes 10027008 | tf_op jit(solution)/shard_map/attend/pallas_call | solution.py:87
  25.1 5.8 %collective-permute-done.14 = bf16[200,896]{1,0:T(8,128)(2,1)S(1)} collective-permute-done((bf16[200,896]{1,0:T(8,128)(2,1)S(1)}, bf16[200,896]{1,0:T(8,128)(2,1)S(1)}, u32[]{:S(2)}, u32[]{:S(2)}) %collective-permute-start.14) | collective-permute-done | bytes 358432 | tf_op jit(solution)/shard_map/ppermute | solution.py:216
  34.2 1.4 collective-permute-start.15
  35.6 2.7 %collective-permute-start.16 = (bf16[16,24,512]{2,1,0:T(8,128)(2,1)S(1)}, bf16[16,24,512]{2,1,0:T(8,128)(2,1)}, u32[]{:S(2)}, u32[]{:S(2)}) collective-permute-start(bf16[16,24,512]{2,1,0:T(8,128)(2,1)S(1)} %get-tuple-element.509), channel_id=1, source_target_pairs={{0,128},{8,136},{16,144},{24,152},{32,160},{40,168},{48,176},{56,1... | collective-permute-start | bytes 1179656 | tf_op jit(solution)/shard_map/ppermute | solution.py:425
  38.3 1.4 collective-permute-start.17
  42.7 3.7 %collective-permute-done.15.refs_1_ = bf16[16,24,512]{2,1,0:T(8,128)(2,1)} collective-permute-done((bf16[16,24,512]{2,1,0:T(8,128)(2,1)S(1)}, bf16[16,24,512]{2,1,0:T(8,128)(2,1)}, u32[]{:S(2)}, u32[]{:S(2)}) %collective-permute-start.15) | collective-permute-done | bytes 393248 | tf_op jit(solution)/shard_map/ppermute | solution.py:425
  46.4 9.5 %collective-permute-done.16.refs_2_ = bf16[16,24,512]{2,1,0:T(8,128)(2,1)} collective-permute-done((bf16[16,24,512]{2,1,0:T(8,128)(2,1)S(1)}, bf16[16,24,512]{2,1,0:T(8,128)(2,1)}, u32[]{:S(2)}, u32[]{:S(2)}) %collective-permute-start.16) | collective-permute-done | bytes 393248 | tf_op jit(solution)/shard_map/ppermute | solution.py:425
  55.9 6.4 %packed_values.7 = bf16[8,64,256]{2,1,0:T(8,128)(2,1)} custom-call(s32[1,96]{1,0:T(1,128)S(1)} %sub.237.local, bf16[16,24,512]{2,1,0:T(8,128)(2,1)} %get-tuple-element.734.refs_0_, bf16[16,24,512]{2,1,0:T(8,128)(2,1)} %collective-permute-done.15.refs_1_, bf16[16,24,512]{2,1,0:T(8,128)(2,1)} %collective-permute-done.16.refs_2_, ...), custom_call_target="tpu_custom_call" | custom-call | flops 226492416 | bytes 3670016 | tf_op jit(solution)/shard_map/packed_values/pallas_call | solution.py:133
  62.3 8.6 %all-to-all-start.4 = ((bf16[8,64,256]{2,1,0:T(8,128)(2,1)}), bf16[8,64,256]{2,1,0:T(8,128)(2,1)S(1)}, u32[]{:S(2)}, u32[]{:S(2)}) async-start(bf16[8,64,256]{2,1,0:T(8,128)(2,1)} %packed_values.7), calls=%async_computation.4 | async-start | bytes 524288 | tf_op jit(solution)/shard_map/all_to_all | solution.py:260
  72.2 1.9 constant_dynamic-slice_fusion.6
  75.7 6.5 %all-to-all-done.4 = bf16[8,64,256]{2,1,0:T(8,128)(2,1)S(1)} async-done(((bf16[8,64,256]{2,1,0:T(8,128)(2,1)}), bf16[8,64,256]{2,1,0:T(8,128)(2,1)S(1)}, u32[]{:S(2)}, u32[]{:S(2)}) %all-to-all-start.4) | async-done | bytes 262176 | tf_op jit(solution)/shard_map/all_to_all | solution.py:260
  82.5 2.4 collective-permute-start.19
  84.9 1.6 collective-permute-start.20
  86.9 1.4 fusion.106
  88.7 2.8 %collective-permute-done.19 = bf16[384,256]{1,0:T(8,128)(2,1)} collective-permute-done((bf16[384,256]{1,0:T(8,128)(2,1)S(1)}, bf16[384,256]{1,0:T(8,128)(2,1)}, u32[]{:S(2)}, u32[]{:S(2)}) %collective-permute-start.19) | collective-permute-done | bytes 196640 | tf_op jit(solution)/shard_map/ppermute | solution.py:269
  91.5 1.5 fusion.71
  93.9 1.3 fusion.70
  95.2 2.2 fusion.62
  97.4 3.5 %all-to-all-start.5 = ((bf16[8,48,896]{2,1,0:T(8,128)(2,1)}), bf16[8,48,896]{2,1,0:T(8,128)(2,1)S(1)}, u32[]{:S(2)}, u32[]{:S(2)}) async-start(bf16[8,48,896]{2,1,0:T(8,128)(2,1)} %bitcast.66), calls=%async_computation.5 | async-start | bytes 1376256 | tf_op jit(solution)/shard_map/all_to_all | solution.py:291
  101.0 0.9 slice_bitcast_fusion.21
  101.9 18.1 %all-to-all-done.5 = bf16[8,48,896]{2,1,0:T(8,128)(2,1)S(1)} async-done(((bf16[8,48,896]{2,1,0:T(8,128)(2,1)}), bf16[8,48,896]{2,1,0:T(8,128)(2,1)S(1)}, u32[]{:S(2)}, u32[]{:S(2)}) %all-to-all-start.5) | async-done | bytes 688160 | tf_op jit(solution)/shard_map/all_to_all | solution.py:291
  121.0 3.5 %all-to-all-start.6 = ((bf16[8,48,896]{2,1,0:T(8,128)(2,1)}), bf16[8,48,896]{2,1,0:T(8,128)(2,1)S(1)}, u32[]{:S(2)}, u32[]{:S(2)}) async-start(bf16[8,48,896]{2,1,0:T(8,128)(2,1)} %broadcast_in_dim.212), calls=%async_computation.6 | async-start | bytes 1376256 | tf_op jit(solution)/shard_map/all_to_all | solution.py:300
  126.5 16.7 %all-to-all-done.6 = bf16[8,48,896]{2,1,0:T(8,128)(2,1)S(1)} async-done(((bf16[8,48,896]{2,1,0:T(8,128)(2,1)}), bf16[8,48,896]{2,1,0:T(8,128)(2,1)S(1)}, u32[]{:S(2)}, u32[]{:S(2)}) %all-to-all-start.6) | async-done | bytes 688160 | tf_op jit(solution)/shard_map/all_to_all | solution.py:300
  143.6 2.1 fusion.64
  145.7 6.0 %collective-permute-start.21 = (bf16[592,384]{1,0:T(8,128)(2,1)S(1)}, bf16[592,384]{1,0:T(8,128)(2,1)S(1)}, u32[]{:S(2)}, u32[]{:S(2)}) collective-permute-start(bf16[592,384]{1,0:T(8,128)(2,1)S(1)} %fusion.64), channel_id=1, source_target_pairs={{0,192},{8,200},{16,208},{24,216},{32,224},{40,232},{48,240},{56,2... | collective-permute-start | bytes 1363976 | tf_op jit(solution)/shard_map/ppermute | solution.py:321
  151.7 2.1 fusion.65
  154.5 2.1 fusion.66
  156.8 1.9 constant_dynamic-slice_fusion.5.refs_4_
  158.7 1.3 dynamic-slice_bitcast_fusion.3
  160.0 11.2 %collective-permute-done.21 = bf16[592,384]{1,0:T(8,128)(2,1)S(1)} collective-permute-done((bf16[592,384]{1,0:T(8,128)(2,1)S(1)}, bf16[592,384]{1,0:T(8,128)(2,1)S(1)}, u32[]{:S(2)}, u32[]{:S(2)}) %collective-permute-start.21) | collective-permute-done | bytes 454688 | tf_op jit(solution)/shard_map/ppermute | solution.py:321
  171.3 5.9 %collective-permute-done.23 = bf16[592,384]{1,0:T(8,128)(2,1)S(1)} collective-permute-done((bf16[592,384]{1,0:T(8,128)(2,1)S(1)}, bf16[592,384]{1,0:T(8,128)(2,1)S(1)}, u32[]{:S(2)}, u32[]{:S(2)}) %collective-permute-start.23) | collective-permute-done | bytes 454688 | tf_op jit(solution)/shard_map/ppermute | solution.py:321
  177.1 0.9 add_add_fusion.1
  178.4 2.1 collective-permute-start.25
  180.4 1.3 collective-permute-start.26
  181.7 1.5 slice_bitcast_fusion.9
  183.2 8.5 %collective-permute-done.24.refs_1_ = bf16[288,384]{1,0:T(8,128)(2,1)S(1)} collective-permute-done((bf16[288,384]{1,0:T(8,128)(2,1)S(1)}, bf16[288,384]{1,0:T(8,128)(2,1)S(1)}, u32[]{:S(2)}, u32[]{:S(2)}) %collective-permute-start.24) | collective-permute-done | bytes 221216 | tf_op jit(solution)/shard_map/ppermute | solution.py:326
  192.3 5.5 %down_rows.7 = bf16[8,64,896]{2,1,0:T(8,128)(2,1)} custom-call(s32[8]{0:T(128)S(1)} %fusion.94.target, bf16[288,384]{1,0:T(8,128)(2,1)S(1)} %fusion.73.refs_0_, bf16[288,384]{1,0:T(8,128)(2,1)S(1)} %collective-permute-done.24.refs_1_, bf16[288,384]{1,0:T(8,128)(2,1)S(1)} %collective-permute-done.25.refs_2_, ...), custom_call_target="tpu_custom_call" | custom-call | flops 1145044992 | bytes 3866624 | tf_op jit(solution)/shard_map/down_rows/pallas_call | solution.py:170
  197.8 4.4 %all-to-all-start.7 = ((bf16[8,64,896]{2,1,0:T(8,128)(2,1)}), bf16[8,64,896]{2,1,0:T(8,128)(2,1)}, u32[]{:S(2)}, u32[]{:S(2)}) async-start(bf16[8,64,896]{2,1,0:T(8,128)(2,1)} %down_rows.7), calls=%async_computation.7 | async-start | bytes 1835008 | tf_op jit(solution)/shard_map/all_to_all | solution.py:329
  210.3 1.1 pad.4
  213.6 13.8 %all-to-all-done.7 = bf16[8,64,896]{2,1,0:T(8,128)(2,1)} async-done(((bf16[8,64,896]{2,1,0:T(8,128)(2,1)}), bf16[8,64,896]{2,1,0:T(8,128)(2,1)}, u32[]{:S(2)}, u32[]{:S(2)}) %all-to-all-start.7) | async-done | bytes 917536 | tf_op jit(solution)/shard_map/all_to_all | solution.py:329
  227.4 1.3 reduce_sum.108
  229.0 3.2 %collective-permute-start.27 = (bf16[24,896]{1,0:T(8,128)(2,1)S(1)}, bf16[24,896]{1,0:T(8,128)(2,1)S(1)}, u32[]{:S(2)}, u32[]{:S(2)}) collective-permute-start(bf16[24,896]{1,0:T(8,128)(2,1)S(1)} %get-tuple-element.520), channel_id=1, source_target_pairs={{0,192},{8,200},{16,208},{24,216},{32,224},{40,232},{48,240},{56,2... | collective-permute-start | bytes 129032 | tf_op jit(solution)/shard_map/ppermute | solution.py:346
  233.9 3.9 %collective-permute-done.28 = bf16[24,896]{1,0:T(8,128)(2,1)S(1)} collective-permute-done((bf16[24,896]{1,0:T(8,128)(2,1)S(1)}, bf16[24,896]{1,0:T(8,128)(2,1)S(1)}, u32[]{:S(2)}, u32[]{:S(2)}) %collective-permute-start.28) | collective-permute-done | bytes 43040 | tf_op jit(solution)/shard_map/ppermute | solution.py:346
  (128 shorter events, 24.0 us)
Async XLA Ops:
  6.5 49.3 %all-gather.5.cloned.1.call-start = ((), (), s32[]{:S(2)}) async-start(), calls=%async_computation.8 | async-start | bytes 2359296 | tf_op jit(solution)/shard_map/all_gather | solution.py:411
  7.3 81.4 %all-gather.7.cloned.1.call-start = ((), (), s32[]{:S(2)}) async-start(), calls=%async_computation.9 | async-start | bytes 1548288 | tf_op jit(solution)/shard_map/all_gather | solution.py:225
  11.4 13.7 %collective-permute-start.13 = (bf16[200,896]{1,0:T(8,128)(2,1)S(1)}, bf16[200,896]{1,0:T(8,128)(2,1)S(1)}, u32[]{:S(2)}, u32[]{:S(2)}) collective-permute-start(bf16[200,896]{1,0:T(8,128)(2,1)S(1)} %pad_maximum_fusion.2), channel_id=1, source_target_pairs={{0,128},{8,136},{16,144},{24,152},{32,160},{40,168},{48,176},{56,1... | collective-permute-start | bytes 1075208 | tf_op jit(solution)/shard_map/ppermute | solution.py:216
  14.6 16.4 %collective-permute-start.14 = (bf16[200,896]{1,0:T(8,128)(2,1)S(1)}, bf16[200,896]{1,0:T(8,128)(2,1)S(1)}, u32[]{:S(2)}, u32[]{:S(2)}) collective-permute-start(bf16[200,896]{1,0:T(8,128)(2,1)S(1)} %pad_maximum_fusion.3), channel_id=1, source_target_pairs={{0,192},{8,200},{16,208},{24,216},{32,224},{40,232},{48,240},{56,2... | collective-permute-start | bytes 1075208 | tf_op jit(solution)/shard_map/ppermute | solution.py:216
  15.8 15.1 %collective-permute-start.12 = (bf16[200,896]{1,0:T(8,128)(2,1)S(1)}, bf16[200,896]{1,0:T(8,128)(2,1)S(1)}, u32[]{:S(2)}, u32[]{:S(2)}) collective-permute-start(bf16[200,896]{1,0:T(8,128)(2,1)S(1)} %pad_maximum_fusion.1), channel_id=1, source_target_pairs={{0,64},{8,72},{16,80},{24,88},{32,96},{40,104},{48,112},{56,120},{... | collective-permute-start | bytes 1075208 | tf_op jit(solution)/shard_map/ppermute | solution.py:216
  25.1 7.7 %copy-start.7 = (bf16[200,896]{1,0:T(8,128)(2,1)}, bf16[200,896]{1,0:T(8,128)(2,1)S(1)}, u32[]{:S(2)}) copy-start(bf16[200,896]{1,0:T(8,128)(2,1)S(1)} %collective-permute-done.13) | copy-start | bytes 1075204
  30.9 1.8 copy-start.8
  31.7 1.6 copy-start.2
  31.8 111.8 %all-gather.9.cloned.1.call-start = ((), (), s32[]{:S(2)}) async-start(), calls=%async_computation.10 | async-start | bytes 4644864 | tf_op jit(solution)/shard_map/all_gather | solution.py:225
  33.3 6.3 %copy-start.16 = (s32[32]{0:T(128)S(1)}, s32[32]{0:T(128)}, u32[]{:S(2)}) copy-start(s32[32]{0:T(128)} %param.16) | copy-start | bytes 388
  34.2 12.1 %collective-permute-start.15 = (bf16[16,24,512]{2,1,0:T(8,128)(2,1)S(1)}, bf16[16,24,512]{2,1,0:T(8,128)(2,1)}, u32[]{:S(2)}, u32[]{:S(2)}) collective-permute-start(bf16[16,24,512]{2,1,0:T(8,128)(2,1)S(1)} %get-tuple-element.510), channel_id=1, source_target_pairs={{0,64},{8,72},{16,80},{24,88},{32,96},{40,104},{48,112},{56,120},{... | collective-permute-start | bytes 1179656 | tf_op jit(solution)/shard_map/ppermute | solution.py:425
  35.6 20.3 %collective-permute-start.16 = (bf16[16,24,512]{2,1,0:T(8,128)(2,1)S(1)}, bf16[16,24,512]{2,1,0:T(8,128)(2,1)}, u32[]{:S(2)}, u32[]{:S(2)}) collective-permute-start(bf16[16,24,512]{2,1,0:T(8,128)(2,1)S(1)} %get-tuple-element.509), channel_id=1, source_target_pairs={{0,128},{8,136},{16,144},{24,152},{32,160},{40,168},{48,176},{56,1... | collective-permute-start | bytes 1179656 | tf_op jit(solution)/shard_map/ppermute | solution.py:425
  38.3 17.5 %collective-permute-start.17 = (bf16[16,24,512]{2,1,0:T(8,128)(2,1)S(1)}, bf16[16,24,512]{2,1,0:T(8,128)(2,1)}, u32[]{:S(2)}, u32[]{:S(2)}) collective-permute-start(bf16[16,24,512]{2,1,0:T(8,128)(2,1)S(1)} %get-tuple-element.508), channel_id=1, source_target_pairs={{0,192},{8,200},{16,208},{24,216},{32,224},{40,232},{48,240},{56,2... | collective-permute-start | bytes 1179656 | tf_op jit(solution)/shard_map/ppermute | solution.py:425
  41.9 29.1 %copy-start.11 = (s32[4,8,24]{2,0,1:T(4,128)}, s32[4,8,24]{2,0,1:T(4,128)S(1)}, u32[]{:S(2)}) copy-start(s32[4,8,24]{2,0,1:T(4,128)S(1)} %get-tuple-element.728) | copy-start | bytes 9220
  42.5 19.8 %copy-start.9 = (s32[4,24]{1,0:T(4,128)}, s32[4,24]{1,0:T(4,128)S(1)}, u32[]{:S(2)}) copy-start(s32[4,24]{1,0:T(4,128)S(1)} %gather_fusion.2) | copy-start | bytes 1156
  42.6 19.6 %copy-start.12 = (s32[2,8]{1,0:T(2,128)}, s32[2,8]{1,0:T(2,128)S(1)}, u32[]{:S(2)}) copy-start(s32[2,8]{1,0:T(2,128)S(1)} %get-tuple-element.730) | copy-start | bytes 196
  42.6 19.6 %copy-start.14 = (s32[2,8]{1,0:T(2,128)}, s32[2,8]{1,0:T(2,128)S(1)}, u32[]{:S(2)}) copy-start(s32[2,8]{1,0:T(2,128)S(1)} %get-tuple-element.732) | copy-start | bytes 196
  62.3 19.9 %all-to-all-start.4 = ((bf16[8,64,256]{2,1,0:T(8,128)(2,1)}), bf16[8,64,256]{2,1,0:T(8,128)(2,1)S(1)}, u32[]{:S(2)}, u32[]{:S(2)}) async-start(bf16[8,64,256]{2,1,0:T(8,128)(2,1)} %packed_values.7), calls=%async_computation.4 | async-start | bytes 524288 | tf_op jit(solution)/shard_map/all_to_all | solution.py:260
  82.5 9.0 %collective-permute-start.19 = (bf16[384,256]{1,0:T(8,128)(2,1)S(1)}, bf16[384,256]{1,0:T(8,128)(2,1)}, u32[]{:S(2)}, u32[]{:S(2)}) collective-permute-start(bf16[384,256]{1,0:T(8,128)(2,1)S(1)} %convolution_convert_fusion.1), channel_id=1, source_target_pairs={{0,128},{8,136},{16,144},{24,152},{32,160},{40,168},{48,176},{56,1... | collective-permute-start | bytes 589832 | tf_op jit(solution)/shard_map/ppermute | solution.py:269
  84.9 9.0 %collective-permute-start.20 = (bf16[384,256]{1,0:T(8,128)(2,1)S(1)}, bf16[384,256]{1,0:T(8,128)(2,1)}, u32[]{:S(2)}, u32[]{:S(2)}) collective-permute-start(bf16[384,256]{1,0:T(8,128)(2,1)S(1)} %convolution_convert_fusion.1), channel_id=1, source_target_pairs={{0,192},{8,200},{16,208},{24,216},{32,224},{40,232},{48,240},{56,2... | collective-permute-start | bytes 589832 | tf_op jit(solution)/shard_map/ppermute | solution.py:269
  86.5 8.7 %collective-permute-start.18 = (bf16[384,256]{1,0:T(8,128)(2,1)S(1)}, bf16[384,256]{1,0:T(8,128)(2,1)}, u32[]{:S(2)}, u32[]{:S(2)}) collective-permute-start(bf16[384,256]{1,0:T(8,128)(2,1)S(1)} %convolution_convert_fusion.1), channel_id=1, source_target_pairs={{0,64},{8,72},{16,80},{24,88},{32,96},{40,104},{48,112},{56,120},{... | collective-permute-start | bytes 589832 | tf_op jit(solution)/shard_map/ppermute | solution.py:269
  88.7 5.2 %copy-start = (bf16[3,256,896]{2,1,0:T(8,128)(2,1)S(1)}, bf16[3,256,896]{2,1,0:T(8,128)(2,1)}, u32[]{:S(2)}) copy-start(bf16[3,256,896]{2,1,0:T(8,128)(2,1)} %all-gather.7.cloned.1.call-done) | copy-start | bytes 4128772
  97.4 22.6 %all-to-all-start.5 = ((bf16[8,48,896]{2,1,0:T(8,128)(2,1)}), bf16[8,48,896]{2,1,0:T(8,128)(2,1)S(1)}, u32[]{:S(2)}, u32[]{:S(2)}) async-start(bf16[8,48,896]{2,1,0:T(8,128)(2,1)} %bitcast.66), calls=%async_computation.5 | async-start | bytes 1376256 | tf_op jit(solution)/shard_map/all_to_all | solution.py:291
  121.0 22.2 %all-to-all-start.6 = ((bf16[8,48,896]{2,1,0:T(8,128)(2,1)}), bf16[8,48,896]{2,1,0:T(8,128)(2,1)S(1)}, u32[]{:S(2)}, u32[]{:S(2)}) async-start(bf16[8,48,896]{2,1,0:T(8,128)(2,1)} %broadcast_in_dim.212), calls=%async_computation.6 | async-start | bytes 1376256 | tf_op jit(solution)/shard_map/all_to_all | solution.py:300
  124.6 57.1 %all-gather.11.cloned.1.call-start = ((), (), s32[]{:S(2)}) async-start(), calls=%async_computation.11 | async-start | bytes 2322432 | tf_op jit(solution)/shard_map/all_gather | solution.py:225
  145.7 25.6 %collective-permute-start.21 = (bf16[592,384]{1,0:T(8,128)(2,1)S(1)}, bf16[592,384]{1,0:T(8,128)(2,1)S(1)}, u32[]{:S(2)}, u32[]{:S(2)}) collective-permute-start(bf16[592,384]{1,0:T(8,128)(2,1)S(1)} %fusion.64), channel_id=1, source_target_pairs={{0,192},{8,200},{16,208},{24,216},{32,224},{40,232},{48,240},{56,2... | collective-permute-start | bytes 1363976 | tf_op jit(solution)/shard_map/ppermute | solution.py:321
  153.7 17.6 %collective-permute-start.22 = (bf16[592,384]{1,0:T(8,128)(2,1)S(1)}, bf16[592,384]{1,0:T(8,128)(2,1)S(1)}, u32[]{:S(2)}, u32[]{:S(2)}) collective-permute-start(bf16[592,384]{1,0:T(8,128)(2,1)S(1)} %fusion.65), channel_id=1, source_target_pairs={{0,128},{8,136},{16,144},{24,152},{32,160},{40,168},{48,176},{56,1... | collective-permute-start | bytes 1363976 | tf_op jit(solution)/shard_map/ppermute | solution.py:321
  156.6 20.6 %collective-permute-start.23 = (bf16[592,384]{1,0:T(8,128)(2,1)S(1)}, bf16[592,384]{1,0:T(8,128)(2,1)S(1)}, u32[]{:S(2)}, u32[]{:S(2)}) collective-permute-start(bf16[592,384]{1,0:T(8,128)(2,1)S(1)} %fusion.66), channel_id=1, source_target_pairs={{0,64},{8,72},{16,80},{24,88},{32,96},{40,104},{48,112},{56,120},{... | collective-permute-start | bytes 1363976 | tf_op jit(solution)/shard_map/ppermute | solution.py:321
  160.0 18.0 %copy-start.4 = (bf16[576,896]{1,0:T(8,128)(2,1)}, bf16[576,896]{1,0:T(8,128)(2,1)S(1)}, u32[]{:S(2)}) copy-start(bf16[576,896]{1,0:T(8,128)(2,1)S(1)} %dynamic-slice_bitcast_fusion.3) | copy-start | bytes 3096580
  178.3 13.4 %collective-permute-start.24 = (bf16[288,384]{1,0:T(8,128)(2,1)S(1)}, bf16[288,384]{1,0:T(8,128)(2,1)S(1)}, u32[]{:S(2)}, u32[]{:S(2)}) collective-permute-start(bf16[288,384]{1,0:T(8,128)(2,1)S(1)} %fusion.73.refs_0_), channel_id=1, source_target_pairs={{0,64},{8,72},{16,80},{24,88},{32,96},{40,104},{48,112},{56,120},{... | collective-permute-start | bytes 663560 | tf_op jit(solution)/shard_map/ppermute | solution.py:326
  178.4 13.3 %collective-permute-start.25 = (bf16[288,384]{1,0:T(8,128)(2,1)S(1)}, bf16[288,384]{1,0:T(8,128)(2,1)S(1)}, u32[]{:S(2)}, u32[]{:S(2)}) collective-permute-start(bf16[288,384]{1,0:T(8,128)(2,1)S(1)} %fusion.73.refs_0_), channel_id=1, source_target_pairs={{0,128},{8,136},{16,144},{24,152},{32,160},{40,168},{48,176},{56,1... | collective-permute-start | bytes 663560 | tf_op jit(solution)/shard_map/ppermute | solution.py:326
  180.4 11.9 %collective-permute-start.26 = (bf16[288,384]{1,0:T(8,128)(2,1)S(1)}, bf16[288,384]{1,0:T(8,128)(2,1)S(1)}, u32[]{:S(2)}, u32[]{:S(2)}) collective-permute-start(bf16[288,384]{1,0:T(8,128)(2,1)S(1)} %fusion.73.refs_0_), channel_id=1, source_target_pairs={{0,192},{8,200},{16,208},{24,216},{32,224},{40,232},{48,240},{56,2... | collective-permute-start | bytes 663560 | tf_op jit(solution)/shard_map/ppermute | solution.py:326
  197.8 12.5 %copy-start.5 = (bf16[576,896]{1,0:T(8,128)(2,1)S(1)}, bf16[576,896]{1,0:T(8,128)(2,1)}, u32[]{:S(2)}) copy-start(bf16[576,896]{1,0:T(8,128)(2,1)} %copy-done.4) | copy-start | bytes 3096580
  197.8 29.6 %all-to-all-start.7 = ((bf16[8,64,896]{2,1,0:T(8,128)(2,1)}), bf16[8,64,896]{2,1,0:T(8,128)(2,1)}, u32[]{:S(2)}, u32[]{:S(2)}) async-start(bf16[8,64,896]{2,1,0:T(8,128)(2,1)} %down_rows.7), calls=%async_computation.7 | async-start | bytes 1835008 | tf_op jit(solution)/shard_map/all_to_all | solution.py:329
  202.2 9.9 %copy-start.13 = (s32[2,8]{1,0:T(2,128)S(1)}, s32[2,8]{1,0:T(2,128)}, u32[]{:S(2)}) copy-start(s32[2,8]{1,0:T(2,128)} %copy-done.12) | copy-start | bytes 196
  202.2 10.5 %copy-start.17 = (pred[4,24]{1,0:T(4,128)(4,1)S(1)}, pred[4,24]{1,0:T(4,128)(4,1)}, u32[]{:S(2)}) copy-start(pred[4,24]{1,0:T(4,128)(4,1)} %get-tuple-element.475) | copy-start | bytes 292
  213.6 24.7 %copy-start.10 = (s32[4,24]{1,0:T(4,128)S(1)}, s32[4,24]{1,0:T(4,128)}, u32[]{:S(2)}) copy-start(s32[4,24]{1,0:T(4,128)} %copy-done.9) | copy-start | bytes 1156
  213.6 24.7 %copy-start.15 = (s32[2,8]{1,0:T(2,128)S(1)}, s32[2,8]{1,0:T(2,128)}, u32[]{:S(2)}) copy-start(s32[2,8]{1,0:T(2,128)} %copy-done.14) | copy-start | bytes 196
  229.0 4.9 %collective-permute-start.27 = (bf16[24,896]{1,0:T(8,128)(2,1)S(1)}, bf16[24,896]{1,0:T(8,128)(2,1)S(1)}, u32[]{:S(2)}, u32[]{:S(2)}) collective-permute-start(bf16[24,896]{1,0:T(8,128)(2,1)S(1)} %get-tuple-element.520), channel_id=1, source_target_pairs={{0,192},{8,200},{16,208},{24,216},{32,224},{40,232},{48,240},{56,2... | collective-permute-start | bytes 129032 | tf_op jit(solution)/shard_map/ppermute | solution.py:346
  232.2 5.6 %collective-permute-start.28 = (bf16[24,896]{1,0:T(8,128)(2,1)S(1)}, bf16[24,896]{1,0:T(8,128)(2,1)S(1)}, u32[]{:S(2)}, u32[]{:S(2)}) collective-permute-start(bf16[24,896]{1,0:T(8,128)(2,1)S(1)} %get-tuple-element.519), channel_id=1, source_target_pairs={{0,128},{8,136},{16,144},{24,152},{32,160},{40,168},{48,176},{56,1... | collective-permute-start | bytes 129032 | tf_op jit(solution)/shard_map/ppermute | solution.py:346
  232.5 5.7 %collective-permute-start.29 = (bf16[24,896]{1,0:T(8,128)(2,1)S(1)}, bf16[24,896]{1,0:T(8,128)(2,1)S(1)}, u32[]{:S(2)}, u32[]{:S(2)}) collective-permute-start(bf16[24,896]{1,0:T(8,128)(2,1)S(1)} %get-tuple-element.518), channel_id=1, source_target_pairs={{0,64},{8,72},{16,80},{24,88},{32,96},{40,104},{48,112},{56,120},{... | collective-permute-start | bytes 129032 | tf_op jit(solution)/shard_map/ppermute | solution.py:346
  238.6 0.7 copy-start.3
Sparse Core Ops, SparseCore 0:
  9.1 44.0 all-gather.4
  55.1 23.2 all-gather.6
  80.2 34.3 all-gather.8
  127.0 28.7 all-gather.10

commit v5 on v4

--- a/solution.py
+++ b/solution.py
@@ -145,6 +145,43 @@
     )(local[None], *latents, value_up)
 
 
+def share_kernel(mixed, gain, mine, full, *outs):
+    wide = mixed[...].astype(F32)
+    both = mine.shape[0]
+    squares = wide * wide
+    high = squares.astype(BF16)
+    low = (squares - high.astype(F32)).astype(BF16)
+    ones = jnp.ones((EXTRA, wide.shape[1]), BF16)
+    total = dot_nt(ones, high) + dot_nt(ones, low)
+    top = total.astype(BF16).astype(F32)
+    line = lax.broadcasted_iota(jnp.int32, total.shape, 0)
+    extra = jnp.where(line == 0, top, jnp.where(line == 1, total - top, 0.0)).astype(BF16)
+    scaled = (wide * gain[...]).astype(BF16)
+    for k, out in enumerate(outs):
+        join = mine[...] if k == 0 else full[k - 1, :both]
+        out[:both] = dot_nt(join, scaled).astype(BF16)
+        out[both:] = extra
+
+
+def gate_up_shares(mixed, gain, mine, full):
+    both, block = mine.shape
+    cap = mixed.shape[0]
+    out = jax.ShapeDtypeStruct((both + EXTRA, cap), BF16)
+    return pl.pallas_call(
+        share_kernel,
+        out_shape=[out] * NX,
+        in_specs=[pl.BlockSpec(memory_space=pltpu.VMEM)] * 4,
+        out_specs=[pl.BlockSpec(memory_space=pltpu.VMEM)] * NX,
+        compiler_params=pltpu.CompilerParams(vmem_limit_bytes=40 * 2**20),
+        cost_estimate=pl.CostEstimate(
+            flops=2 * NX * both * block * cap,
+            bytes_accessed=2 * (cap * block + NX * both * (block + cap)),
+            transcendentals=0,
+        ),
+        name="gate_up_shares",
+    )(mixed, gain[None], mine, full)
+
+
 def down_kernel(terms, target, *refs):
     hiddens, downs, out = refs[:terms], refs[terms : 2 * terms], refs[2 * terms]
     total = dot_tn(hiddens[0][...], downs[0][...])
@@ -154,9 +191,7 @@
     nz, rows, _ = out.shape
     at = lax.broadcasted_iota(jnp.int32, (rows, total.shape[0]), 1)
     turn = lax.broadcasted_iota(jnp.int32, (rows, total.shape[0]), 0)
-
-    @pl.loop(0, nz)
-    def _(z):
+    for z in range(nz):
         pick = (at == turn + target[z]).astype(F32).astype(BF16)
         out[z] = dot(pick, total).astype(BF16)
 
@@ -205,8 +240,7 @@
     parts = [part_rows(m.shape[0], members) for m in matrices]
 
     def cut(matrix, rows, x):
-        piece = lax.dynamic_slice(matrix, (member * rows, x * block), (rows, block))
-        return jnp.where(member * rows < matrix.shape[0], piece, jnp.zeros((), BF16))
+        return lax.dynamic_slice(matrix, (member * rows, x * block), (rows, block))
 
     got = []
     for k in range(1, NX):
@@ -226,9 +260,7 @@
 
 
 def weight_blocks(mine, full):
-    height = mine.shape[0]
-    full = jnp.pad(full, ((0, 0), (0, max(0, height - full.shape[1])), (0, 0)))
-    return [mine] + [full[k, :height] for k in range(NX - 1)]
+    return [mine] + [full[k, : mine.shape[0]] for k in range(NX - 1)]
 
 
 def x_order(my_x):
@@ -276,7 +308,7 @@
     return part.astype(BF16)
 
 
-def finish(index, part, joins, downs, gain, pack, width):
+def finish(index, part, my_join, full_join, downs, gain, pack, width):
     place, _, _, bases, passes_first = pack
     ranks, slots = place.shape
     nz = ranks // NX
@@ -306,20 +338,11 @@
         axis_index_groups=groups_z(ranks),
     ).reshape(CAP, block)
 
-    wide = mixed.astype(F32)
-    square = jnp.sum(wide * wide, axis=1)
-    high = lax.reduce_precision(square, 8, 7)
-    both = joins[0].shape[0] - EXTRA
-    line = jnp.arange(both + EXTRA, dtype=jnp.int32)[:, None]
-    extra = jnp.where(line == both, high, jnp.where(line == both + 1, square - high, 0.0))
-    scaled = (wide * gain[None, :]).astype(BF16)
-
-    def share(join):
-        return (dot_nt(join, scaled) + extra).astype(BF16)
-
+    shares = gate_up_shares(mixed, gain, my_join, full_join)
+    both = my_join.shape[0]
     back = [shift_x(ranks, NX - k) for k in range(1, NX)]
-    arrived = [lax.ppermute(share(join), "rank", perm) for join, perm in zip(joins[1:], back)]
-    joined = share(joins[0]).astype(F32) + sum(a.astype(F32) for a in arrived)
+    arrived = [lax.ppermute(share, "rank", perm) for share, perm in zip(shares[1:], back)]
+    joined = shares[0].astype(F32) + sum(a.astype(F32) for a in arrived)
     factor = lax.rsqrt((joined[both] + joined[both + 1]) / width + 1e-06)[None, :]
     gate, up = joined[: both // 2] * factor, joined[both // 2 : both] * factor
     hidden = (jax.nn.silu(gate) * up).astype(BF16)
@@ -407,34 +430,32 @@
 
     parts, got = exchange_parts([out_proj, gate_up.T, down_proj], [residual], member, block)
     latent = attend(queries, latent_cache, lengths, latent_width, value_width)
-    got = lax.optimization_barrier((got, latent))[0]
     value_up = lax.all_gather(
         value_up, "rank", axis=0, tiled=True, axis_index_groups=groups_z(ranks)
     )
+    each = latent.shape[0] // NX
+
+    def heads_of(x):
+        return lax.dynamic_slice_in_dim(latent, x * each, each, 0)
+
+    latents = [heads_of(my_x)] + [
+        lax.ppermute(heads_of(lax.rem(my_x + k, NX)), "rank", shift_x(ranks, k))
+        for k in range(1, NX)
+    ]
+    got = lax.optimization_barrier((got, latents))[0]
     projs, *feeds = gather_parts(parts, got)
     my_proj = take_cols(out_proj, my_x, block)
     res = [take_cols(residual, my_x, block)] + [g[sum(parts) :] for g in got]
     res = jnp.concatenate(res, axis=0)
 
-    each = latent.shape[0] // NX
-
-    def heads_of(x):
-        return lax.dynamic_slice_in_dim(latent, x * each, each, 0)
-
-    latents = [heads_of(my_x)] + [
-        lax.ppermute(heads_of(lax.rem(my_x + k, NX)), "rank", shift_x(ranks, k))
-        for k in range(1, NX)
-    ]
     sent = local_values(0, latents, value_up, pack)
-
-    my_join = jnp.pad(take_cols(gate_up.T, my_x, block), ((0, EXTRA), (0, 0)))
+    my_join = take_cols(gate_up.T, my_x, block)
     my_down = take_cols(down_proj, my_x, block)
 
     def run(index, sent):
         part = project(index, sent, res, weight_blocks(my_proj, projs), pack)
-        joins = weight_blocks(my_join, feeds[0])
         downs = weight_blocks(my_down, feeds[1])
-        return finish(index, part, joins, downs, gain, pack, width)
+        return finish(index, part, my_join, feeds[0], downs, gain, pack, width)
 
     def more(state):
         index, out = state

time: 247 us -> 248 us (level)
  waiting for transfers between devices: 109 us -> 121 us
  matrix products: 14.7 us -> 7.59 us
  other arithmetic: 11.8 us -> 7.26 us
  starting transfers between devices: 50.2 us -> 46.2 us
  Pallas kernels: 20.2 us -> 23.9 us
    ppermute x3, waiting for transfers between devices: 5.85 us -> 23.1 us  [exchange_parts(): lax.ppermute(jnp.concatenate(pieces, axis=0), 'rank', shift_x(ranks, k))]
    ppermute x3, waiting for transfers between devices: 13.2 us -> 0.01 us  [per_device(): lax.ppermute(heads_of(lax.rem(my_x + k, NX)), 'rank', shift_x(ranks, k))]
    dot_general x4 -> x0, matrix products: 7.1 us -> none  [dot_nt(): lax.dot_general(a, b, (((1,), (1,)), ((), ())), preferred_element_type=F32)]
    pallas_call x0 -> x1, Pallas kernels: none -> 5.04 us  [gate_up_shares(): pl.pallas_call(share_kernel, out_shape=[out] * NX, in_specs=[pl.BlockSpec...]
    ppermute x3, waiting for transfers between devices: 17.1 us -> 20.9 us  [finish(): lax.ppermute(share, 'rank', perm)]
    all_to_all x1, waiting for transfers between devices: 6.51 us -> 9.88 us  [project(): lax.all_to_all(sent, 'rank', split_axis=0, concat_axis=0, tiled=True, axi...]
    select_n x3 -> x0, other arithmetic: 3.14 us -> none  [cut(): jnp.where(member * rows < matrix.shape[0], piece, jnp.zeros((), BF16))]
    dynamic_slice x0 -> x3, local copies, waits for them, and re-layouts: none -> 3.06 us  [cut(): return lax.dynamic_slice(matrix, (member * rows, x * block), (rows, block))]
  transfers between devices with their start and end apart: 26 -> 26, of which waited for: 15 -> 13; matrix products, arithmetic and copies ran while one was open for 17% -> 13% of each run, Pallas kernels for 6% -> 8%
where the time goes in v5:
time: 248 us; the launch traced here: 246 us
  waiting for transfers between devices  121 us (49%)
  starting transfers between devices  46.2 us (19%)
  Pallas kernels  23.9 us (10%)
  between operations  22.5 us (9%)
  local copies, waits for them, and re-layouts  17.3 us (7%)
  matrix products  7.59 us (3%)
  other arithmetic  7.26 us (3%)
    ppermute x3, waiting for transfers between devices, exchange_parts(): lax.ppermute(jnp.concatenate(pieces, axis=0), 'rank', shift_x(ranks, k))  23.1 us
    ppermute x3, waiting for transfers between devices, finish(): lax.ppermute(share, 'rank', perm)  20.9 us
    all_to_all x1, waiting for transfers between devices, finish(): lax.all_to_all(part.reshape(nz, rows_z, block), 'rank', split_axis=0, con...  18.8 us
    all_to_all x1, waiting for transfers between devices, finish(): lax.all_to_all(jnp.broadcast_to(mixed[None], (nz, rows_z, block)), 'rank'...  16.8 us
    all_to_all x1, waiting for transfers between devices, finish(): lax.all_to_all(sent, 'rank', split_axis=0, concat_axis=0, tiled=True, axi...  14.2 us
    all_to_all x1, waiting for transfers between devices, project(): lax.all_to_all(sent, 'rank', split_axis=0, concat_axis=0, tiled=True, axi...  9.88 us
    ppermute x3, waiting for transfers between devices, finish(): lax.ppermute(hidden, 'rank', perm)  8.87 us
    all_to_all x1, starting transfers between devices, project(): lax.all_to_all(sent, 'rank', split_axis=0, concat_axis=0, tiled=True, axi...  8.44 us
  transfers between devices with their start and end apart: 26, of which 13 were waited for; matrix products, arithmetic and copies ran while one was open for 13% of the time, Pallas kernels for 8%

profile of v5, /device:TPU:24, one launch (start us, length us, event | category | flops | bytes accessed | tf_op | source)
XLA Modules:
  0.0 246.3 jit_solution(9584625086571616238)
XLA Ops:
  6.5 0.7 all-gather.5.cloned.1.call-update
  7.4 0.9 constant_dynamic-slice_fusion.16
  8.2 0.9 fusion.74
  9.2 1.0 fusion.73
  10.2 1.1 dynamic-slice_bitcast_fusion.4
  11.4 3.1 %collective-permute-start.13 = (bf16[200,896]{1,0:T(8,128)(2,1)S(1)}, bf16[200,896]{1,0:T(8,128)(2,1)S(1)}, u32[]{:S(2)}, u32[]{:S(2)}) collective-permute-start(bf16[200,896]{1,0:T(8,128)(2,1)S(1)} %pad_maximum_fusion.2), channel_id=1, source_target_pairs={{0,128},{8,136},{16,144},{24,152},{32,160},{40,168},{48,176},{56,1... | collective-permute-start | bytes 1075208 | tf_op jit(solution)/shard_map/ppermute | solution.py:250
  14.5 8.2 %attend.1 = bf16[64,24,512]{2,1,0:T(8,128)(2,1)} custom-call(s32[24]{0:T(128)} %lengths.1, bf16[24,64,576]{2,1,0:T(8,128)(2,1)} %queries.1, bf16[24,576,128]{2,1,0:T(8,128)(2,1)} %bitcast.331), custom_call_target="tpu_custom_call" | custom-call | flops 427819008 | bytes 10027008 | tf_op jit(solution)/shard_map/attend/pallas_call | solution.py:87
  22.7 2.2 constant_dynamic-slice_fusion.9
  25.5 2.0 collective-permute-start.16
  28.2 1.5 collective-permute-start.14
  30.3 23.1 %collective-permute-done.14 = bf16[200,896]{1,0:T(8,128)(2,1)S(1)} collective-permute-done((bf16[200,896]{1,0:T(8,128)(2,1)S(1)}, bf16[200,896]{1,0:T(8,128)(2,1)S(1)}, u32[]{:S(2)}, u32[]{:S(2)}) %collective-permute-start.14) | collective-permute-done | bytes 358432 | tf_op jit(solution)/shard_map/ppermute | solution.py:250
  54.3 0.9 pad_maximum_fusion
  55.7 0.7 fusion.70
  59.5 1.9 constant_dynamic-slice_fusion.6
  61.5 6.4 %packed_values.7 = bf16[8,64,256]{2,1,0:T(8,128)(2,1)} custom-call(s32[1,96]{1,0:T(1,128)S(1)} %sub.226.local, bf16[16,24,512]{2,1,0:T(8,128)(2,1)} %get-tuple-element.840.refs_0_, bf16[16,24,512]{2,1,0:T(8,128)(2,1)} %collective-permute-done.15.refs_1_, bf16[16,24,512]{2,1,0:T(8,128)(2,1)} %collective-permute-done.16.refs_2_, ...), custom_call_target="tpu_custom_call" | custom-call | flops 226492416 | bytes 3670016 | tf_op jit(solution)/shard_map/packed_values/pallas_call | solution.py:133
  67.9 8.4 %all-to-all-start.4 = ((bf16[8,64,256]{2,1,0:T(8,128)(2,1)}), bf16[8,64,256]{2,1,0:T(8,128)(2,1)S(1)}, u32[]{:S(2)}, u32[]{:S(2)}) async-start(bf16[8,64,256]{2,1,0:T(8,128)(2,1)} %packed_values.7), calls=%async_computation.4 | async-start | bytes 524288 | tf_op jit(solution)/shard_map/all_to_all | solution.py:292
  77.0 9.9 %all-to-all-done.4 = bf16[8,64,256]{2,1,0:T(8,128)(2,1)S(1)} async-done(((bf16[8,64,256]{2,1,0:T(8,128)(2,1)}), bf16[8,64,256]{2,1,0:T(8,128)(2,1)S(1)}, u32[]{:S(2)}, u32[]{:S(2)}) %all-to-all-start.4) | async-done | bytes 262176 | tf_op jit(solution)/shard_map/all_to_all | solution.py:292
  87.2 1.5 collective-permute-start.19
  88.7 3.1 %collective-permute-start.20 = (bf16[384,256]{1,0:T(8,128)(2,1)S(1)}, bf16[384,256]{1,0:T(8,128)(2,1)}, u32[]{:S(2)}, u32[]{:S(2)}) collective-permute-start(bf16[384,256]{1,0:T(8,128)(2,1)S(1)} %convolution_convert_fusion.1), channel_id=1, source_target_pairs={{0,192},{8,200},{16,208},{24,216},{32,224},{40,232},{48,240},{56,2... | collective-permute-start | bytes 589832 | tf_op jit(solution)/shard_map/ppermute | solution.py:301
  91.8 1.4 fusion.78
  93.6 2.9 %collective-permute-done.19 = bf16[384,256]{1,0:T(8,128)(2,1)} collective-permute-done((bf16[384,256]{1,0:T(8,128)(2,1)S(1)}, bf16[384,256]{1,0:T(8,128)(2,1)}, u32[]{:S(2)}, u32[]{:S(2)}) %collective-permute-start.19) | collective-permute-done | bytes 196640 | tf_op jit(solution)/shard_map/ppermute | solution.py:301
  96.5 1.5 fusion.45
  98.0 0.8 collective-permute-done.20
  98.8 1.3 fusion.44
  100.1 2.2 fusion.42
  102.3 3.7 %all-to-all-start.5 = ((bf16[8,48,896]{2,1,0:T(8,128)(2,1)}), bf16[8,48,896]{2,1,0:T(8,128)(2,1)S(1)}, u32[]{:S(2)}, u32[]{:S(2)}) async-start(bf16[8,48,896]{2,1,0:T(8,128)(2,1)} %bitcast.57), calls=%async_computation.5 | async-start | bytes 1376256 | tf_op jit(solution)/shard_map/all_to_all | solution.py:323
  106.1 0.7 pad_maximum_fusion.4
  106.9 18.8 %all-to-all-done.5 = bf16[8,48,896]{2,1,0:T(8,128)(2,1)S(1)} async-done(((bf16[8,48,896]{2,1,0:T(8,128)(2,1)}), bf16[8,48,896]{2,1,0:T(8,128)(2,1)S(1)}, u32[]{:S(2)}, u32[]{:S(2)}) %all-to-all-start.5) | async-done | bytes 688160 | tf_op jit(solution)/shard_map/all_to_all | solution.py:323
  125.8 0.9 broadcast_in_dim.108
  126.7 3.8 %all-to-all-start.6 = ((bf16[8,48,896]{2,1,0:T(8,128)(2,1)}), bf16[8,48,896]{2,1,0:T(8,128)(2,1)S(1)}, u32[]{:S(2)}, u32[]{:S(2)}) async-start(bf16[8,48,896]{2,1,0:T(8,128)(2,1)} %broadcast_in_dim.108), calls=%async_computation.6 | async-start | bytes 1376256 | tf_op jit(solution)/shard_map/all_to_all | solution.py:332
  130.5 0.8 dynamic-slice_convert_fusion
  131.3 1.3 dynamic-slice_bitcast_fusion.3.mine
  132.6 16.8 %all-to-all-done.6 = bf16[8,48,896]{2,1,0:T(8,128)(2,1)S(1)} async-done(((bf16[8,48,896]{2,1,0:T(8,128)(2,1)}), bf16[8,48,896]{2,1,0:T(8,128)(2,1)S(1)}, u32[]{:S(2)}, u32[]{:S(2)}) %all-to-all-start.6) | async-done | bytes 688160 | tf_op jit(solution)/shard_map/all_to_all | solution.py:332
  149.4 5.0 %gate_up_shares.7 = (bf16[592,384]{1,0:T(8,128)(2,1)S(1)}, bf16[592,384]{1,0:T(8,128)(2,1)S(1)}, bf16[592,384]{1,0:T(8,128)(2,1)S(1)}, bf16[592,384]{1,0:T(8,128)(2,1)S(1)}) custom-call(bf16[384,896]{1,0:T(8,128)(2,1)S(1)} %bitcast.324, f32[1,896]{1,0:T(1,128)S(1)} %broadcast_in_dim.109.gain, bf16[576,896]{1,0:T(8,128)(2,1)S(1)} %dynamic-slice_bitcast_fusion.3.mine, ...), custom_call_target="tpu_custom_call" | custom-call | flops 1585446912 | bytes 6586368 | tf_op jit(solution)/shard_map/gate_up_shares/pallas_call | solution.py:170
  154.5 4.5 %collective-permute-start.21 = (bf16[592,384]{1,0:T(8,128)(2,1)S(1)}, bf16[592,384]{1,0:T(8,128)(2,1)S(1)}, u32[]{:S(2)}, u32[]{:S(2)}) collective-permute-start(bf16[592,384]{1,0:T(8,128)(2,1)S(1)} %get-tuple-element.433), channel_id=1, source_target_pairs={{0,192},{8,200},{16,208},{24,216},{32,224},{40,232},{48,240},{56,2... | collective-permute-start | bytes 1363976 | tf_op jit(solution)/shard_map/ppermute | solution.py:344
  159.0 1.0 collective-permute-start.23
  160.0 1.1 constant_dynamic-slice_fusion.5.refs_4_
  161.1 17.4 %collective-permute-done.21 = bf16[592,384]{1,0:T(8,128)(2,1)S(1)} collective-permute-done((bf16[592,384]{1,0:T(8,128)(2,1)S(1)}, bf16[592,384]{1,0:T(8,128)(2,1)S(1)}, u32[]{:S(2)}, u32[]{:S(2)}) %collective-permute-start.21) | collective-permute-done | bytes 454688 | tf_op jit(solution)/shard_map/ppermute | solution.py:344
  178.5 3.4 %collective-permute-done.23 = bf16[592,384]{1,0:T(8,128)(2,1)S(1)} collective-permute-done((bf16[592,384]{1,0:T(8,128)(2,1)S(1)}, bf16[592,384]{1,0:T(8,128)(2,1)S(1)}, u32[]{:S(2)}, u32[]{:S(2)}) %collective-permute-start.23) | collective-permute-done | bytes 454688 | tf_op jit(solution)/shard_map/ppermute | solution.py:344
  182.4 2.3 collective-permute-start.25
  184.8 0.9 collective-permute-start.26
  185.7 1.5 slice_bitcast_fusion.3
  187.1 8.2 %collective-permute-done.24.refs_1_ = bf16[288,384]{1,0:T(8,128)(2,1)S(1)} collective-permute-done((bf16[288,384]{1,0:T(8,128)(2,1)S(1)}, bf16[288,384]{1,0:T(8,128)(2,1)S(1)}, u32[]{:S(2)}, u32[]{:S(2)}) %collective-permute-start.24) | collective-permute-done | bytes 221216 | tf_op jit(solution)/shard_map/ppermute | solution.py:349
  196.0 4.2 %down_rows.7 = bf16[8,64,896]{2,1,0:T(8,128)(2,1)} custom-call(s32[8]{0:T(128)S(1)} %fusion.68.target, bf16[288,384]{1,0:T(8,128)(2,1)S(1)} %fusion.47.refs_0_, bf16[288,384]{1,0:T(8,128)(2,1)S(1)} %collective-permute-done.24.refs_1_, bf16[288,384]{1,0:T(8,128)(2,1)S(1)} %collective-permute-done.25.refs_2_, ...), custom_call_target="tpu_custom_call" | custom-call | flops 1145044992 | bytes 3866624 | tf_op jit(solution)/shard_map/down_rows/pallas_call | solution.py:205
  200.2 3.7 %all-to-all-start.7 = ((bf16[8,64,896]{2,1,0:T(8,128)(2,1)}), bf16[8,64,896]{2,1,0:T(8,128)(2,1)S(1)}, u32[]{:S(2)}, u32[]{:S(2)}) async-start(bf16[8,64,896]{2,1,0:T(8,128)(2,1)} %down_rows.7), calls=%async_computation.7 | async-start | bytes 1835008 | tf_op jit(solution)/shard_map/all_to_all | solution.py:352
  214.5 14.2 %all-to-all-done.7 = bf16[8,64,896]{2,1,0:T(8,128)(2,1)S(1)} async-done(((bf16[8,64,896]{2,1,0:T(8,128)(2,1)}), bf16[8,64,896]{2,1,0:T(8,128)(2,1)S(1)}, u32[]{:S(2)}, u32[]{:S(2)}) %all-to-all-start.7) | async-done | bytes 917536 | tf_op jit(solution)/shard_map/all_to_all | solution.py:352
  229.1 3.6 %collective-permute-start.27 = (bf16[24,896]{1,0:T(8,128)(2,1)S(1)}, bf16[24,896]{1,0:T(8,128)(2,1)S(1)}, u32[]{:S(2)}, u32[]{:S(2)}) collective-permute-start(bf16[24,896]{1,0:T(8,128)(2,1)S(1)} %get-tuple-element.522), channel_id=1, source_target_pairs={{0,192},{8,200},{16,208},{24,216},{32,224},{40,232},{48,240},{56,2... | collective-permute-start | bytes 129032 | tf_op jit(solution)/shard_map/ppermute | solution.py:369
  234.4 3.9 %collective-permute-done.28 = bf16[24,896]{1,0:T(8,128)(2,1)S(1)} collective-permute-done((bf16[24,896]{1,0:T(8,128)(2,1)S(1)}, bf16[24,896]{1,0:T(8,128)(2,1)S(1)}, u32[]{:S(2)}, u32[]{:S(2)}) %collective-permute-start.28) | collective-permute-done | bytes 43040 | tf_op jit(solution)/shard_map/ppermute | solution.py:369
  (119 shorter events, 14.3 us)
Async XLA Ops:
  6.5 55.0 %all-gather.5.cloned.1.call-start = ((), (), s32[]{:S(2)}) async-start(), calls=%async_computation.8 | async-start | bytes 2359296 | tf_op jit(solution)/shard_map/all_gather | solution.py:433
  7.3 86.4 %all-gather.7.cloned.1.call-start = ((), (), s32[]{:S(2)}) async-start(), calls=%async_computation.9 | async-start | bytes 1548288 | tf_op jit(solution)/shard_map/all_gather | solution.py:259
  8.2 85.0 %copy-start.11 = (bf16[24,896]{1,0:T(8,128)(2,1)}, bf16[24,896]{1,0:T(8,128)(2,1)S(1)}, u32[]{:S(2)}) copy-start(bf16[24,896]{1,0:T(8,128)(2,1)S(1)} %get-tuple-element.523) | copy-start | bytes 129028
  11.4 18.4 %collective-permute-start.13 = (bf16[200,896]{1,0:T(8,128)(2,1)S(1)}, bf16[200,896]{1,0:T(8,128)(2,1)S(1)}, u32[]{:S(2)}, u32[]{:S(2)}) collective-permute-start(bf16[200,896]{1,0:T(8,128)(2,1)S(1)} %pad_maximum_fusion.2), channel_id=1, source_target_pairs={{0,128},{8,136},{16,144},{24,152},{32,160},{40,168},{48,176},{56,1... | collective-permute-start | bytes 1075208 | tf_op jit(solution)/shard_map/ppermute | solution.py:250
  24.9 28.5 %collective-permute-start.15 = (bf16[16,24,512]{2,1,0:T(8,128)(2,1)S(1)}, bf16[16,24,512]{2,1,0:T(8,128)(2,1)}, u32[]{:S(2)}, u32[]{:S(2)}) collective-permute-start(bf16[16,24,512]{2,1,0:T(8,128)(2,1)S(1)} %get-tuple-element.514), channel_id=1, source_target_pairs={{0,64},{8,72},{16,80},{24,88},{32,96},{40,104},{48,112},{56,120},{... | collective-permute-start | bytes 1179656 | tf_op jit(solution)/shard_map/ppermute | solution.py:442
  25.5 28.0 %collective-permute-start.16 = (bf16[16,24,512]{2,1,0:T(8,128)(2,1)S(1)}, bf16[16,24,512]{2,1,0:T(8,128)(2,1)}, u32[]{:S(2)}, u32[]{:S(2)}) collective-permute-start(bf16[16,24,512]{2,1,0:T(8,128)(2,1)S(1)} %get-tuple-element.513), channel_id=1, source_target_pairs={{0,128},{8,136},{16,144},{24,152},{32,160},{40,168},{48,176},{56,1... | collective-permute-start | bytes 1179656 | tf_op jit(solution)/shard_map/ppermute | solution.py:442
  27.5 26.0 %collective-permute-start.17 = (bf16[16,24,512]{2,1,0:T(8,128)(2,1)S(1)}, bf16[16,24,512]{2,1,0:T(8,128)(2,1)}, u32[]{:S(2)}, u32[]{:S(2)}) collective-permute-start(bf16[16,24,512]{2,1,0:T(8,128)(2,1)S(1)} %get-tuple-element.512), channel_id=1, source_target_pairs={{0,192},{8,200},{16,208},{24,216},{32,224},{40,232},{48,240},{56,2... | collective-permute-start | bytes 1179656 | tf_op jit(solution)/shard_map/ppermute | solution.py:442
  28.2 25.2 %collective-permute-start.14 = (bf16[200,896]{1,0:T(8,128)(2,1)S(1)}, bf16[200,896]{1,0:T(8,128)(2,1)S(1)}, u32[]{:S(2)}, u32[]{:S(2)}) collective-permute-start(bf16[200,896]{1,0:T(8,128)(2,1)S(1)} %pad_maximum_fusion.3), channel_id=1, source_target_pairs={{0,192},{8,200},{16,208},{24,216},{32,224},{40,232},{48,240},{56,2... | collective-permute-start | bytes 1075208 | tf_op jit(solution)/shard_map/ppermute | solution.py:250
  29.7 23.7 %collective-permute-start.12 = (bf16[200,896]{1,0:T(8,128)(2,1)S(1)}, bf16[200,896]{1,0:T(8,128)(2,1)S(1)}, u32[]{:S(2)}, u32[]{:S(2)}) collective-permute-start(bf16[200,896]{1,0:T(8,128)(2,1)S(1)} %pad_maximum_fusion.1), channel_id=1, source_target_pairs={{0,64},{8,72},{16,80},{24,88},{32,96},{40,104},{48,112},{56,120},{... | collective-permute-start | bytes 1075208 | tf_op jit(solution)/shard_map/ppermute | solution.py:250
  54.2 1.0 copy-start.15
  54.2 95.2 %all-gather.9.cloned.1.call-start = ((), (), s32[]{:S(2)}) async-start(), calls=%async_computation.10 | async-start | bytes 4644864 | tf_op jit(solution)/shard_map/all_gather | solution.py:259
  61.4 31.8 %copy-start.7 = (bf16[24,896]{1,0:T(8,128)(2,1)}, bf16[24,896]{1,0:T(8,128)(2,1)S(1)}, u32[]{:S(2)}) copy-start(bf16[24,896]{1,0:T(8,128)(2,1)S(1)} %slice.199) | copy-start | bytes 129028
  61.5 31.8 %copy-start.9 = (bf16[24,896]{1,0:T(8,128)(2,1)}, bf16[24,896]{1,0:T(8,128)(2,1)S(1)}, u32[]{:S(2)}) copy-start(bf16[24,896]{1,0:T(8,128)(2,1)S(1)} %slice.200) | copy-start | bytes 129028
  67.9 19.0 %all-to-all-start.4 = ((bf16[8,64,256]{2,1,0:T(8,128)(2,1)}), bf16[8,64,256]{2,1,0:T(8,128)(2,1)S(1)}, u32[]{:S(2)}, u32[]{:S(2)}) async-start(bf16[8,64,256]{2,1,0:T(8,128)(2,1)} %packed_values.7), calls=%async_computation.4 | async-start | bytes 524288 | tf_op jit(solution)/shard_map/all_to_all | solution.py:292
  87.2 9.3 %collective-permute-start.19 = (bf16[384,256]{1,0:T(8,128)(2,1)S(1)}, bf16[384,256]{1,0:T(8,128)(2,1)}, u32[]{:S(2)}, u32[]{:S(2)}) collective-permute-start(bf16[384,256]{1,0:T(8,128)(2,1)S(1)} %convolution_convert_fusion.1), channel_id=1, source_target_pairs={{0,128},{8,136},{16,144},{24,152},{32,160},{40,168},{48,176},{56,1... | collective-permute-start | bytes 589832 | tf_op jit(solution)/shard_map/ppermute | solution.py:301
  88.7 10.1 %collective-permute-start.20 = (bf16[384,256]{1,0:T(8,128)(2,1)S(1)}, bf16[384,256]{1,0:T(8,128)(2,1)}, u32[]{:S(2)}, u32[]{:S(2)}) collective-permute-start(bf16[384,256]{1,0:T(8,128)(2,1)S(1)} %convolution_convert_fusion.1), channel_id=1, source_target_pairs={{0,192},{8,200},{16,208},{24,216},{32,224},{40,232},{48,240},{56,2... | collective-permute-start | bytes 589832 | tf_op jit(solution)/shard_map/ppermute | solution.py:301
  91.8 8.3 %collective-permute-start.18 = (bf16[384,256]{1,0:T(8,128)(2,1)S(1)}, bf16[384,256]{1,0:T(8,128)(2,1)}, u32[]{:S(2)}, u32[]{:S(2)}) collective-permute-start(bf16[384,256]{1,0:T(8,128)(2,1)S(1)} %convolution_convert_fusion.1), channel_id=1, source_target_pairs={{0,64},{8,72},{16,80},{24,88},{32,96},{40,104},{48,112},{56,120},{... | collective-permute-start | bytes 589832 | tf_op jit(solution)/shard_map/ppermute | solution.py:301
  93.6 5.2 %copy-start = (bf16[3,256,896]{2,1,0:T(8,128)(2,1)S(1)}, bf16[3,256,896]{2,1,0:T(8,128)(2,1)}, u32[]{:S(2)}) copy-start(bf16[3,256,896]{2,1,0:T(8,128)(2,1)} %all-gather.7.cloned.1.call-done) | copy-start | bytes 4128772
  102.3 3.7 %copy-start.13 = (bf16[1,48,896]{2,1,0:T(8,128)(2,1)S(1)}, bf16[1,48,896]{2,1,0:T(8,128)(2,1)}, u32[]{:S(2)}) copy-start(bf16[1,48,896]{2,1,0:T(8,128)(2,1)} %get-tuple-element.546) | copy-start | bytes 258052
  102.3 23.4 %all-to-all-start.5 = ((bf16[8,48,896]{2,1,0:T(8,128)(2,1)}), bf16[8,48,896]{2,1,0:T(8,128)(2,1)S(1)}, u32[]{:S(2)}, u32[]{:S(2)}) async-start(bf16[8,48,896]{2,1,0:T(8,128)(2,1)} %bitcast.57), calls=%async_computation.5 | async-start | bytes 1376256 | tf_op jit(solution)/shard_map/all_to_all | solution.py:323
  106.0 79.6 %all-gather.11.cloned.1.call-start = ((), (), s32[]{:S(2)}) async-start(), calls=%async_computation.11 | async-start | bytes 2322432 | tf_op jit(solution)/shard_map/all_gather | solution.py:259
  126.7 22.7 %all-to-all-start.6 = ((bf16[8,48,896]{2,1,0:T(8,128)(2,1)}), bf16[8,48,896]{2,1,0:T(8,128)(2,1)S(1)}, u32[]{:S(2)}, u32[]{:S(2)}) async-start(bf16[8,48,896]{2,1,0:T(8,128)(2,1)} %broadcast_in_dim.108), calls=%async_computation.6 | async-start | bytes 1376256 | tf_op jit(solution)/shard_map/all_to_all | solution.py:332
  131.3 80.9 %copy-start.14 = (f32[896]{0:T(1024)}, f32[896]{0:T(1024)S(1)}, u32[]{:S(2)}) copy-start(f32[896]{0:T(1024)S(1)} %dynamic-slice_convert_fusion) | copy-start | bytes 10756
  132.6 21.9 %copy-start.3 = (bf16[576,896]{1,0:T(8,128)(2,1)}, bf16[576,896]{1,0:T(8,128)(2,1)S(1)}, u32[]{:S(2)}) copy-start(bf16[576,896]{1,0:T(8,128)(2,1)S(1)} %dynamic-slice_bitcast_fusion.3.mine) | copy-start | bytes 3096580
  154.5 24.0 %collective-permute-start.21 = (bf16[592,384]{1,0:T(8,128)(2,1)S(1)}, bf16[592,384]{1,0:T(8,128)(2,1)S(1)}, u32[]{:S(2)}, u32[]{:S(2)}) collective-permute-start(bf16[592,384]{1,0:T(8,128)(2,1)S(1)} %get-tuple-element.433), channel_id=1, source_target_pairs={{0,192},{8,200},{16,208},{24,216},{32,224},{40,232},{48,240},{56,2... | collective-permute-start | bytes 1363976 | tf_op jit(solution)/shard_map/ppermute | solution.py:344
  159.0 19.5 %collective-permute-start.22 = (bf16[592,384]{1,0:T(8,128)(2,1)S(1)}, bf16[592,384]{1,0:T(8,128)(2,1)S(1)}, u32[]{:S(2)}, u32[]{:S(2)}) collective-permute-start(bf16[592,384]{1,0:T(8,128)(2,1)S(1)} %get-tuple-element.434), channel_id=1, source_target_pairs={{0,128},{8,136},{16,144},{24,152},{32,160},{40,168},{48,176},{56,1... | collective-permute-start | bytes 1363976 | tf_op jit(solution)/shard_map/ppermute | solution.py:344
  159.0 22.9 %collective-permute-start.23 = (bf16[592,384]{1,0:T(8,128)(2,1)S(1)}, bf16[592,384]{1,0:T(8,128)(2,1)S(1)}, u32[]{:S(2)}, u32[]{:S(2)}) collective-permute-start(bf16[592,384]{1,0:T(8,128)(2,1)S(1)} %get-tuple-element.435), channel_id=1, source_target_pairs={{0,64},{8,72},{16,80},{24,88},{32,96},{40,104},{48,112},{56,120},{... | collective-permute-start | bytes 1363976 | tf_op jit(solution)/shard_map/ppermute | solution.py:344
  161.1 34.9 %copy-start.5 = (bf16[288,896]{1,0:T(8,128)(2,1)}, bf16[288,896]{1,0:T(8,128)(2,1)S(1)}, u32[]{:S(2)}) copy-start(bf16[288,896]{1,0:T(8,128)(2,1)S(1)} %constant_dynamic-slice_fusion.5.refs_4_) | copy-start | bytes 1548292
  182.3 13.0 %collective-permute-start.24 = (bf16[288,384]{1,0:T(8,128)(2,1)S(1)}, bf16[288,384]{1,0:T(8,128)(2,1)S(1)}, u32[]{:S(2)}, u32[]{:S(2)}) collective-permute-start(bf16[288,384]{1,0:T(8,128)(2,1)S(1)} %fusion.47.refs_0_), channel_id=1, source_target_pairs={{0,64},{8,72},{16,80},{24,88},{32,96},{40,104},{48,112},{56,120},{... | collective-permute-start | bytes 663560 | tf_op jit(solution)/shard_map/ppermute | solution.py:349
  182.4 12.9 %collective-permute-start.25 = (bf16[288,384]{1,0:T(8,128)(2,1)S(1)}, bf16[288,384]{1,0:T(8,128)(2,1)S(1)}, u32[]{:S(2)}, u32[]{:S(2)}) collective-permute-start(bf16[288,384]{1,0:T(8,128)(2,1)S(1)} %fusion.47.refs_0_), channel_id=1, source_target_pairs={{0,128},{8,136},{16,144},{24,152},{32,160},{40,168},{48,176},{56,1... | collective-permute-start | bytes 663560 | tf_op jit(solution)/shard_map/ppermute | solution.py:349
  184.8 11.2 %collective-permute-start.26 = (bf16[288,384]{1,0:T(8,128)(2,1)S(1)}, bf16[288,384]{1,0:T(8,128)(2,1)S(1)}, u32[]{:S(2)}, u32[]{:S(2)}) collective-permute-start(bf16[288,384]{1,0:T(8,128)(2,1)S(1)} %fusion.47.refs_0_), channel_id=1, source_target_pairs={{0,192},{8,200},{16,208},{24,216},{32,224},{40,232},{48,240},{56,2... | collective-permute-start | bytes 663560 | tf_op jit(solution)/shard_map/ppermute | solution.py:349
  200.2 13.2 %copy-start.16 = (pred[4,24]{1,0:T(4,128)(4,1)S(1)}, pred[4,24]{1,0:T(4,128)(4,1)}, u32[]{:S(2)}) copy-start(pred[4,24]{1,0:T(4,128)(4,1)} %get-tuple-element.485) | copy-start | bytes 292
  200.2 28.5 %all-to-all-start.7 = ((bf16[8,64,896]{2,1,0:T(8,128)(2,1)}), bf16[8,64,896]{2,1,0:T(8,128)(2,1)S(1)}, u32[]{:S(2)}, u32[]{:S(2)}) async-start(bf16[8,64,896]{2,1,0:T(8,128)(2,1)} %down_rows.7), calls=%async_computation.7 | async-start | bytes 1835008 | tf_op jit(solution)/shard_map/all_to_all | solution.py:352
  214.1 19.6 %copy-start.8 = (bf16[24,896]{1,0:T(8,128)(2,1)S(1)}, bf16[24,896]{1,0:T(8,128)(2,1)}, u32[]{:S(2)}) copy-start(bf16[24,896]{1,0:T(8,128)(2,1)} %copy-done.7) | copy-start | bytes 129028
  214.1 19.6 %copy-start.10 = (bf16[24,896]{1,0:T(8,128)(2,1)S(1)}, bf16[24,896]{1,0:T(8,128)(2,1)}, u32[]{:S(2)}) copy-start(bf16[24,896]{1,0:T(8,128)(2,1)} %copy-done.9) | copy-start | bytes 129028
  214.2 19.5 %copy-start.12 = (bf16[24,896]{1,0:T(8,128)(2,1)S(1)}, bf16[24,896]{1,0:T(8,128)(2,1)}, u32[]{:S(2)}) copy-start(bf16[24,896]{1,0:T(8,128)(2,1)} %copy-done.11) | copy-start | bytes 129028
  229.1 5.3 %collective-permute-start.27 = (bf16[24,896]{1,0:T(8,128)(2,1)S(1)}, bf16[24,896]{1,0:T(8,128)(2,1)S(1)}, u32[]{:S(2)}, u32[]{:S(2)}) collective-permute-start(bf16[24,896]{1,0:T(8,128)(2,1)S(1)} %get-tuple-element.522), channel_id=1, source_target_pairs={{0,192},{8,200},{16,208},{24,216},{32,224},{40,232},{48,240},{56,2... | collective-permute-start | bytes 129032 | tf_op jit(solution)/shard_map/ppermute | solution.py:369
  232.7 5.6 %collective-permute-start.28 = (bf16[24,896]{1,0:T(8,128)(2,1)S(1)}, bf16[24,896]{1,0:T(8,128)(2,1)S(1)}, u32[]{:S(2)}, u32[]{:S(2)}) collective-permute-start(bf16[24,896]{1,0:T(8,128)(2,1)S(1)} %get-tuple-element.521), channel_id=1, source_target_pairs={{0,128},{8,136},{16,144},{24,152},{32,160},{40,168},{48,176},{56,1... | collective-permute-start | bytes 129032 | tf_op jit(solution)/shard_map/ppermute | solution.py:369
  233.0 5.7 %collective-permute-start.29 = (bf16[24,896]{1,0:T(8,128)(2,1)S(1)}, bf16[24,896]{1,0:T(8,128)(2,1)S(1)}, u32[]{:S(2)}, u32[]{:S(2)}) collective-permute-start(bf16[24,896]{1,0:T(8,128)(2,1)S(1)} %get-tuple-element.520), channel_id=1, source_target_pairs={{0,64},{8,72},{16,80},{24,88},{32,96},{40,104},{48,112},{56,120},{... | collective-permute-start | bytes 129032 | tf_op jit(solution)/shard_map/ppermute | solution.py:369
  239.1 0.7 copy-start.2
Sparse Core Ops, SparseCore 0:
  9.1 43.8 all-gather.4
  54.8 26.6 all-gather.6
  83.3 34.4 all-gather.8
  119.5 28.1 all-gather.10

commit v6 on v5

--- a/solution.py
+++ b/solution.py
@@ -115,14 +115,11 @@
     pick = (turn == local[...]).astype(F32).astype(BF16)
     each = heads // blocks
 
-    @pl.loop(0, blocks)
-    def _(block):
-        for i in range(each):
-            head = block * each + i
-            latent = jnp.concatenate([ref[head].astype(F32) for ref in latents], axis=0)
-            values = dot(latent.astype(BF16), value_up[head]).astype(BF16)
-            columns = slice(i * value_width, (i + 1) * value_width)
-            out[block, :, columns] = dot(pick, values).astype(BF16)
+    for head in range(heads):
+        latent = jnp.concatenate([ref[head].astype(F32) for ref in latents], axis=0)
+        values = dot(latent.astype(BF16), value_up[head]).astype(BF16)
+        columns = slice(head % each * value_width, (head % each + 1) * value_width)
+        out[head // each, :, columns] = dot(pick, values).astype(BF16)
 
 
 def packed_values(latents, value_up, local, blocks):
@@ -227,9 +224,9 @@
 
 
 def part_rows(height, members):
-    rows = -(-height // (16 * members)) * 16
+    rows = -(-height // (8 * members)) * 8
     while height % rows:
-        rows += 16
+        rows += 8
     return rows
 
 
@@ -433,6 +430,8 @@
     value_up = lax.all_gather(
         value_up, "rank", axis=0, tiled=True, axis_index_groups=groups_z(ranks)
     )
+    got = lax.optimization_barrier((got, latent))[0]
+
     each = latent.shape[0] // NX
 
     def heads_of(x):
@@ -442,7 +441,6 @@
         lax.ppermute(heads_of(lax.rem(my_x + k, NX)), "rank", shift_x(ranks, k))
         for k in range(1, NX)
     ]
-    got = lax.optimization_barrier((got, latents))[0]
     projs, *feeds = gather_parts(parts, got)
     my_proj = take_cols(out_proj, my_x, block)
     res = [take_cols(residual, my_x, block)] + [g[sum(parts) :] for g in got]

time: 248 us -> 240 us (0.968)
  waiting for transfers between devices: 121 us -> 109 us
  starting transfers between devices: 46.2 us -> 49.5 us
  local copies, waits for them, and re-layouts: 17.3 us -> 20.2 us
    ppermute x3, waiting for transfers between devices: 23.1 us -> 4.12 us  [exchange_parts(): lax.ppermute(jnp.concatenate(pieces, axis=0), 'rank', shift_x(ranks, k))]
    ppermute x3, waiting for transfers between devices: 0.01 us -> 9.16 us  [per_device(): lax.ppermute(heads_of(lax.rem(my_x + k, NX)), 'rank', shift_x(ranks, k))]
  transfers between devices with their start and end apart: 26 -> 26, of which waited for: 13 -> 15; matrix products, arithmetic and copies ran while one was open for 13% -> 14% of each run, Pallas kernels for 8% -> 8%
where the time goes in v6:
time: 240 us; the launch traced here: 238 us
  waiting for transfers between devices  109 us (45%)
  starting transfers between devices  49.5 us (21%)
  Pallas kernels  22.7 us (9%)
  between operations  22.6 us (9%)
  local copies, waits for them, and re-layouts  20.2 us (8%)
  matrix products  7.45 us (3%)
  other arithmetic  7.17 us (3%)
    ppermute x3, waiting for transfers between devices, finish(): lax.ppermute(share, 'rank', perm)  19.6 us
    all_to_all x1, waiting for transfers between devices, finish(): lax.all_to_all(part.reshape(nz, rows_z, block), 'rank', split_axis=0, con...  18.5 us
    all_to_all x1, waiting for transfers between devices, finish(): lax.all_to_all(jnp.broadcast_to(mixed[None], (nz, rows_z, block)), 'rank'...  16.6 us
    all_to_all x1, waiting for transfers between devices, finish(): lax.all_to_all(sent, 'rank', split_axis=0, concat_axis=0, tiled=True, axi...  14.5 us
    all_to_all x1, waiting for transfers between devices, project(): lax.all_to_all(sent, 'rank', split_axis=0, concat_axis=0, tiled=True, axi...  9.37 us
    ppermute x3, waiting for transfers between devices, per_device(): lax.ppermute(heads_of(lax.rem(my_x + k, NX)), 'rank', shift_x(ranks, k))  9.16 us
    all_to_all x1, starting transfers between devices, project(): lax.all_to_all(sent, 'rank', split_axis=0, concat_axis=0, tiled=True, axi...  8.36 us
    pallas_call x1, Pallas kernels, attend(): pl.pallas_call(functools.partial(attend_kernel, scale, step_slots), out_s...  8.19 us
  transfers between devices with their start and end apart: 26, of which 15 were waited for; matrix products, arithmetic and copies ran while one was open for 14% of the time, Pallas kernels for 8%

profile of v6, /device:TPU:24, one launch (start us, length us, event | category | flops | bytes accessed | tf_op | source)
XLA Modules:
  0.0 238.5 jit_solution(7124889907893626561)
XLA Ops:
  8.2 0.9 fusion.74
  9.2 1.0 fusion.73
  10.2 1.1 dynamic-slice_bitcast_fusion.4
  11.3 3.1 %collective-permute-start.13 = (bf16[176,896]{1,0:T(8,128)(2,1)S(1)}, bf16[176,896]{1,0:T(8,128)(2,1)S(1)}, u32[]{:S(2)}, u32[]{:S(2)}) collective-permute-start(bf16[176,896]{1,0:T(8,128)(2,1)S(1)} %pad_maximum_fusion.2), channel_id=1, source_target_pairs={{0,128},{8,136},{16,144},{24,152},{32,160},{40,168},{48,176},{56,1... | collective-permute-start | bytes 946184 | tf_op jit(solution)/shard_map/ppermute | solution.py:247
  14.4 1.2 collective-permute-start.14
  15.7 1.0 collective-permute-start.12
  16.6 8.2 %attend.1 = bf16[64,24,512]{2,1,0:T(8,128)(2,1)} custom-call(s32[24]{0:T(128)} %lengths.1, bf16[24,64,576]{2,1,0:T(8,128)(2,1)} %queries.1, bf16[24,576,128]{2,1,0:T(8,128)(2,1)} %bitcast.331), custom_call_target="tpu_custom_call" | custom-call | flops 427819008 | bytes 10027008 | tf_op jit(solution)/shard_map/attend/pallas_call | solution.py:87
  24.8 4.1 %collective-permute-done.14 = bf16[176,896]{1,0:T(8,128)(2,1)S(1)} collective-permute-done((bf16[176,896]{1,0:T(8,128)(2,1)S(1)}, bf16[176,896]{1,0:T(8,128)(2,1)S(1)}, u32[]{:S(2)}, u32[]{:S(2)}) %collective-permute-start.14) | collective-permute-done | bytes 315424 | tf_op jit(solution)/shard_map/ppermute | solution.py:247
  30.5 0.9 slice_bitcast_fusion.12
  33.2 1.4 collective-permute-start.15
  34.5 2.7 %collective-permute-start.16 = (bf16[16,24,512]{2,1,0:T(8,128)(2,1)S(1)}, bf16[16,24,512]{2,1,0:T(8,128)(2,1)}, u32[]{:S(2)}, u32[]{:S(2)}) collective-permute-start(bf16[16,24,512]{2,1,0:T(8,128)(2,1)S(1)} %get-tuple-element.513), channel_id=1, source_target_pairs={{0,128},{8,136},{16,144},{24,152},{32,160},{40,168},{48,176},{56,1... | collective-permute-start | bytes 1179656 | tf_op jit(solution)/shard_map/ppermute | solution.py:441
  42.3 1.8 constant_dynamic-slice_fusion.6
  45.8 9.2 %collective-permute-done.16.refs_2_ = bf16[16,24,512]{2,1,0:T(8,128)(2,1)} collective-permute-done((bf16[16,24,512]{2,1,0:T(8,128)(2,1)S(1)}, bf16[16,24,512]{2,1,0:T(8,128)(2,1)}, u32[]{:S(2)}, u32[]{:S(2)}) %collective-permute-start.16) | collective-permute-done | bytes 393248 | tf_op jit(solution)/shard_map/ppermute | solution.py:441
  54.9 5.5 %packed_values.7 = bf16[8,64,256]{2,1,0:T(8,128)(2,1)} custom-call(s32[1,96]{1,0:T(1,128)S(1)} %sub.226.local, bf16[16,24,512]{2,1,0:T(8,128)(2,1)} %get-tuple-element.840.refs_0_, bf16[16,24,512]{2,1,0:T(8,128)(2,1)} %collective-permute-done.15.refs_1_, bf16[16,24,512]{2,1,0:T(8,128)(2,1)} %collective-permute-done.16.refs_2_, ...), custom_call_target="tpu_custom_call" | custom-call | flops 226492416 | bytes 3670016 | tf_op jit(solution)/shard_map/packed_values/pallas_call | solution.py:130
  60.4 8.4 %all-to-all-start.4 = ((bf16[8,64,256]{2,1,0:T(8,128)(2,1)}), bf16[8,64,256]{2,1,0:T(8,128)(2,1)S(1)}, u32[]{:S(2)}, u32[]{:S(2)}) async-start(bf16[8,64,256]{2,1,0:T(8,128)(2,1)} %packed_values.7), calls=%async_computation.4 | async-start | bytes 524288 | tf_op jit(solution)/shard_map/all_to_all | solution.py:289
  68.8 0.9 slice_bitcast_fusion.17
  69.7 0.9 slice_bitcast_fusion.15
  70.6 9.4 %all-to-all-done.4 = bf16[8,64,256]{2,1,0:T(8,128)(2,1)S(1)} async-done(((bf16[8,64,256]{2,1,0:T(8,128)(2,1)}), bf16[8,64,256]{2,1,0:T(8,128)(2,1)S(1)}, u32[]{:S(2)}, u32[]{:S(2)}) %all-to-all-start.4) | async-done | bytes 262176 | tf_op jit(solution)/shard_map/all_to_all | solution.py:289
  80.0 1.0 convolution_convert_fusion.1
  80.9 1.9 collective-permute-start.19
  82.9 2.4 collective-permute-start.20
  85.2 1.5 fusion.78
  87.1 3.0 %collective-permute-done.19 = bf16[384,256]{1,0:T(8,128)(2,1)} collective-permute-done((bf16[384,256]{1,0:T(8,128)(2,1)}, bf16[384,256]{1,0:T(8,128)(2,1)}, u32[]{:S(2)}, u32[]{:S(2)}) %collective-permute-start.19) | collective-permute-done | bytes 196640 | tf_op jit(solution)/shard_map/ppermute | solution.py:298
  90.1 1.5 fusion.45
  92.4 1.3 fusion.44
  93.8 1.3 fusion.42
  95.1 3.5 %all-to-all-start.5 = ((bf16[8,48,896]{2,1,0:T(8,128)(2,1)}), bf16[8,48,896]{2,1,0:T(8,128)(2,1)S(1)}, u32[]{:S(2)}, u32[]{:S(2)}) async-start(bf16[8,48,896]{2,1,0:T(8,128)(2,1)} %bitcast.57), calls=%async_computation.5 | async-start | bytes 1376256 | tf_op jit(solution)/shard_map/all_to_all | solution.py:320
  99.4 18.5 %all-to-all-done.5 = bf16[8,48,896]{2,1,0:T(8,128)(2,1)S(1)} async-done(((bf16[8,48,896]{2,1,0:T(8,128)(2,1)}), bf16[8,48,896]{2,1,0:T(8,128)(2,1)S(1)}, u32[]{:S(2)}, u32[]{:S(2)}) %all-to-all-start.5) | async-done | bytes 688160 | tf_op jit(solution)/shard_map/all_to_all | solution.py:320
  118.0 0.9 broadcast_in_dim.108
  118.9 3.5 %all-to-all-start.6 = ((bf16[8,48,896]{2,1,0:T(8,128)(2,1)}), bf16[8,48,896]{2,1,0:T(8,128)(2,1)S(1)}, u32[]{:S(2)}, u32[]{:S(2)}) async-start(bf16[8,48,896]{2,1,0:T(8,128)(2,1)} %broadcast_in_dim.108), calls=%async_computation.6 | async-start | bytes 1376256 | tf_op jit(solution)/shard_map/all_to_all | solution.py:329
  123.3 1.3 dynamic-slice_bitcast_fusion.3.mine
  124.6 16.6 %all-to-all-done.6 = bf16[8,48,896]{2,1,0:T(8,128)(2,1)S(1)} async-done(((bf16[8,48,896]{2,1,0:T(8,128)(2,1)}), bf16[8,48,896]{2,1,0:T(8,128)(2,1)S(1)}, u32[]{:S(2)}, u32[]{:S(2)}) %all-to-all-start.6) | async-done | bytes 688160 | tf_op jit(solution)/shard_map/all_to_all | solution.py:329
  141.2 4.7 %gate_up_shares.7 = (bf16[592,384]{1,0:T(8,128)(2,1)S(1)}, bf16[592,384]{1,0:T(8,128)(2,1)S(1)}, bf16[592,384]{1,0:T(8,128)(2,1)S(1)}, bf16[592,384]{1,0:T(8,128)(2,1)S(1)}) custom-call(bf16[384,896]{1,0:T(8,128)(2,1)S(1)} %bitcast.324, f32[1,896]{1,0:T(1,128)S(1)} %broadcast_in_dim.109.gain, bf16[576,896]{1,0:T(8,128)(2,1)S(1)} %dynamic-slice_bitcast_fusion.3.mine, ...), custom_call_target="tpu_custom_call" | custom-call | flops 1585446912 | bytes 6586368 | tf_op jit(solution)/shard_map/gate_up_shares/pallas_call | solution.py:167
  146.0 5.4 %collective-permute-start.21 = (bf16[592,384]{1,0:T(8,128)(2,1)S(1)}, bf16[592,384]{1,0:T(8,128)(2,1)S(1)}, u32[]{:S(2)}, u32[]{:S(2)}) collective-permute-start(bf16[592,384]{1,0:T(8,128)(2,1)S(1)} %get-tuple-element.433), channel_id=1, source_target_pairs={{0,192},{8,200},{16,208},{24,216},{32,224},{40,232},{48,240},{56,2... | collective-permute-start | bytes 1363976 | tf_op jit(solution)/shard_map/ppermute | solution.py:341
  151.4 1.8 collective-permute-start.22
  153.2 1.1 constant_dynamic-slice_fusion.5.refs_4_
  154.3 8.1 %collective-permute-done.21 = bf16[592,384]{1,0:T(8,128)(2,1)S(1)} collective-permute-done((bf16[592,384]{1,0:T(8,128)(2,1)S(1)}, bf16[592,384]{1,0:T(8,128)(2,1)S(1)}, u32[]{:S(2)}, u32[]{:S(2)}) %collective-permute-start.21) | collective-permute-done | bytes 454688 | tf_op jit(solution)/shard_map/ppermute | solution.py:341
  162.3 4.0 %collective-permute-done.22 = bf16[592,384]{1,0:T(8,128)(2,1)S(1)} collective-permute-done((bf16[592,384]{1,0:T(8,128)(2,1)S(1)}, bf16[592,384]{1,0:T(8,128)(2,1)S(1)}, u32[]{:S(2)}, u32[]{:S(2)}) %collective-permute-start.22) | collective-permute-done | bytes 454688 | tf_op jit(solution)/shard_map/ppermute | solution.py:341
  166.3 7.5 %collective-permute-done.23 = bf16[592,384]{1,0:T(8,128)(2,1)S(1)} collective-permute-done((bf16[592,384]{1,0:T(8,128)(2,1)S(1)}, bf16[592,384]{1,0:T(8,128)(2,1)S(1)}, u32[]{:S(2)}, u32[]{:S(2)}) %collective-permute-start.23) | collective-permute-done | bytes 454688 | tf_op jit(solution)/shard_map/ppermute | solution.py:341
  174.2 1.3 collective-permute-start.24
  176.4 2.3 collective-permute-start.26
  178.7 1.5 slice_bitcast_fusion.3
  180.2 7.4 %collective-permute-done.24.refs_1_ = bf16[288,384]{1,0:T(8,128)(2,1)S(1)} collective-permute-done((bf16[288,384]{1,0:T(8,128)(2,1)S(1)}, bf16[288,384]{1,0:T(8,128)(2,1)S(1)}, u32[]{:S(2)}, u32[]{:S(2)}) %collective-permute-start.24) | collective-permute-done | bytes 221216 | tf_op jit(solution)/shard_map/ppermute | solution.py:346
  188.2 4.3 %down_rows.7 = bf16[8,64,896]{2,1,0:T(8,128)(2,1)} custom-call(s32[8]{0:T(128)S(1)} %fusion.68.target, bf16[288,384]{1,0:T(8,128)(2,1)S(1)} %fusion.47.refs_0_, bf16[288,384]{1,0:T(8,128)(2,1)S(1)} %collective-permute-done.24.refs_1_, bf16[288,384]{1,0:T(8,128)(2,1)S(1)} %collective-permute-done.25.refs_2_, ...), custom_call_target="tpu_custom_call" | custom-call | flops 1145044992 | bytes 3866624 | tf_op jit(solution)/shard_map/down_rows/pallas_call | solution.py:202
  192.5 3.7 %all-to-all-start.7 = ((bf16[8,64,896]{2,1,0:T(8,128)(2,1)}), bf16[8,64,896]{2,1,0:T(8,128)(2,1)S(1)}, u32[]{:S(2)}, u32[]{:S(2)}) async-start(bf16[8,64,896]{2,1,0:T(8,128)(2,1)} %down_rows.7), calls=%async_computation.7 | async-start | bytes 1835008 | tf_op jit(solution)/shard_map/all_to_all | solution.py:349
  206.9 14.5 %all-to-all-done.7 = bf16[8,64,896]{2,1,0:T(8,128)(2,1)S(1)} async-done(((bf16[8,64,896]{2,1,0:T(8,128)(2,1)}), bf16[8,64,896]{2,1,0:T(8,128)(2,1)S(1)}, u32[]{:S(2)}, u32[]{:S(2)}) %all-to-all-start.7) | async-done | bytes 917536 | tf_op jit(solution)/shard_map/all_to_all | solution.py:349
  221.8 3.2 %collective-permute-start.27 = (bf16[24,896]{1,0:T(8,128)(2,1)S(1)}, bf16[24,896]{1,0:T(8,128)(2,1)S(1)}, u32[]{:S(2)}, u32[]{:S(2)}) collective-permute-start(bf16[24,896]{1,0:T(8,128)(2,1)S(1)} %get-tuple-element.522), channel_id=1, source_target_pairs={{0,192},{8,200},{16,208},{24,216},{32,224},{40,232},{48,240},{56,2... | collective-permute-start | bytes 129032 | tf_op jit(solution)/shard_map/ppermute | solution.py:366
  226.7 3.9 %collective-permute-done.28 = bf16[24,896]{1,0:T(8,128)(2,1)S(1)} collective-permute-done((bf16[24,896]{1,0:T(8,128)(2,1)S(1)}, bf16[24,896]{1,0:T(8,128)(2,1)S(1)}, u32[]{:S(2)}, u32[]{:S(2)}) %collective-permute-start.28) | collective-permute-done | bytes 43040 | tf_op jit(solution)/shard_map/ppermute | solution.py:366
  (125 shorter events, 21.4 us)
Async XLA Ops:
  6.5 48.4 %all-gather.5.cloned.1.call-start = ((), (), s32[]{:S(2)}) async-start(), calls=%async_computation.8 | async-start | bytes 2359296 | tf_op jit(solution)/shard_map/all_gather | solution.py:430
  7.3 79.9 %all-gather.7.cloned.1.call-start = ((), (), s32[]{:S(2)}) async-start(), calls=%async_computation.9 | async-start | bytes 1548288 | tf_op jit(solution)/shard_map/all_gather | solution.py:256
  8.2 78.5 %copy-start.12 = (bf16[24,896]{1,0:T(8,128)(2,1)}, bf16[24,896]{1,0:T(8,128)(2,1)S(1)}, u32[]{:S(2)}) copy-start(bf16[24,896]{1,0:T(8,128)(2,1)S(1)} %get-tuple-element.523) | copy-start | bytes 129028
  11.3 13.5 %collective-permute-start.13 = (bf16[176,896]{1,0:T(8,128)(2,1)S(1)}, bf16[176,896]{1,0:T(8,128)(2,1)S(1)}, u32[]{:S(2)}, u32[]{:S(2)}) collective-permute-start(bf16[176,896]{1,0:T(8,128)(2,1)S(1)} %pad_maximum_fusion.2), channel_id=1, source_target_pairs={{0,128},{8,136},{16,144},{24,152},{32,160},{40,168},{48,176},{56,1... | collective-permute-start | bytes 946184 | tf_op jit(solution)/shard_map/ppermute | solution.py:247
  14.4 14.5 %collective-permute-start.14 = (bf16[176,896]{1,0:T(8,128)(2,1)S(1)}, bf16[176,896]{1,0:T(8,128)(2,1)S(1)}, u32[]{:S(2)}, u32[]{:S(2)}) collective-permute-start(bf16[176,896]{1,0:T(8,128)(2,1)S(1)} %pad_maximum_fusion.3), channel_id=1, source_target_pairs={{0,192},{8,200},{16,208},{24,216},{32,224},{40,232},{48,240},{56,2... | collective-permute-start | bytes 946184 | tf_op jit(solution)/shard_map/ppermute | solution.py:247
  15.7 13.3 %collective-permute-start.12 = (bf16[176,896]{1,0:T(8,128)(2,1)S(1)}, bf16[176,896]{1,0:T(8,128)(2,1)S(1)}, u32[]{:S(2)}, u32[]{:S(2)}) collective-permute-start(bf16[176,896]{1,0:T(8,128)(2,1)S(1)} %pad_maximum_fusion.1), channel_id=1, source_target_pairs={{0,64},{8,72},{16,80},{24,88},{32,96},{40,104},{48,112},{56,120},{... | collective-permute-start | bytes 946184 | tf_op jit(solution)/shard_map/ppermute | solution.py:247
  24.8 20.1 %copy-start.14 = (bf16[176,896]{1,0:T(8,128)(2,1)}, bf16[176,896]{1,0:T(8,128)(2,1)S(1)}, u32[]{:S(2)}) copy-start(bf16[176,896]{1,0:T(8,128)(2,1)S(1)} %collective-permute-done.13) | copy-start | bytes 946180
  29.0 0.7 copy-start.15
  29.0 1.5 copy-start.16
  29.7 2.6 %copy-start.2 = (bf16[64,24,512]{2,1,0:T(8,128)(2,1)S(1)}, bf16[64,24,512]{2,1,0:T(8,128)(2,1)}, u32[]{:S(2)}) copy-start(bf16[64,24,512]{2,1,0:T(8,128)(2,1)} %attend.1) | copy-start | bytes 4718596
  30.4 94.2 %all-gather.9.cloned.1.call-start = ((), (), s32[]{:S(2)}) async-start(), calls=%async_computation.10 | async-start | bytes 3483648 | tf_op jit(solution)/shard_map/all_gather | solution.py:256
  32.3 5.8 %copy-start.18 = (s32[32]{0:T(128)S(1)}, s32[32]{0:T(128)}, u32[]{:S(2)}) copy-start(s32[32]{0:T(128)} %param.16) | copy-start | bytes 388
  33.2 12.6 %collective-permute-start.15 = (bf16[16,24,512]{2,1,0:T(8,128)(2,1)S(1)}, bf16[16,24,512]{2,1,0:T(8,128)(2,1)}, u32[]{:S(2)}, u32[]{:S(2)}) collective-permute-start(bf16[16,24,512]{2,1,0:T(8,128)(2,1)S(1)} %get-tuple-element.514), channel_id=1, source_target_pairs={{0,64},{8,72},{16,80},{24,88},{32,96},{40,104},{48,112},{56,120},{... | collective-permute-start | bytes 1179656 | tf_op jit(solution)/shard_map/ppermute | solution.py:441
  34.5 20.4 %collective-permute-start.16 = (bf16[16,24,512]{2,1,0:T(8,128)(2,1)S(1)}, bf16[16,24,512]{2,1,0:T(8,128)(2,1)}, u32[]{:S(2)}, u32[]{:S(2)}) collective-permute-start(bf16[16,24,512]{2,1,0:T(8,128)(2,1)S(1)} %get-tuple-element.513), channel_id=1, source_target_pairs={{0,128},{8,136},{16,144},{24,152},{32,160},{40,168},{48,176},{56,1... | collective-permute-start | bytes 1179656 | tf_op jit(solution)/shard_map/ppermute | solution.py:441
  37.3 17.7 %collective-permute-start.17 = (bf16[16,24,512]{2,1,0:T(8,128)(2,1)S(1)}, bf16[16,24,512]{2,1,0:T(8,128)(2,1)}, u32[]{:S(2)}, u32[]{:S(2)}) collective-permute-start(bf16[16,24,512]{2,1,0:T(8,128)(2,1)S(1)} %get-tuple-element.512), channel_id=1, source_target_pairs={{0,192},{8,200},{16,208},{24,216},{32,224},{40,232},{48,240},{56,2... | collective-permute-start | bytes 1179656 | tf_op jit(solution)/shard_map/ppermute | solution.py:441
  44.9 41.8 %copy-start.8 = (bf16[24,896]{1,0:T(8,128)(2,1)}, bf16[24,896]{1,0:T(8,128)(2,1)S(1)}, u32[]{:S(2)}) copy-start(bf16[24,896]{1,0:T(8,128)(2,1)S(1)} %slice.199) | copy-start | bytes 129028
  45.8 41.0 %copy-start.10 = (bf16[24,896]{1,0:T(8,128)(2,1)}, bf16[24,896]{1,0:T(8,128)(2,1)S(1)}, u32[]{:S(2)}) copy-start(bf16[24,896]{1,0:T(8,128)(2,1)S(1)} %slice.200) | copy-start | bytes 129028
  60.4 19.6 %all-to-all-start.4 = ((bf16[8,64,256]{2,1,0:T(8,128)(2,1)}), bf16[8,64,256]{2,1,0:T(8,128)(2,1)S(1)}, u32[]{:S(2)}, u32[]{:S(2)}) async-start(bf16[8,64,256]{2,1,0:T(8,128)(2,1)} %packed_values.7), calls=%async_computation.4 | async-start | bytes 524288 | tf_op jit(solution)/shard_map/all_to_all | solution.py:289
  80.9 9.2 %collective-permute-start.19 = (bf16[384,256]{1,0:T(8,128)(2,1)}, bf16[384,256]{1,0:T(8,128)(2,1)}, u32[]{:S(2)}, u32[]{:S(2)}) collective-permute-start(bf16[384,256]{1,0:T(8,128)(2,1)} %convolution_convert_fusion.1), channel_id=1, source_target_pairs={{0,128},{8,136},{16,144},{24,152},{32,160},{40,168},{48,176},{56,1... | collective-permute-start | bytes 589832 | tf_op jit(solution)/shard_map/ppermute | solution.py:298
  82.9 9.6 %collective-permute-start.20 = (bf16[384,256]{1,0:T(8,128)(2,1)}, bf16[384,256]{1,0:T(8,128)(2,1)}, u32[]{:S(2)}, u32[]{:S(2)}) collective-permute-start(bf16[384,256]{1,0:T(8,128)(2,1)} %convolution_convert_fusion.1), channel_id=1, source_target_pairs={{0,192},{8,200},{16,208},{24,216},{32,224},{40,232},{48,240},{56,2... | collective-permute-start | bytes 589832 | tf_op jit(solution)/shard_map/ppermute | solution.py:298
  85.2 8.5 %collective-permute-start.18 = (bf16[384,256]{1,0:T(8,128)(2,1)}, bf16[384,256]{1,0:T(8,128)(2,1)S(1)}, u32[]{:S(2)}, u32[]{:S(2)}) collective-permute-start(bf16[384,256]{1,0:T(8,128)(2,1)} %convolution_convert_fusion.1), channel_id=1, source_target_pairs={{0,64},{8,72},{16,80},{24,88},{32,96},{40,104},{48,112},{56,120},{... | collective-permute-start | bytes 589832 | tf_op jit(solution)/shard_map/ppermute | solution.py:298
  87.1 5.3 %copy-start = (bf16[3,256,896]{2,1,0:T(8,128)(2,1)S(1)}, bf16[3,256,896]{2,1,0:T(8,128)(2,1)}, u32[]{:S(2)}) copy-start(bf16[3,256,896]{2,1,0:T(8,128)(2,1)} %all-gather.7.cloned.1.call-done) | copy-start | bytes 4128772
  95.1 22.8 %all-to-all-start.5 = ((bf16[8,48,896]{2,1,0:T(8,128)(2,1)}), bf16[8,48,896]{2,1,0:T(8,128)(2,1)S(1)}, u32[]{:S(2)}, u32[]{:S(2)}) async-start(bf16[8,48,896]{2,1,0:T(8,128)(2,1)} %bitcast.57), calls=%async_computation.5 | async-start | bytes 1376256 | tf_op jit(solution)/shard_map/all_to_all | solution.py:320
  98.6 80.1 %all-gather.11.cloned.1.call-start = ((), (), s32[]{:S(2)}) async-start(), calls=%async_computation.11 | async-start | bytes 2322432 | tf_op jit(solution)/shard_map/all_gather | solution.py:256
  118.9 22.3 %all-to-all-start.6 = ((bf16[8,48,896]{2,1,0:T(8,128)(2,1)}), bf16[8,48,896]{2,1,0:T(8,128)(2,1)S(1)}, u32[]{:S(2)}, u32[]{:S(2)}) async-start(bf16[8,48,896]{2,1,0:T(8,128)(2,1)} %broadcast_in_dim.108), calls=%async_computation.6 | async-start | bytes 1376256 | tf_op jit(solution)/shard_map/all_to_all | solution.py:329
  123.3 81.4 %copy-start.17 = (f32[896]{0:T(1024)}, f32[896]{0:T(1024)S(1)}, u32[]{:S(2)}) copy-start(f32[896]{0:T(1024)S(1)} %dynamic-slice_convert_fusion) | copy-start | bytes 10756
  124.6 21.4 %copy-start.4 = (bf16[576,896]{1,0:T(8,128)(2,1)}, bf16[576,896]{1,0:T(8,128)(2,1)S(1)}, u32[]{:S(2)}) copy-start(bf16[576,896]{1,0:T(8,128)(2,1)S(1)} %dynamic-slice_bitcast_fusion.3.mine) | copy-start | bytes 3096580
  146.0 16.3 %collective-permute-start.21 = (bf16[592,384]{1,0:T(8,128)(2,1)S(1)}, bf16[592,384]{1,0:T(8,128)(2,1)S(1)}, u32[]{:S(2)}, u32[]{:S(2)}) collective-permute-start(bf16[592,384]{1,0:T(8,128)(2,1)S(1)} %get-tuple-element.433), channel_id=1, source_target_pairs={{0,192},{8,200},{16,208},{24,216},{32,224},{40,232},{48,240},{56,2... | collective-permute-start | bytes 1363976 | tf_op jit(solution)/shard_map/ppermute | solution.py:341
  151.4 14.9 %collective-permute-start.22 = (bf16[592,384]{1,0:T(8,128)(2,1)S(1)}, bf16[592,384]{1,0:T(8,128)(2,1)S(1)}, u32[]{:S(2)}, u32[]{:S(2)}) collective-permute-start(bf16[592,384]{1,0:T(8,128)(2,1)S(1)} %get-tuple-element.434), channel_id=1, source_target_pairs={{0,128},{8,136},{16,144},{24,152},{32,160},{40,168},{48,176},{56,1... | collective-permute-start | bytes 1363976 | tf_op jit(solution)/shard_map/ppermute | solution.py:341
  153.2 20.7 %collective-permute-start.23 = (bf16[592,384]{1,0:T(8,128)(2,1)S(1)}, bf16[592,384]{1,0:T(8,128)(2,1)S(1)}, u32[]{:S(2)}, u32[]{:S(2)}) collective-permute-start(bf16[592,384]{1,0:T(8,128)(2,1)S(1)} %get-tuple-element.435), channel_id=1, source_target_pairs={{0,64},{8,72},{16,80},{24,88},{32,96},{40,104},{48,112},{56,120},{... | collective-permute-start | bytes 1363976 | tf_op jit(solution)/shard_map/ppermute | solution.py:341
  154.2 34.0 %copy-start.6 = (bf16[288,896]{1,0:T(8,128)(2,1)}, bf16[288,896]{1,0:T(8,128)(2,1)S(1)}, u32[]{:S(2)}) copy-start(bf16[288,896]{1,0:T(8,128)(2,1)S(1)} %constant_dynamic-slice_fusion.5.refs_4_) | copy-start | bytes 1548292
  174.2 13.4 %collective-permute-start.24 = (bf16[288,384]{1,0:T(8,128)(2,1)S(1)}, bf16[288,384]{1,0:T(8,128)(2,1)S(1)}, u32[]{:S(2)}, u32[]{:S(2)}) collective-permute-start(bf16[288,384]{1,0:T(8,128)(2,1)S(1)} %fusion.47.refs_0_), channel_id=1, source_target_pairs={{0,64},{8,72},{16,80},{24,88},{32,96},{40,104},{48,112},{56,120},{... | collective-permute-start | bytes 663560 | tf_op jit(solution)/shard_map/ppermute | solution.py:346
  175.5 12.1 %collective-permute-start.25 = (bf16[288,384]{1,0:T(8,128)(2,1)S(1)}, bf16[288,384]{1,0:T(8,128)(2,1)S(1)}, u32[]{:S(2)}, u32[]{:S(2)}) collective-permute-start(bf16[288,384]{1,0:T(8,128)(2,1)S(1)} %fusion.47.refs_0_), channel_id=1, source_target_pairs={{0,128},{8,136},{16,144},{24,152},{32,160},{40,168},{48,176},{56,1... | collective-permute-start | bytes 663560 | tf_op jit(solution)/shard_map/ppermute | solution.py:346
  176.4 11.9 %collective-permute-start.26 = (bf16[288,384]{1,0:T(8,128)(2,1)S(1)}, bf16[288,384]{1,0:T(8,128)(2,1)S(1)}, u32[]{:S(2)}, u32[]{:S(2)}) collective-permute-start(bf16[288,384]{1,0:T(8,128)(2,1)S(1)} %fusion.47.refs_0_), channel_id=1, source_target_pairs={{0,192},{8,200},{16,208},{24,216},{32,224},{40,232},{48,240},{56,2... | collective-permute-start | bytes 663560 | tf_op jit(solution)/shard_map/ppermute | solution.py:346
  192.5 13.4 %copy-start.19 = (pred[4,24]{1,0:T(4,128)(4,1)S(1)}, pred[4,24]{1,0:T(4,128)(4,1)}, u32[]{:S(2)}) copy-start(pred[4,24]{1,0:T(4,128)(4,1)} %get-tuple-element.485) | copy-start | bytes 292
  192.5 28.9 %all-to-all-start.7 = ((bf16[8,64,896]{2,1,0:T(8,128)(2,1)}), bf16[8,64,896]{2,1,0:T(8,128)(2,1)S(1)}, u32[]{:S(2)}, u32[]{:S(2)}) async-start(bf16[8,64,896]{2,1,0:T(8,128)(2,1)} %down_rows.7), calls=%async_computation.7 | async-start | bytes 1835008 | tf_op jit(solution)/shard_map/all_to_all | solution.py:349
  206.6 19.4 %copy-start.9 = (bf16[24,896]{1,0:T(8,128)(2,1)S(1)}, bf16[24,896]{1,0:T(8,128)(2,1)}, u32[]{:S(2)}) copy-start(bf16[24,896]{1,0:T(8,128)(2,1)} %copy-done.8) | copy-start | bytes 129028
  206.6 19.4 %copy-start.11 = (bf16[24,896]{1,0:T(8,128)(2,1)S(1)}, bf16[24,896]{1,0:T(8,128)(2,1)}, u32[]{:S(2)}) copy-start(bf16[24,896]{1,0:T(8,128)(2,1)} %copy-done.10) | copy-start | bytes 129028
  206.6 19.4 %copy-start.13 = (bf16[24,896]{1,0:T(8,128)(2,1)S(1)}, bf16[24,896]{1,0:T(8,128)(2,1)}, u32[]{:S(2)}) copy-start(bf16[24,896]{1,0:T(8,128)(2,1)} %copy-done.12) | copy-start | bytes 129028
  221.8 4.9 %collective-permute-start.27 = (bf16[24,896]{1,0:T(8,128)(2,1)S(1)}, bf16[24,896]{1,0:T(8,128)(2,1)S(1)}, u32[]{:S(2)}, u32[]{:S(2)}) collective-permute-start(bf16[24,896]{1,0:T(8,128)(2,1)S(1)} %get-tuple-element.522), channel_id=1, source_target_pairs={{0,192},{8,200},{16,208},{24,216},{32,224},{40,232},{48,240},{56,2... | collective-permute-start | bytes 129032 | tf_op jit(solution)/shard_map/ppermute | solution.py:366
  225.0 5.6 %collective-permute-start.28 = (bf16[24,896]{1,0:T(8,128)(2,1)S(1)}, bf16[24,896]{1,0:T(8,128)(2,1)S(1)}, u32[]{:S(2)}, u32[]{:S(2)}) collective-permute-start(bf16[24,896]{1,0:T(8,128)(2,1)S(1)} %get-tuple-element.521), channel_id=1, source_target_pairs={{0,128},{8,136},{16,144},{24,152},{32,160},{40,168},{48,176},{56,1... | collective-permute-start | bytes 129032 | tf_op jit(solution)/shard_map/ppermute | solution.py:366
  225.2 5.7 %collective-permute-start.29 = (bf16[24,896]{1,0:T(8,128)(2,1)S(1)}, bf16[24,896]{1,0:T(8,128)(2,1)S(1)}, u32[]{:S(2)}, u32[]{:S(2)}) collective-permute-start(bf16[24,896]{1,0:T(8,128)(2,1)S(1)} %get-tuple-element.520), channel_id=1, source_target_pairs={{0,64},{8,72},{16,80},{24,88},{32,96},{40,104},{48,112},{56,120},{... | collective-permute-start | bytes 129032 | tf_op jit(solution)/shard_map/ppermute | solution.py:366
  231.3 0.7 copy-start.3
Sparse Core Ops, SparseCore 0:
  9.1 43.9 all-gather.4
  54.9 23.3 all-gather.6
  80.2 30.7 all-gather.8
  112.7 27.5 all-gather.10

commit v7 on v6

--- a/solution.py
+++ b/solution.py
@@ -441,7 +441,9 @@
         lax.ppermute(heads_of(lax.rem(my_x + k, NX)), "rank", shift_x(ranks, k))
         for k in range(1, NX)
     ]
-    projs, *feeds = gather_parts(parts, got)
+    (projs,) = gather_parts(parts[:1], got)
+    late = lax.optimization_barrier(([g[parts[0] : sum(parts)] for g in got], latents[1]))[0]
+    feeds = gather_parts(parts[1:], late)
     my_proj = take_cols(out_proj, my_x, block)
     res = [take_cols(residual, my_x, block)] + [g[sum(parts) :] for g in got]
     res = jnp.concatenate(res, axis=0)

time: 240 us -> 252 us (1.050)
  waiting for transfers between devices: 109 us -> 123 us
  local copies, waits for them, and re-layouts: 20.2 us -> 16.5 us
    ppermute x3, waiting for transfers between devices: 9.16 us -> 20.8 us  [per_device(): lax.ppermute(heads_of(lax.rem(my_x + k, NX)), 'rank', shift_x(ranks, k))]
    another operation x6, local copies, waits for them, and re-layouts: 2.79 us -> 0.08 us  [gather_parts(): gathered.append(jnp.stack([g[first:first + rows] for g in got]))]
  transfers between devices with their start and end apart: 26 -> 26, of which waited for: 15 -> 16; matrix products, arithmetic and copies ran while one was open for 14% -> 12% of each run, Pallas kernels for 8% -> 7%
where the time goes in v7:
time: 252 us; the launch traced here: 251 us
  waiting for transfers between devices  123 us (49%)
  starting transfers between devices  51.2 us (20%)
  Pallas kernels  22.9 us (9%)
  between operations  22.4 us (9%)
  local copies, waits for them, and re-layouts  16.5 us (7%)
  matrix products  7.45 us (3%)
  other arithmetic  7.26 us (3%)
    ppermute x3, waiting for transfers between devices, per_device(): lax.ppermute(heads_of(lax.rem(my_x + k, NX)), 'rank', shift_x(ranks, k))  20.8 us
    ppermute x3, waiting for transfers between devices, finish(): lax.ppermute(share, 'rank', perm)  20.4 us
    all_to_all x1, waiting for transfers between devices, finish(): lax.all_to_all(part.reshape(nz, rows_z, block), 'rank', split_axis=0, con...  18.2 us
    all_to_all x1, waiting for transfers between devices, finish(): lax.all_to_all(jnp.broadcast_to(mixed[None], (nz, rows_z, block)), 'rank'...  16.7 us
    all_to_all x1, waiting for transfers between devices, finish(): lax.all_to_all(sent, 'rank', split_axis=0, concat_axis=0, tiled=True, axi...  14.9 us
    all_to_all x1, waiting for transfers between devices, project(): lax.all_to_all(sent, 'rank', split_axis=0, concat_axis=0, tiled=True, axi...  10.9 us
    pallas_call x1, Pallas kernels, attend(): pl.pallas_call(functools.partial(attend_kernel, scale, step_slots), out_s...  8.2 us
    all_to_all x1, starting transfers between devices, project(): lax.all_to_all(sent, 'rank', split_axis=0, concat_axis=0, tiled=True, axi...  8.07 us
  transfers between devices with their start and end apart: 26, of which 16 were waited for; matrix products, arithmetic and copies ran while one was open for 12% of the time, Pallas kernels for 7%

profile of v7, /device:TPU:24, one launch (start us, length us, event | category | flops | bytes accessed | tf_op | source)
XLA Modules:
  0.0 250.8 jit_solution(9546879658000326205)
XLA Ops:
  9.2 1.0 fusion.73
  10.2 1.1 dynamic-slice_bitcast_fusion.4
  11.3 3.1 %collective-permute-start.13 = (bf16[176,896]{1,0:T(8,128)(2,1)S(1)}, bf16[176,896]{1,0:T(8,128)(2,1)S(1)}, u32[]{:S(2)}, u32[]{:S(2)}) collective-permute-start(bf16[176,896]{1,0:T(8,128)(2,1)S(1)} %pad_maximum_fusion.2), channel_id=1, source_target_pairs={{0,128},{8,136},{16,144},{24,152},{32,160},{40,168},{48,176},{56,1... | collective-permute-start | bytes 946184 | tf_op jit(solution)/shard_map/ppermute | solution.py:247
  14.4 1.2 collective-permute-start.14
  15.7 1.0 collective-permute-start.12
  16.6 8.2 %attend.1 = bf16[64,24,512]{2,1,0:T(8,128)(2,1)} custom-call(s32[24]{0:T(128)} %lengths.1, bf16[24,64,576]{2,1,0:T(8,128)(2,1)} %queries.1, bf16[24,576,128]{2,1,0:T(8,128)(2,1)} %bitcast.331), custom_call_target="tpu_custom_call" | custom-call | flops 427819008 | bytes 10027008 | tf_op jit(solution)/shard_map/attend/pallas_call | solution.py:87
  24.8 4.1 %collective-permute-done.14 = bf16[176,896]{1,0:T(8,128)(2,1)S(1)} collective-permute-done((bf16[176,896]{1,0:T(8,128)(2,1)S(1)}, bf16[176,896]{1,0:T(8,128)(2,1)S(1)}, u32[]{:S(2)}, u32[]{:S(2)}) %collective-permute-start.14) | collective-permute-done | bytes 315424 | tf_op jit(solution)/shard_map/ppermute | solution.py:247
  29.8 2.2 constant_dynamic-slice_fusion.7
  32.0 1.4 collective-permute-start.15
  33.5 10.8 %collective-permute-done.15.refs_1_ = bf16[16,24,512]{2,1,0:T(8,128)(2,1)} collective-permute-done((bf16[16,24,512]{2,1,0:T(8,128)(2,1)S(1)}, bf16[16,24,512]{2,1,0:T(8,128)(2,1)}, u32[]{:S(2)}, u32[]{:S(2)}) %collective-permute-start.15) | collective-permute-done | bytes 393248 | tf_op jit(solution)/shard_map/ppermute | solution.py:441
  45.2 1.9 collective-permute-start.16
  47.1 1.2 collective-permute-start.17
  52.7 1.8 constant_dynamic-slice_fusion.6
  54.6 2.5 collective-permute-done.16.refs_2_
  57.1 7.5 %collective-permute-done.17.refs_3_ = bf16[16,24,512]{2,1,0:T(8,128)(2,1)} collective-permute-done((bf16[16,24,512]{2,1,0:T(8,128)(2,1)S(1)}, bf16[16,24,512]{2,1,0:T(8,128)(2,1)}, u32[]{:S(2)}, u32[]{:S(2)}) %collective-permute-start.17) | collective-permute-done | bytes 393248 | tf_op jit(solution)/shard_map/ppermute | solution.py:441
  64.6 5.6 %packed_values.7 = bf16[8,64,256]{2,1,0:T(8,128)(2,1)} custom-call(s32[1,96]{1,0:T(1,128)S(1)} %sub.226.local, bf16[16,24,512]{2,1,0:T(8,128)(2,1)} %get-tuple-element.846.refs_0_, bf16[16,24,512]{2,1,0:T(8,128)(2,1)} %collective-permute-done.15.refs_1_, bf16[16,24,512]{2,1,0:T(8,128)(2,1)} %collective-permute-done.16.refs_2_, ...), custom_call_target="tpu_custom_call" | custom-call | flops 226492416 | bytes 3670016 | tf_op jit(solution)/shard_map/packed_values/pallas_call | solution.py:130
  70.2 8.1 %all-to-all-start.4 = ((bf16[8,64,256]{2,1,0:T(8,128)(2,1)}), bf16[8,64,256]{2,1,0:T(8,128)(2,1)S(1)}, u32[]{:S(2)}, u32[]{:S(2)}) async-start(bf16[8,64,256]{2,1,0:T(8,128)(2,1)} %packed_values.7), calls=%async_computation.4 | async-start | bytes 524288 | tf_op jit(solution)/shard_map/all_to_all | solution.py:289
  78.3 10.9 %all-to-all-done.4 = bf16[8,64,256]{2,1,0:T(8,128)(2,1)S(1)} async-done(((bf16[8,64,256]{2,1,0:T(8,128)(2,1)}), bf16[8,64,256]{2,1,0:T(8,128)(2,1)S(1)}, u32[]{:S(2)}, u32[]{:S(2)}) %all-to-all-start.4) | async-done | bytes 262176 | tf_op jit(solution)/shard_map/all_to_all | solution.py:289
  89.2 1.0 convolution_convert_fusion.1
  90.2 2.2 collective-permute-start.19
  92.4 3.2 %collective-permute-start.20 = (bf16[384,256]{1,0:T(8,128)(2,1)}, bf16[384,256]{1,0:T(8,128)(2,1)}, u32[]{:S(2)}, u32[]{:S(2)}) collective-permute-start(bf16[384,256]{1,0:T(8,128)(2,1)} %convolution_convert_fusion.1), channel_id=1, source_target_pairs={{0,192},{8,200},{16,208},{24,216},{32,224},{40,232},{48,240},{56,2... | collective-permute-start | bytes 589832 | tf_op jit(solution)/shard_map/ppermute | solution.py:298
  95.5 1.5 fusion.78
  97.4 1.9 collective-permute-done.19
  99.4 1.5 fusion.45
  100.9 1.8 collective-permute-done.20
  102.7 1.3 fusion.44
  104.0 1.3 fusion.42
  105.3 3.5 %all-to-all-start.5 = ((bf16[8,48,896]{2,1,0:T(8,128)(2,1)}), bf16[8,48,896]{2,1,0:T(8,128)(2,1)S(1)}, u32[]{:S(2)}, u32[]{:S(2)}) async-start(bf16[8,48,896]{2,1,0:T(8,128)(2,1)} %bitcast.57), calls=%async_computation.5 | async-start | bytes 1376256 | tf_op jit(solution)/shard_map/all_to_all | solution.py:320
  109.9 18.2 %all-to-all-done.5 = bf16[8,48,896]{2,1,0:T(8,128)(2,1)S(1)} async-done(((bf16[8,48,896]{2,1,0:T(8,128)(2,1)}), bf16[8,48,896]{2,1,0:T(8,128)(2,1)S(1)}, u32[]{:S(2)}, u32[]{:S(2)}) %all-to-all-start.5) | async-done | bytes 688160 | tf_op jit(solution)/shard_map/all_to_all | solution.py:320
  128.2 0.9 broadcast_in_dim.108
  129.2 3.5 %all-to-all-start.6 = ((bf16[8,48,896]{2,1,0:T(8,128)(2,1)}), bf16[8,48,896]{2,1,0:T(8,128)(2,1)S(1)}, u32[]{:S(2)}, u32[]{:S(2)}) async-start(bf16[8,48,896]{2,1,0:T(8,128)(2,1)} %broadcast_in_dim.108), calls=%async_computation.6 | async-start | bytes 1376256 | tf_op jit(solution)/shard_map/all_to_all | solution.py:329
  133.5 1.3 dynamic-slice_bitcast_fusion.3.mine
  134.8 16.7 %all-to-all-done.6 = bf16[8,48,896]{2,1,0:T(8,128)(2,1)S(1)} async-done(((bf16[8,48,896]{2,1,0:T(8,128)(2,1)}), bf16[8,48,896]{2,1,0:T(8,128)(2,1)S(1)}, u32[]{:S(2)}, u32[]{:S(2)}) %all-to-all-start.6) | async-done | bytes 688160 | tf_op jit(solution)/shard_map/all_to_all | solution.py:329
  151.5 4.7 %gate_up_shares.7 = (bf16[592,384]{1,0:T(8,128)(2,1)S(1)}, bf16[592,384]{1,0:T(8,128)(2,1)S(1)}, bf16[592,384]{1,0:T(8,128)(2,1)S(1)}, bf16[592,384]{1,0:T(8,128)(2,1)S(1)}) custom-call(bf16[384,896]{1,0:T(8,128)(2,1)S(1)} %bitcast.324, f32[1,896]{1,0:T(1,128)S(1)} %broadcast_in_dim.109.gain, bf16[576,896]{1,0:T(8,128)(2,1)S(1)} %dynamic-slice_bitcast_fusion.3.mine, ...), custom_call_target="tpu_custom_call" | custom-call | flops 1585446912 | bytes 6586368 | tf_op jit(solution)/shard_map/gate_up_shares/pallas_call | solution.py:167
  156.3 5.8 %collective-permute-start.21 = (bf16[592,384]{1,0:T(8,128)(2,1)S(1)}, bf16[592,384]{1,0:T(8,128)(2,1)S(1)}, u32[]{:S(2)}, u32[]{:S(2)}) collective-permute-start(bf16[592,384]{1,0:T(8,128)(2,1)S(1)} %get-tuple-element.439), channel_id=1, source_target_pairs={{0,192},{8,200},{16,208},{24,216},{32,224},{40,232},{48,240},{56,2... | collective-permute-start | bytes 1363976 | tf_op jit(solution)/shard_map/ppermute | solution.py:341
  162.1 1.9 collective-permute-start.22
  164.0 1.1 constant_dynamic-slice_fusion.5.refs_4_
  165.1 16.7 %collective-permute-done.21 = bf16[592,384]{1,0:T(8,128)(2,1)S(1)} collective-permute-done((bf16[592,384]{1,0:T(8,128)(2,1)S(1)}, bf16[592,384]{1,0:T(8,128)(2,1)S(1)}, u32[]{:S(2)}, u32[]{:S(2)}) %collective-permute-start.21) | collective-permute-done | bytes 454688 | tf_op jit(solution)/shard_map/ppermute | solution.py:341
  181.8 3.7 %collective-permute-done.23 = bf16[592,384]{1,0:T(8,128)(2,1)S(1)} collective-permute-done((bf16[592,384]{1,0:T(8,128)(2,1)S(1)}, bf16[592,384]{1,0:T(8,128)(2,1)S(1)}, u32[]{:S(2)}, u32[]{:S(2)}) %collective-permute-start.23) | collective-permute-done | bytes 454688 | tf_op jit(solution)/shard_map/ppermute | solution.py:341
  186.3 1.7 collective-permute-start.25
  188.0 2.3 collective-permute-start.26
  190.3 1.5 slice_bitcast_fusion.3
  191.8 7.4 %collective-permute-done.24.refs_1_ = bf16[288,384]{1,0:T(8,128)(2,1)S(1)} collective-permute-done((bf16[288,384]{1,0:T(8,128)(2,1)S(1)}, bf16[288,384]{1,0:T(8,128)(2,1)S(1)}, u32[]{:S(2)}, u32[]{:S(2)}) %collective-permute-start.24) | collective-permute-done | bytes 221216 | tf_op jit(solution)/shard_map/ppermute | solution.py:346
  199.8 4.3 %down_rows.7 = bf16[8,64,896]{2,1,0:T(8,128)(2,1)} custom-call(s32[8]{0:T(128)S(1)} %fusion.68.target, bf16[288,384]{1,0:T(8,128)(2,1)S(1)} %fusion.47.refs_0_, bf16[288,384]{1,0:T(8,128)(2,1)S(1)} %collective-permute-done.24.refs_1_, bf16[288,384]{1,0:T(8,128)(2,1)S(1)} %collective-permute-done.25.refs_2_, ...), custom_call_target="tpu_custom_call" | custom-call | flops 1145044992 | bytes 3866624 | tf_op jit(solution)/shard_map/down_rows/pallas_call | solution.py:202
  204.1 3.7 %all-to-all-start.7 = ((bf16[8,64,896]{2,1,0:T(8,128)(2,1)}), bf16[8,64,896]{2,1,0:T(8,128)(2,1)S(1)}, u32[]{:S(2)}, u32[]{:S(2)}) async-start(bf16[8,64,896]{2,1,0:T(8,128)(2,1)} %down_rows.7), calls=%async_computation.7 | async-start | bytes 1835008 | tf_op jit(solution)/shard_map/all_to_all | solution.py:349
  218.2 14.9 %all-to-all-done.7 = bf16[8,64,896]{2,1,0:T(8,128)(2,1)S(1)} async-done(((bf16[8,64,896]{2,1,0:T(8,128)(2,1)}), bf16[8,64,896]{2,1,0:T(8,128)(2,1)S(1)}, u32[]{:S(2)}, u32[]{:S(2)}) %all-to-all-start.7) | async-done | bytes 917536 | tf_op jit(solution)/shard_map/all_to_all | solution.py:349
  233.5 3.8 %collective-permute-start.27 = (bf16[24,896]{1,0:T(8,128)(2,1)S(1)}, bf16[24,896]{1,0:T(8,128)(2,1)S(1)}, u32[]{:S(2)}, u32[]{:S(2)}) collective-permute-start(bf16[24,896]{1,0:T(8,128)(2,1)S(1)} %get-tuple-element.528), channel_id=1, source_target_pairs={{0,192},{8,200},{16,208},{24,216},{32,224},{40,232},{48,240},{56,2... | collective-permute-start | bytes 129032 | tf_op jit(solution)/shard_map/ppermute | solution.py:366
  238.9 3.9 %collective-permute-done.28 = bf16[24,896]{1,0:T(8,128)(2,1)S(1)} collective-permute-done((bf16[24,896]{1,0:T(8,128)(2,1)S(1)}, bf16[24,896]{1,0:T(8,128)(2,1)S(1)}, u32[]{:S(2)}, u32[]{:S(2)}) %collective-permute-start.28) | collective-permute-done | bytes 43040 | tf_op jit(solution)/shard_map/ppermute | solution.py:366
  (120 shorter events, 17.8 us)
Async XLA Ops:
  6.5 58.0 %all-gather.5.cloned.1.call-start = ((), (), s32[]{:S(2)}) async-start(), calls=%async_computation.8 | async-start | bytes 2359296 | tf_op jit(solution)/shard_map/all_gather | solution.py:430
  7.3 90.1 %all-gather.7.cloned.1.call-start = ((), (), s32[]{:S(2)}) async-start(), calls=%async_computation.9 | async-start | bytes 1548288 | tf_op jit(solution)/shard_map/all_gather | solution.py:256
  8.2 88.8 %copy-start.11 = (bf16[24,896]{1,0:T(8,128)(2,1)}, bf16[24,896]{1,0:T(8,128)(2,1)S(1)}, u32[]{:S(2)}) copy-start(bf16[24,896]{1,0:T(8,128)(2,1)S(1)} %get-tuple-element.529) | copy-start | bytes 129028
  11.3 13.6 %collective-permute-start.13 = (bf16[176,896]{1,0:T(8,128)(2,1)S(1)}, bf16[176,896]{1,0:T(8,128)(2,1)S(1)}, u32[]{:S(2)}, u32[]{:S(2)}) collective-permute-start(bf16[176,896]{1,0:T(8,128)(2,1)S(1)} %pad_maximum_fusion.2), channel_id=1, source_target_pairs={{0,128},{8,136},{16,144},{24,152},{32,160},{40,168},{48,176},{56,1... | collective-permute-start | bytes 946184 | tf_op jit(solution)/shard_map/ppermute | solution.py:247
  14.4 14.5 %collective-permute-start.14 = (bf16[176,896]{1,0:T(8,128)(2,1)S(1)}, bf16[176,896]{1,0:T(8,128)(2,1)S(1)}, u32[]{:S(2)}, u32[]{:S(2)}) collective-permute-start(bf16[176,896]{1,0:T(8,128)(2,1)S(1)} %pad_maximum_fusion.3), channel_id=1, source_target_pairs={{0,192},{8,200},{16,208},{24,216},{32,224},{40,232},{48,240},{56,2... | collective-permute-start | bytes 946184 | tf_op jit(solution)/shard_map/ppermute | solution.py:247
  15.7 13.3 %collective-permute-start.12 = (bf16[176,896]{1,0:T(8,128)(2,1)S(1)}, bf16[176,896]{1,0:T(8,128)(2,1)S(1)}, u32[]{:S(2)}, u32[]{:S(2)}) collective-permute-start(bf16[176,896]{1,0:T(8,128)(2,1)S(1)} %pad_maximum_fusion.1), channel_id=1, source_target_pairs={{0,64},{8,72},{16,80},{24,88},{32,96},{40,104},{48,112},{56,120},{... | collective-permute-start | bytes 946184 | tf_op jit(solution)/shard_map/ppermute | solution.py:247
  29.7 105.1 %all-gather.9.cloned.1.call-start = ((), (), s32[]{:S(2)}) async-start(), calls=%async_computation.10 | async-start | bytes 3483648 | tf_op jit(solution)/shard_map/all_gather | solution.py:256
  32.0 12.3 %collective-permute-start.15 = (bf16[16,24,512]{2,1,0:T(8,128)(2,1)S(1)}, bf16[16,24,512]{2,1,0:T(8,128)(2,1)}, u32[]{:S(2)}, u32[]{:S(2)}) collective-permute-start(bf16[16,24,512]{2,1,0:T(8,128)(2,1)S(1)} %get-tuple-element.520), channel_id=1, source_target_pairs={{0,64},{8,72},{16,80},{24,88},{32,96},{40,104},{48,112},{56,120},{... | collective-permute-start | bytes 1179656 | tf_op jit(solution)/shard_map/ppermute | solution.py:441
  33.5 14.8 %copy-start.14 = (s32[32]{0:T(128)S(1)}, s32[32]{0:T(128)}, u32[]{:S(2)}) copy-start(s32[32]{0:T(128)} %param.16) | copy-start | bytes 388
  45.2 11.8 %collective-permute-start.16 = (bf16[16,24,512]{2,1,0:T(8,128)(2,1)S(1)}, bf16[16,24,512]{2,1,0:T(8,128)(2,1)}, u32[]{:S(2)}, u32[]{:S(2)}) collective-permute-start(bf16[16,24,512]{2,1,0:T(8,128)(2,1)S(1)} %get-tuple-element.519), channel_id=1, source_target_pairs={{0,128},{8,136},{16,144},{24,152},{32,160},{40,168},{48,176},{56,1... | collective-permute-start | bytes 1179656 | tf_op jit(solution)/shard_map/ppermute | solution.py:441
  47.1 17.5 %collective-permute-start.17 = (bf16[16,24,512]{2,1,0:T(8,128)(2,1)S(1)}, bf16[16,24,512]{2,1,0:T(8,128)(2,1)}, u32[]{:S(2)}, u32[]{:S(2)}) collective-permute-start(bf16[16,24,512]{2,1,0:T(8,128)(2,1)S(1)} %get-tuple-element.518), channel_id=1, source_target_pairs={{0,192},{8,200},{16,208},{24,216},{32,224},{40,232},{48,240},{56,2... | collective-permute-start | bytes 1179656 | tf_op jit(solution)/shard_map/ppermute | solution.py:441
  54.6 42.5 %copy-start.7 = (bf16[24,896]{1,0:T(8,128)(2,1)}, bf16[24,896]{1,0:T(8,128)(2,1)S(1)}, u32[]{:S(2)}) copy-start(bf16[24,896]{1,0:T(8,128)(2,1)S(1)} %slice.208) | copy-start | bytes 129028
  54.6 42.5 %copy-start.9 = (bf16[24,896]{1,0:T(8,128)(2,1)}, bf16[24,896]{1,0:T(8,128)(2,1)S(1)}, u32[]{:S(2)}) copy-start(bf16[24,896]{1,0:T(8,128)(2,1)S(1)} %slice.209) | copy-start | bytes 129028
  70.2 19.0 %all-to-all-start.4 = ((bf16[8,64,256]{2,1,0:T(8,128)(2,1)}), bf16[8,64,256]{2,1,0:T(8,128)(2,1)S(1)}, u32[]{:S(2)}, u32[]{:S(2)}) async-start(bf16[8,64,256]{2,1,0:T(8,128)(2,1)} %packed_values.7), calls=%async_computation.4 | async-start | bytes 524288 | tf_op jit(solution)/shard_map/all_to_all | solution.py:289
  90.2 9.2 %collective-permute-start.19 = (bf16[384,256]{1,0:T(8,128)(2,1)}, bf16[384,256]{1,0:T(8,128)(2,1)}, u32[]{:S(2)}, u32[]{:S(2)}) collective-permute-start(bf16[384,256]{1,0:T(8,128)(2,1)} %convolution_convert_fusion.1), channel_id=1, source_target_pairs={{0,128},{8,136},{16,144},{24,152},{32,160},{40,168},{48,176},{56,1... | collective-permute-start | bytes 589832 | tf_op jit(solution)/shard_map/ppermute | solution.py:298
  92.4 10.3 %collective-permute-start.20 = (bf16[384,256]{1,0:T(8,128)(2,1)}, bf16[384,256]{1,0:T(8,128)(2,1)}, u32[]{:S(2)}, u32[]{:S(2)}) collective-permute-start(bf16[384,256]{1,0:T(8,128)(2,1)} %convolution_convert_fusion.1), channel_id=1, source_target_pairs={{0,192},{8,200},{16,208},{24,216},{32,224},{40,232},{48,240},{56,2... | collective-permute-start | bytes 589832 | tf_op jit(solution)/shard_map/ppermute | solution.py:298
  95.5 8.4 %collective-permute-start.18 = (bf16[384,256]{1,0:T(8,128)(2,1)}, bf16[384,256]{1,0:T(8,128)(2,1)S(1)}, u32[]{:S(2)}, u32[]{:S(2)}) collective-permute-start(bf16[384,256]{1,0:T(8,128)(2,1)} %convolution_convert_fusion.1), channel_id=1, source_target_pairs={{0,64},{8,72},{16,80},{24,88},{32,96},{40,104},{48,112},{56,120},{... | collective-permute-start | bytes 589832 | tf_op jit(solution)/shard_map/ppermute | solution.py:298
  97.4 5.2 %copy-start = (bf16[3,256,896]{2,1,0:T(8,128)(2,1)S(1)}, bf16[3,256,896]{2,1,0:T(8,128)(2,1)}, u32[]{:S(2)}) copy-start(bf16[3,256,896]{2,1,0:T(8,128)(2,1)} %all-gather.7.cloned.1.call-done) | copy-start | bytes 4128772
  105.3 22.9 %all-to-all-start.5 = ((bf16[8,48,896]{2,1,0:T(8,128)(2,1)}), bf16[8,48,896]{2,1,0:T(8,128)(2,1)S(1)}, u32[]{:S(2)}, u32[]{:S(2)}) async-start(bf16[8,48,896]{2,1,0:T(8,128)(2,1)} %bitcast.57), calls=%async_computation.5 | async-start | bytes 1376256 | tf_op jit(solution)/shard_map/all_to_all | solution.py:320
  108.8 81.5 %all-gather.11.cloned.1.call-start = ((), (), s32[]{:S(2)}) async-start(), calls=%async_computation.11 | async-start | bytes 2322432 | tf_op jit(solution)/shard_map/all_gather | solution.py:256
  129.2 22.4 %all-to-all-start.6 = ((bf16[8,48,896]{2,1,0:T(8,128)(2,1)}), bf16[8,48,896]{2,1,0:T(8,128)(2,1)S(1)}, u32[]{:S(2)}, u32[]{:S(2)}) async-start(bf16[8,48,896]{2,1,0:T(8,128)(2,1)} %broadcast_in_dim.108), calls=%async_computation.6 | async-start | bytes 1376256 | tf_op jit(solution)/shard_map/all_to_all | solution.py:329
  133.5 82.4 %copy-start.13 = (f32[896]{0:T(1024)}, f32[896]{0:T(1024)S(1)}, u32[]{:S(2)}) copy-start(f32[896]{0:T(1024)S(1)} %dynamic-slice_convert_fusion) | copy-start | bytes 10756
  134.8 21.5 %copy-start.3 = (bf16[576,896]{1,0:T(8,128)(2,1)}, bf16[576,896]{1,0:T(8,128)(2,1)S(1)}, u32[]{:S(2)}) copy-start(bf16[576,896]{1,0:T(8,128)(2,1)S(1)} %dynamic-slice_bitcast_fusion.3.mine) | copy-start | bytes 3096580
  156.3 25.5 %collective-permute-start.21 = (bf16[592,384]{1,0:T(8,128)(2,1)S(1)}, bf16[592,384]{1,0:T(8,128)(2,1)S(1)}, u32[]{:S(2)}, u32[]{:S(2)}) collective-permute-start(bf16[592,384]{1,0:T(8,128)(2,1)S(1)} %get-tuple-element.439), channel_id=1, source_target_pairs={{0,192},{8,200},{16,208},{24,216},{32,224},{40,232},{48,240},{56,2... | collective-permute-start | bytes 1363976 | tf_op jit(solution)/shard_map/ppermute | solution.py:341
  162.1 19.7 %collective-permute-start.22 = (bf16[592,384]{1,0:T(8,128)(2,1)S(1)}, bf16[592,384]{1,0:T(8,128)(2,1)S(1)}, u32[]{:S(2)}, u32[]{:S(2)}) collective-permute-start(bf16[592,384]{1,0:T(8,128)(2,1)S(1)} %get-tuple-element.440), channel_id=1, source_target_pairs={{0,128},{8,136},{16,144},{24,152},{32,160},{40,168},{48,176},{56,1... | collective-permute-start | bytes 1363976 | tf_op jit(solution)/shard_map/ppermute | solution.py:341
  164.0 21.5 %collective-permute-start.23 = (bf16[592,384]{1,0:T(8,128)(2,1)S(1)}, bf16[592,384]{1,0:T(8,128)(2,1)S(1)}, u32[]{:S(2)}, u32[]{:S(2)}) collective-permute-start(bf16[592,384]{1,0:T(8,128)(2,1)S(1)} %get-tuple-element.441), channel_id=1, source_target_pairs={{0,64},{8,72},{16,80},{24,88},{32,96},{40,104},{48,112},{56,120},{... | collective-permute-start | bytes 1363976 | tf_op jit(solution)/shard_map/ppermute | solution.py:341
  165.0 34.8 %copy-start.5 = (bf16[288,896]{1,0:T(8,128)(2,1)}, bf16[288,896]{1,0:T(8,128)(2,1)S(1)}, u32[]{:S(2)}) copy-start(bf16[288,896]{1,0:T(8,128)(2,1)S(1)} %constant_dynamic-slice_fusion.5.refs_4_) | copy-start | bytes 1548292
  185.8 13.4 %collective-permute-start.24 = (bf16[288,384]{1,0:T(8,128)(2,1)S(1)}, bf16[288,384]{1,0:T(8,128)(2,1)S(1)}, u32[]{:S(2)}, u32[]{:S(2)}) collective-permute-start(bf16[288,384]{1,0:T(8,128)(2,1)S(1)} %fusion.47.refs_0_), channel_id=1, source_target_pairs={{0,64},{8,72},{16,80},{24,88},{32,96},{40,104},{48,112},{56,120},{... | collective-permute-start | bytes 663560 | tf_op jit(solution)/shard_map/ppermute | solution.py:346
  186.3 12.9 %collective-permute-start.25 = (bf16[288,384]{1,0:T(8,128)(2,1)S(1)}, bf16[288,384]{1,0:T(8,128)(2,1)S(1)}, u32[]{:S(2)}, u32[]{:S(2)}) collective-permute-start(bf16[288,384]{1,0:T(8,128)(2,1)S(1)} %fusion.47.refs_0_), channel_id=1, source_target_pairs={{0,128},{8,136},{16,144},{24,152},{32,160},{40,168},{48,176},{56,1... | collective-permute-start | bytes 663560 | tf_op jit(solution)/shard_map/ppermute | solution.py:346
  188.0 11.9 %collective-permute-start.26 = (bf16[288,384]{1,0:T(8,128)(2,1)S(1)}, bf16[288,384]{1,0:T(8,128)(2,1)S(1)}, u32[]{:S(2)}, u32[]{:S(2)}) collective-permute-start(bf16[288,384]{1,0:T(8,128)(2,1)S(1)} %fusion.47.refs_0_), channel_id=1, source_target_pairs={{0,192},{8,200},{16,208},{24,216},{32,224},{40,232},{48,240},{56,2... | collective-permute-start | bytes 663560 | tf_op jit(solution)/shard_map/ppermute | solution.py:346
  204.1 13.0 %copy-start.15 = (pred[4,24]{1,0:T(4,128)(4,1)S(1)}, pred[4,24]{1,0:T(4,128)(4,1)}, u32[]{:S(2)}) copy-start(pred[4,24]{1,0:T(4,128)(4,1)} %get-tuple-element.491) | copy-start | bytes 292
  204.1 28.9 %all-to-all-start.7 = ((bf16[8,64,896]{2,1,0:T(8,128)(2,1)}), bf16[8,64,896]{2,1,0:T(8,128)(2,1)S(1)}, u32[]{:S(2)}, u32[]{:S(2)}) async-start(bf16[8,64,896]{2,1,0:T(8,128)(2,1)} %down_rows.7), calls=%async_computation.7 | async-start | bytes 1835008 | tf_op jit(solution)/shard_map/all_to_all | solution.py:349
  217.8 20.4 %copy-start.8 = (bf16[24,896]{1,0:T(8,128)(2,1)S(1)}, bf16[24,896]{1,0:T(8,128)(2,1)}, u32[]{:S(2)}) copy-start(bf16[24,896]{1,0:T(8,128)(2,1)} %copy-done.7) | copy-start | bytes 129028
  217.8 20.4 %copy-start.10 = (bf16[24,896]{1,0:T(8,128)(2,1)S(1)}, bf16[24,896]{1,0:T(8,128)(2,1)}, u32[]{:S(2)}) copy-start(bf16[24,896]{1,0:T(8,128)(2,1)} %copy-done.9) | copy-start | bytes 129028
  217.8 20.4 %copy-start.12 = (bf16[24,896]{1,0:T(8,128)(2,1)S(1)}, bf16[24,896]{1,0:T(8,128)(2,1)}, u32[]{:S(2)}) copy-start(bf16[24,896]{1,0:T(8,128)(2,1)} %copy-done.11) | copy-start | bytes 129028
  233.5 5.5 %collective-permute-start.27 = (bf16[24,896]{1,0:T(8,128)(2,1)S(1)}, bf16[24,896]{1,0:T(8,128)(2,1)S(1)}, u32[]{:S(2)}, u32[]{:S(2)}) collective-permute-start(bf16[24,896]{1,0:T(8,128)(2,1)S(1)} %get-tuple-element.528), channel_id=1, source_target_pairs={{0,192},{8,200},{16,208},{24,216},{32,224},{40,232},{48,240},{56,2... | collective-permute-start | bytes 129032 | tf_op jit(solution)/shard_map/ppermute | solution.py:366
  237.2 5.6 %collective-permute-start.28 = (bf16[24,896]{1,0:T(8,128)(2,1)S(1)}, bf16[24,896]{1,0:T(8,128)(2,1)S(1)}, u32[]{:S(2)}, u32[]{:S(2)}) collective-permute-start(bf16[24,896]{1,0:T(8,128)(2,1)S(1)} %get-tuple-element.527), channel_id=1, source_target_pairs={{0,128},{8,136},{16,144},{24,152},{32,160},{40,168},{48,176},{56,1... | collective-permute-start | bytes 129032 | tf_op jit(solution)/shard_map/ppermute | solution.py:366
  237.7 5.6 %collective-permute-start.29 = (bf16[24,896]{1,0:T(8,128)(2,1)S(1)}, bf16[24,896]{1,0:T(8,128)(2,1)S(1)}, u32[]{:S(2)}, u32[]{:S(2)}) collective-permute-start(bf16[24,896]{1,0:T(8,128)(2,1)S(1)} %get-tuple-element.526), channel_id=1, source_target_pairs={{0,64},{8,72},{16,80},{24,88},{32,96},{40,104},{48,112},{56,120},{... | collective-permute-start | bytes 129032 | tf_op jit(solution)/shard_map/ppermute | solution.py:366
  243.6 0.7 copy-start.2
Sparse Core Ops, SparseCore 0:
  9.1 44.0 all-gather.4
  55.1 23.2 all-gather.6
  80.2 30.7 all-gather.8
  112.7 27.7 all-gather.10
